TPU v7x, 512 devices: a whole 4x8x8 slice. The times are simulated.
512 devices in a mesh: dp: 128 (over x, y, z_lo, core), mp: 4 (over z_hi).
Axes of the slice: x: 4, y: 8, z: 8 (z_hi: 4, z_lo: 2; z = z_hi * 2 + z_lo), core: 2. Of those that a mesh axis runs over, the one named last changes fastest.
Arguments:
- patches: bfloat16 [256, 256, 1152], P('dp', None, 'mp'), may hold values from -6 to 6
- patch_count: int32 [256], P('dp'), may hold values from 1 to 256, as said below
- ln1_gain: float32 [1152], replicated, may hold values from 0.5 to 1.5
- w_qkv: bfloat16 [3, 1152, 1152], P(None, None, 'mp'), may hold values from -0.1875 to 0.1875
- w_out: bfloat16 [1152, 1152], P('mp'), may hold values from -0.1875 to 0.1875
- ln2_gain: float32 [1152], replicated, may hold values from 0.5 to 1.5
- pool_kv: bfloat16 [2, 1152, 1152], P(None, None, 'mp'), may hold values from -0.1875 to 0.1875
- pool_query: bfloat16 [1152], P('mp'), may hold values from -5 to 5
- pool_out: bfloat16 [1152, 1152], P('mp'), may hold values from -0.1875 to 0.1875
- text_emb: bfloat16 [256, 1152], P('dp'), may hold values from -6 to 6
- image_pair: int32 [256], P('dp'), may hold values from 0 to 255, each once
- logit_scale: float32 [], replicated, may hold values from 2 to 2.5
- logit_bias: float32 [], replicated, may hold values from -5 to -2.5
Outputs:
- image_grad: float32 [256, 1152], P('dp')
- text_grad: float32 [256, 1152], P('dp')
Inputs may be any that keep to these rules, and one draw needn't show every extreme that they name: `patch_count`: each count is the product of an image grid's two sides, each 1 to 16; some image of every draw fills all 256 positions. `image_pair`: every text is the pair of exactly one image.
All inputs are finite; a program needn't handle non-finite values.
Results may differ from a plain program's by a relative error of at most 0.014.
Values may be sent and summed in bfloat16 or wider, within the bound.
No kernel may reach another device: no remote copies, remote signals or barrier semaphores. Data moves between devices by JAX's collectives and lax.ppermute only.
A program may use at most 64 MiB of HBM per device.

v0:
```python
import math

import jax
import jax.numpy as jnp
from jax import lax
from jax.sharding import PartitionSpec as P

HDIM = 72


def from_behind(value, axis, steps):
    count = lax.axis_size(axis)
    pairs = [(source, (source + steps) % count) for source in range(count)]
    return lax.ppermute(value, axis, pairs)


def layer_norm(values, gain_vec):
    floats = values.astype(jnp.float32)
    center = floats - jnp.mean(floats, axis=-1, keepdims=True)
    spread = jnp.mean(center * center, axis=-1, keepdims=True)
    return center * lax.rsqrt(spread + 1e-06) * gain_vec


def masked_softmax(scores, valid_keys):
    scores = jnp.where(valid_keys, scores, -1e30)
    highest = jnp.max(scores, axis=-1, keepdims=True)
    raised = jnp.exp(scores - highest)
    return raised / jnp.sum(raised, axis=-1, keepdims=True)


def unit_rows(values):
    inverse = lax.rsqrt(jnp.sum(values * values, axis=-1, keepdims=True) + 1e-06)
    return (values * inverse, inverse)


def per_device(
    patches,
    patch_count,
    ln1_gain,
    w_qkv,
    w_out,
    ln2_gain,
    pool_kv,
    pool_query,
    pool_out,
    text_emb,
    image_pair,
    logit_scale,
    logit_bias,
):
    f32 = jnp.float32
    high = lax.Precision.HIGHEST
    rows_img, pmax, dlocal = patches.shape
    local_heads = dlocal // HDIM
    total_rows = rows_img * pmax
    gathered = lax.all_gather(patches, "mp", axis=2, tiled=True)
    width = gathered.shape[2]
    normed = layer_norm(gathered, ln1_gain).astype(jnp.bfloat16).reshape(total_rows, width)
    proj = jnp.einsum("rd,cde->cre", normed, w_qkv, preferred_element_type=f32).astype(jnp.bfloat16)
    proj = proj.reshape(3, rows_img, pmax, local_heads, HDIM)
    valid_keys = jnp.arange(pmax, dtype=jnp.int32)[None, :] < patch_count[:, None]
    scores = jnp.einsum(
        "iqhe,ikhe->ihqk", proj[0], proj[1], preferred_element_type=f32
    ) / math.sqrt(HDIM)
    attn = masked_softmax(scores, valid_keys[:, None, None, :]).astype(jnp.bfloat16)
    context = jnp.einsum("ihqk,ikhe->iqhe", attn, proj[2], preferred_element_type=f32).astype(
        jnp.bfloat16
    )
    partial_out = jnp.dot(context.reshape(total_rows, dlocal), w_out, preferred_element_type=f32)
    summed = lax.psum_scatter(partial_out, "mp", scatter_dimension=1, tiled=True)
    own_stream = (patches.reshape(total_rows, dlocal).astype(f32) + summed).astype(jnp.bfloat16)
    stream = lax.all_gather(own_stream, "mp", axis=1, tiled=True)
    normed2 = layer_norm(stream, ln2_gain).astype(jnp.bfloat16)
    keyval = jnp.einsum("rd,cde->cre", normed2, pool_kv, preferred_element_type=f32).astype(
        jnp.bfloat16
    )
    keyval = keyval.reshape(2, rows_img, pmax, local_heads, HDIM)
    query = pool_query.reshape(local_heads, HDIM)
    pool_scores = jnp.einsum(
        "he,iphe->ihp", query, keyval[0], preferred_element_type=f32
    ) / math.sqrt(HDIM)
    pool_attn = masked_softmax(pool_scores, valid_keys[:, None, :]).astype(jnp.bfloat16)
    pooled = jnp.einsum("ihp,iphe->ihe", pool_attn, keyval[1], preferred_element_type=f32).astype(
        jnp.bfloat16
    )
    embeds = lax.psum(
        jnp.dot(pooled.reshape(rows_img, dlocal), pool_out, preferred_element_type=f32), "mp"
    )
    zimg, inv_img = unit_rows(embeds)
    ztxt_own, inv_txt = unit_rows(text_emb.astype(f32))
    scale = jnp.exp(logit_scale)
    shards = lax.axis_size("dp")
    rank = lax.axis_index("dp")
    local_ids = jnp.arange(rows_img, dtype=jnp.int32)

    def cycle_turn(turn_index, carry):
        text_block, grad_block, img_acc = carry
        owner = (rank - turn_index) % shards
        text_ids = owner * rows_img + local_ids
        ztxt_blk, unused_inv = unit_rows(text_block.astype(f32))
        logits = scale * jnp.dot(zimg, ztxt_blk.T, precision=high) + logit_bias
        label = jnp.where(image_pair[:, None] == text_ids[None, :], 1.0, -1.0).astype(f32)
        dlog = -label * jax.nn.sigmoid(-label * logits)
        img_acc = img_acc + scale * jnp.dot(dlog, ztxt_blk, precision=high)
        grad_new = grad_block + scale * jnp.dot(dlog.T, zimg, precision=high)
        text_block = from_behind(text_block, "dp", 1)
        grad_block = from_behind(grad_new, "dp", 1)
        return (text_block, grad_block, img_acc)

    start_state = (text_emb, jnp.zeros(zimg.shape, f32), jnp.zeros(zimg.shape, f32))
    unused_text, gtxt, gimg = lax.fori_loop(0, shards, cycle_turn, start_state)
    image_grad = (gimg - zimg * jnp.sum(zimg * gimg, axis=-1, keepdims=True)) * inv_img
    text_grad = (gtxt - ztxt_own * jnp.sum(ztxt_own * gtxt, axis=-1, keepdims=True)) * inv_txt
    return (image_grad, text_grad)


def solution(mesh):
    placed = (
        P("dp", None, "mp"),
        P("dp"),
        P(),
        P(None, None, "mp"),
        P("mp", None),
        P(),
        P(None, None, "mp"),
        P("mp"),
        P("mp", None),
        P("dp", None),
        P("dp"),
        P(),
        P(),
    )
    return jax.shard_map(
        per_device,
        mesh=mesh,
        in_specs=placed,
        out_specs=(P("dp", None), P("dp", None)),
        check_vma=False,
    )
```

profile of v0, /device:TPU:1, one launch (start us, length us, event | category | flops | bytes accessed | tf_op | source)
XLA Modules:
  0.0 1859.9 jit_solution(1501979611399735706)
XLA Ops:
  10.2 45.3 %all-gather.3.cloned.1.call-done = bf16[2,256,1152]{1,0,2:T(2,128)(2,1)} async-done(((bf16[2,256,288]{1,0,2:T(2,128)(2,1)}), bf16[2,256,1152]{1,0,2:T(2,128)(2,1)}) %all-gather.3.cloned.1.call-update) | async-done | bytes 1179664 | tf_op jit(solution)/shard_map/all_gather | solution.py:56
  68.7 55.9 %reduce-scatter.2.cloned.1.call-done = f32[512,288]{0,1:T(8,128)} async-done(((f32[512,1152]{0,1:T(8,128)}), f32[512,288]{0,1:T(8,128)}) %reduce-scatter.2.cloned.1.call-update) | async-done | bytes 589840 | tf_op jit(solution)/shard_map/reduce_scatter | solution.py:70
  128.6 36.2 %all-gather.5.cloned.1.call-done = bf16[512,1152]{0,1:T(8,128)(2,1)} async-done(((bf16[512,288]{0,1:T(8,128)(2,1)}), bf16[512,1152]{0,1:T(8,128)(2,1)}) %all-gather.5.cloned.1.call-update) | async-done | bytes 1179664 | tf_op jit(solution)/shard_map/all_gather | solution.py:72
  172.8 8.7 psum.7
  181.7 1667.9 %while.20 = (s32[]{:T(128)}, bf16[2,1152]{1,0:T(2,128)(2,1)S(1)}, f32[2,1152]{1,0:T(2,128)S(1)}, f32[2,1152]{1,0:T(2,128)}, f32[]{:T(128)}, /*index=5*/s32[2]{0:...) while((s32[]{:T(128)}, bf16[2,1152]{1,0:T(2,128)(2,1)S(1)}, ...), condition=%wide.region_13.14_spmd.clone, body=%wide.region_11.13_spmd.clone.sunk | while | flops 193594 | bytes 134120 | solution.py:111
  181.8 6.7 collective-permute-start
  213.2 3.9 collective-permute-done.1
  226.2 3.9 collective-permute-done.1
  239.3 3.9 collective-permute-done.1
  252.3 3.9 collective-permute-done.1
  265.4 3.9 collective-permute-done.1
  278.5 3.9 collective-permute-done.1
  291.5 3.9 collective-permute-done.1
  304.6 3.9 collective-permute-done.1
  317.7 3.9 collective-permute-done.1
  330.7 3.9 collective-permute-done.1
  343.8 3.9 collective-permute-done.1
  356.8 3.9 collective-permute-done.1
  369.9 3.9 collective-permute-done.1
  383.0 3.9 collective-permute-done.1
  396.0 3.9 collective-permute-done.1
  422.1 3.9 collective-permute-done.1
  435.2 3.9 collective-permute-done.1
  448.3 3.9 collective-permute-done.1
  (1465 shorter events, 1611.3 us)
Async XLA Ops:
  7.2 48.3 %all-gather.3.cloned.1.call-start = ((), (), s32[]{:S(2)}) async-start(), calls=%async_computation.1 | async-start | bytes 1474560 | tf_op jit(solution)/shard_map/all_gather | solution.py:56
  9.4 115.3 %reduce-scatter.2.cloned.1.call-start = ((), (), s32[]{:S(2)}) async-start(), calls=%async_computation.2 | async-start | bytes 2949120 | tf_op jit(solution)/shard_map/reduce_scatter | solution.py:70
  68.5 96.3 %all-gather.5.cloned.1.call-start = ((), (), s32[]{:S(2)}) async-start(), calls=%async_computation.3 | async-start | bytes 1474560 | tf_op jit(solution)/shard_map/all_gather | solution.py:72
  181.8 11.4 collective-permute-start
  193.5 9.3 collective-permute-start
  220.9 9.2 collective-permute-start.1
  247.0 9.2 collective-permute-start.1
  260.1 9.2 collective-permute-start.1
  286.2 9.2 collective-permute-start.1
  312.3 9.2 collective-permute-start.1
  325.4 9.2 collective-permute-start.1
  351.5 9.2 collective-permute-start.1
  364.6 9.2 collective-permute-start.1
  390.7 9.2 collective-permute-start.1
  429.9 9.2 collective-permute-start.1
  456.0 9.2 collective-permute-start.1
  469.1 9.2 collective-permute-start.1
  495.2 9.2 collective-permute-start.1
  508.2 9.2 collective-permute-start.1
  534.4 9.2 collective-permute-start.1
  560.5 9.2 collective-permute-start.1
  573.5 9.2 collective-permute-start.1
  599.7 9.2 collective-permute-start.1
  612.7 9.2 collective-permute-start.1
  (247 other events, 4220.4 us)
Sparse Core Ops, SparseCore 0:
  10.1 45.2 all-gather.2
  68.6 55.9 reduce-scatter.1
  126.8 37.9 all-gather.4
where the time goes:
time: 1880 us; the launch traced here: 1860 us
  waiting for transfers between devices  856 us (46%)
  starting transfers between devices  498 us (26%)
  matrix products  433 us (23%)
  other arithmetic  29.3 us (2%)
    ppermute x256, waiting for transfers between devices, from_behind(): return lax.ppermute(value, axis, pairs)  719 us
    ppermute x256, starting transfers between devices, from_behind(): return lax.ppermute(value, axis, pairs)  498 us
    dot_general x128, matrix products, cycle_turn(): img_acc = img_acc + scale * jnp.dot(dlog, ztxt_blk, precision=high)  200 us
    dot_general x128, matrix products, cycle_turn(): logits = scale * jnp.dot(zimg, ztxt_blk.T, precision=high) + logit_bias  198 us
    reduce_scatter x1, waiting for transfers between devices, per_device(): lax.psum_scatter(partial_out, 'mp', scatter_dimension=1, tiled=True)  55.9 us
    all_gather x1, waiting for transfers between devices, per_device(): gathered = lax.all_gather(patches, 'mp', axis=2, tiled=True)  45.3 us
  transfers between devices with their start and end apart: 259, of which 257 were waited for; matrix products, arithmetic and copies ran while one was open for 24% of the time, Pallas kernels for 0%

commit v1 on v0

v1 whole, which is shorter than its diff:
```python
import math

import jax
import jax.numpy as jnp
from jax import lax
from jax.sharding import PartitionSpec as P

HDIM = 72


def spread_all(value, axis):
    count = lax.axis_size(axis)
    return lax.all_to_all(jnp.broadcast_to(value[None], (count,) + value.shape), axis, 0, 0)


def layer_norm(values, gain_vec):
    floats = values.astype(jnp.float32)
    center = floats - jnp.mean(floats, axis=-1, keepdims=True)
    spread = jnp.mean(center * center, axis=-1, keepdims=True)
    return center * lax.rsqrt(spread + 1e-06) * gain_vec


def masked_softmax(scores, valid_keys):
    scores = jnp.where(valid_keys, scores, -1e30)
    highest = jnp.max(scores, axis=-1, keepdims=True)
    raised = jnp.exp(scores - highest)
    return raised / jnp.sum(raised, axis=-1, keepdims=True)


def split_bf16(values, terms):
    pieces = []
    for _ in range(terms):
        top = values.astype(jnp.bfloat16)
        pieces.append(top)
        values = values - top.astype(jnp.float32)
    return pieces


def per_device(
    patches,
    patch_count,
    ln1_gain,
    w_qkv,
    w_out,
    ln2_gain,
    pool_kv,
    pool_query,
    pool_out,
    text_emb,
    image_pair,
    logit_scale,
    logit_bias,
):
    f32, bf16 = jnp.float32, jnp.bfloat16
    rows_img, pmax, dlocal = patches.shape
    width = w_out.shape[1]
    local_heads = dlocal // HDIM
    heads = width // HDIM
    shards = lax.axis_size("mp")
    me = lax.axis_index("mp")
    rank = lax.axis_index("dp")
    half = pmax // 2
    nt = (((1,), (1,)), ((), ()))

    def dot(left, right, dims=(((1,), (0,)), ((), ()))):
        return lax.dot_general(left, right, dims, preferred_element_type=f32)

    def dot_exact(left, right, dims=(((1,), (0,)), ((), ()))):
        rows = left.shape[0]
        product = dot(jnp.concatenate(split_bf16(left, 3), axis=0), right, dims)
        return product[:rows] + product[rows : 2 * rows] + product[2 * rows :]

    tall = lax.all_gather(patches.transpose(0, 2, 1), "mp")

    texts_pairs = jnp.concatenate(
        [text_emb, jnp.broadcast_to(image_pair.astype(bf16)[:, None], (rows_img, 128))], axis=1
    )
    texts_pairs = spread_all(texts_pairs, "dp").reshape(-1, width + 128)
    text_all, pair_all = texts_pairs[:, :width], texts_pairs[:, width].astype(jnp.int32)
    texts = text_all.astype(f32)
    inv_txt = lax.rsqrt(jnp.sum(texts * texts, axis=-1) + 1e-06)

    head_of = jnp.arange(dlocal, dtype=jnp.int32) // HDIM
    own_head = head_of[None, :] == jnp.arange(local_heads, dtype=jnp.int32)[:, None]
    probe = jnp.where(own_head, pool_query[None, :], 0).astype(bf16)
    probe_keys = dot(probe, pool_kv[0], nt) * (1.0 / math.sqrt(HDIM))
    probe_all = spread_all(jnp.stack(split_bf16(probe_keys, 2)), "mp")
    probe_all = probe_all.transpose(1, 0, 2, 3).reshape(2 * heads, width)

    w_rows = w_qkv.transpose(0, 2, 1).reshape(3 * dlocal, width)
    blocks = []
    for i in range(rows_img):
        floats = tall[:, i].reshape(width, pmax).astype(f32)
        center = floats - jnp.mean(floats, axis=0, keepdims=True)
        spread = jnp.mean(center * center, axis=0, keepdims=True)
        normed = (center * lax.rsqrt(spread + 1e-06) * ln1_gain[:, None]).astype(bf16)
        proj = dot(w_rows, normed).astype(bf16).reshape(3, local_heads, HDIM, pmax)
        valid_keys = jnp.arange(pmax, dtype=jnp.int32) < patch_count[i]
        scores = jnp.einsum("heq,hek->hqk", proj[0], proj[1], preferred_element_type=f32) / math.sqrt(HDIM)
        attn = masked_softmax(scores, valid_keys[None, None, :]).astype(bf16)
        context = jnp.einsum("hek,hqk->heq", proj[2], attn, preferred_element_type=f32).astype(bf16)
        context = context.reshape(dlocal, pmax)
        partial = lax.dot_general(context, w_out, (((0,), (0,)), ((), ())), preferred_element_type=f32)
        blocks.append(partial.astype(bf16).reshape(2, half, width))

    parts = lax.all_to_all(jnp.concatenate(blocks, axis=0), "mp", 0, 0)
    my_image, my_half = me // 2, me % 2
    mine = jnp.where(my_image == 0, tall[:, 0], tall[:, 1]).reshape(width, pmax)
    resid = jnp.where(my_half == 0, mine[:, :half], mine[:, half:]).T
    stream = (resid.astype(f32) + jnp.sum(parts.astype(f32), axis=0)).astype(bf16)
    normed2 = layer_norm(stream, ln2_gain).astype(bf16)
    both = dot(probe_all, normed2, nt)
    pool_scores = both[:heads] + both[heads:]
    row_ids = my_half * half + jnp.arange(half, dtype=jnp.int32)
    my_count = jnp.where(my_image == 0, patch_count[0], patch_count[1])
    pool_scores = jnp.where((row_ids < my_count)[None, :], pool_scores, -1e30)
    highest = jnp.max(pool_scores, axis=-1, keepdims=True)
    raised = jnp.exp(pool_scores - highest)
    total = jnp.sum(raised, axis=-1, keepdims=True)
    mixed = dot((raised / total).astype(bf16), normed2)
    lse = jnp.broadcast_to(highest + jnp.log(total), (heads, 128))
    send = jnp.concatenate([mixed, lse], axis=1).reshape(shards, local_heads, width + 128)
    halves = lax.all_to_all(send, "mp", 0, 0).reshape(rows_img, 2, local_heads, width + 128)
    lse_all = halves[..., width : width + 1]
    share = jnp.exp(lse_all - jnp.max(lse_all, axis=1, keepdims=True))
    share = share / jnp.sum(share, axis=1, keepdims=True)
    mixed = jnp.sum(share * halves[..., :width], axis=1).reshape(rows_img * local_heads, width)
    vals = dot_exact(mixed, pool_kv[1]).reshape(rows_img, local_heads, dlocal)
    pooled = jnp.sum(jnp.where(own_head[None], vals, 0.0), axis=1).astype(bf16)
    embeds = lax.psum(dot(pooled, pool_out), "mp")

    inv_img_own = lax.rsqrt(jnp.sum(embeds * embeds, axis=-1, keepdims=True) + 1e-06)
    zimg_own = embeds * inv_img_own
    zimg = spread_all(zimg_own.astype(bf16), "dp").reshape(-1, width)

    scale = jnp.exp(logit_scale)
    first = rank * rows_img
    own_ids = first + jnp.arange(rows_img, dtype=jnp.int32)
    every = jnp.arange(zimg.shape[0], dtype=jnp.int32)
    text_own = text_emb.astype(f32)
    inv_txt_own = lax.rsqrt(jnp.sum(text_own * text_own, axis=-1, keepdims=True) + 1e-06)
    ztxt_own = text_own * inv_txt_own

    def slope(logits, is_pair):
        label = jnp.where(is_pair, 1.0, -1.0).astype(f32)
        return -label * jax.nn.sigmoid(-label * logits)

    logits_img = scale * dot_exact(zimg_own, text_all, nt) * inv_txt[None, :] + logit_bias
    dlog_img = slope(logits_img, image_pair[:, None] == every[None, :])
    logits_txt = scale * dot(text_emb, zimg, nt) * inv_txt_own + logit_bias
    dlog_txt = slope(logits_txt, pair_all[None, :] == own_ids[:, None])
    gimg = scale * dot_exact(dlog_img * inv_txt[None, :], text_all)
    gtxt = scale * dot_exact(dlog_txt, zimg)
    image_grad = (gimg - zimg_own * jnp.sum(zimg_own * gimg, axis=-1, keepdims=True)) * inv_img_own
    text_grad = (gtxt - ztxt_own * jnp.sum(ztxt_own * gtxt, axis=-1, keepdims=True)) * inv_txt_own
    return (image_grad, text_grad)


def solution(mesh):
    placed = (
        P("dp", None, "mp"),
        P("dp"),
        P(),
        P(None, None, "mp"),
        P("mp", None),
        P(),
        P(None, None, "mp"),
        P("mp"),
        P("mp", None),
        P("dp", None),
        P("dp"),
        P(),
        P(),
    )
    return jax.shard_map(
        per_device,
        mesh=mesh,
        in_specs=placed,
        out_specs=(P("dp", None), P("dp", None)),
        check_vma=False,
    )
```

time: 1880 us -> 216 us (0.11)
  waiting for transfers between devices: 856 us -> 87.5 us
  starting transfers between devices: 498 us -> 47.2 us
  matrix products: 433 us -> 19.3 us
    ppermute x256 -> x0, waiting for transfers between devices: 719 us -> none  [from_behind(): return lax.ppermute(value, axis, pairs)]
    ppermute x256 -> x0, starting transfers between devices: 498 us -> none  [from_behind(): return lax.ppermute(value, axis, pairs)]
    dot_general x391 -> x17, matrix products: 431 us -> 16.3 us  [the longest x11 6.76 us: dot(): return lax.dot_general(left, right, dims, preferred_element_type=f32)]
    reduce_scatter x1 -> x0, waiting for transfers between devices: 55.9 us -> none  [per_device(): lax.psum_scatter(partial_out, 'mp', scatter_dimension=1, tiled=True)]
    all_to_all x0 -> x5, waiting for transfers between devices: none -> 55.4 us  [the longest x3 31.5 us: spread_all(): lax.all_to_all(jnp.broadcast_to(value[None], (count,) + value.shape), axi...]
    all_gather x2 -> x1, waiting for transfers between devices: 81.5 us -> 31.5 us  [per_device(): tall = lax.all_gather(patches.transpose(0, 2, 1), 'mp')]
    all_to_all x0 -> x5, starting transfers between devices: none -> 47.2 us  [the longest x3 36 us: spread_all(): lax.all_to_all(jnp.broadcast_to(value[None], (count,) + value.shape), axi...]
  transfers between devices with their start and end apart: 259 -> 6, of which waited for: 257 -> 5; matrix products, arithmetic and copies ran while one was open for 24% -> 16% of each run, Pallas kernels for 0% -> 0%
where the time goes in v1:
time: 216 us; the launch traced here: 215 us
  waiting for transfers between devices  87.5 us (41%)
  starting transfers between devices  47.2 us (22%)
  other arithmetic  22.5 us (10%)
  matrix products  19.3 us (9%)
  between operations  17.1 us (8%)
  local copies, waits for them, and re-layouts  13.3 us (6%)
  blocking collectives  7.64 us (4%)
    all_to_all x3, starting transfers between devices, spread_all(): lax.all_to_all(jnp.broadcast_to(value[None], (count,) + value.shape), axi...  36 us
    all_to_all x3, waiting for transfers between devices, spread_all(): lax.all_to_all(jnp.broadcast_to(value[None], (count,) + value.shape), axi...  31.5 us
    all_gather x1, waiting for transfers between devices, per_device(): tall = lax.all_gather(patches.transpose(0, 2, 1), 'mp')  31.5 us
    all_to_all x1, waiting for transfers between devices, per_device(): parts = lax.all_to_all(jnp.concatenate(blocks, axis=0), 'mp', 0, 0)  17 us
    psum x1, blocking collectives, per_device(): embeds = lax.psum(dot(pooled, pool_out), 'mp')  7.64 us
    all_to_all x1, starting transfers between devices, per_device(): lax.all_to_all(send, 'mp', 0, 0)  6.97 us
    all_to_all x1, waiting for transfers between devices, per_device(): lax.all_to_all(send, 'mp', 0, 0)  6.85 us
    dot_general x11, matrix products, dot(): return lax.dot_general(left, right, dims, preferred_element_type=f32)  6.76 us
  transfers between devices with their start and end apart: 6, of which 5 were waited for; matrix products, arithmetic and copies ran while one was open for 16% of the time, Pallas kernels for 0%

profile of v1, /device:TPU:1, one launch (start us, length us, event | category | flops | bytes accessed | tf_op | source)
XLA Modules:
  0.0 214.5 jit_solution(1868274545893278794)
XLA Ops:
  10.0 10.8 %all-to-all-start = ((bf16[4,2,4,1152]{3,2,1,0:T(4,128)(2,1)}), bf16[4,2,4,1152]{3,2,1,0:T(4,128)(2,1)S(1)}, u32[]{:S(2)}, u32[]{:S(2)}) async-start(bf16[4,2,4,1152]{3,2,1,0:T(4,128)(2,1)} %broadcast_in_dim.78), calls=%async_computation | async-start | bytes 147456 | tf_op jit(solution)/shard_map/all_to_all | solution.py:13
  24.0 31.5 %all-gather.3.cloned.1.call-done = bf16[8,288,256]{2,1,0:T(8,128)(2,1)} async-done(((bf16[2,288,256]{2,1,0:T(8,128)(2,1)}), bf16[8,288,256]{2,1,0:T(8,128)(2,1)}) %all-gather.3.cloned.1.call-update) | async-done | bytes 1179664 | tf_op jit(solution)/shard_map/all_gather | solution.py:73
  56.8 1.5 fusion.18
  62.6 1.8 fusion.126
  64.3 1.8 fusion.14
  66.8 2.6 %convolution_convert_fusion.5 = bf16[4,72,256]{2,1,0:T(8,128)(2,1)} fusion(bf16[4,72,256]{2,1,0:T(8,128)(2,1)} %bitcast.114, f32[4,256]{1,0:T(4,128)} %fusion.126, f32[4,256,256]{1,2,0:T(8,128)} %fusion.12), kind=kOutput, calls=%fused_computation.37 | convolution fusion | flops 38610176 | bytes 1347584 | tf_op jit(solution)/shard_map/hek,hqk->heq/dot_general | solution.py:101
  70.7 12.2 %all-to-all-start.3 = ((bf16[128,2,1280]{2,1,0:T(2,128)(2,1)}), bf16[128,2,1280]{2,1,0:T(2,128)(2,1)}, u32[]{:S(2)}, u32[]{:S(2)}) async-start(bf16[128,2,1280]{2,1,0:T(2,128)(2,1)} %broadcast_in_dim.88), calls=%async_computation.3 | async-start | bytes 1310720 | tf_op jit(solution)/shard_map/all_to_all | solution.py:13
  84.2 1.3 fusion.11
  85.5 2.0 convolution_convert_fusion.4
  87.6 1.7 convolution_convert_fusion.1
  90.9 12.9 %all-to-all-done.3 = bf16[128,2,1280]{2,1,0:T(2,128)(2,1)} async-done(((bf16[128,2,1280]{2,1,0:T(2,128)(2,1)}), bf16[128,2,1280]{2,1,0:T(2,128)(2,1)}, u32[]{:S(2)}, u32[]{:S(2)}) %all-to-all-start.3) | async-done | bytes 655392 | tf_op jit(solution)/shard_map/all_to_all | solution.py:13
  103.8 4.3 %all-to-all-start.1 = ((bf16[4,128,1152]{2,1,0:T(8,128)(2,1)}), bf16[4,128,1152]{2,1,0:T(8,128)(2,1)}, u32[]{:S(2)}, u32[]{:S(2)}) async-start(bf16[4,128,1152]{2,1,0:T(8,128)(2,1)} %pad_maximum_fusion), calls=%async_computation.1 | async-start | bytes 2359296 | tf_op jit(solution)/shard_map/all_to_all | solution.py:106
  110.9 2.7 %reshape.257 = bf16[256,1280]{1,0:T(8,128)(2,1)} reshape(bf16[128,2,1280]{2,1,0:T(2,128)(2,1)} %all-to-all-done.3) | data formatting | bytes 1310720 | tf_op jit(solution)/shard_map/reshape | solution.py:78
  115.5 17.0 %all-to-all-done.1 = bf16[4,128,1152]{2,1,0:T(8,128)(2,1)} async-done(((bf16[4,128,1152]{2,1,0:T(8,128)(2,1)}), bf16[4,128,1152]{2,1,0:T(8,128)(2,1)}, u32[]{:S(2)}, u32[]{:S(2)}) %all-to-all-start.1) | async-done | bytes 1179680 | tf_op jit(solution)/shard_map/all_to_all | solution.py:106
  132.4 1.5 convert_reduce_fusion
  136.4 7.0 %all-to-all-start.2 = ((f32[4,4,1280]{2,1,0:T(4,128)}), f32[4,4,1280]{2,1,0:T(4,128)S(1)}, u32[]{:S(2)}, u32[]{:S(2)}) async-start(f32[4,4,1280]{2,1,0:T(4,128)} %reshape.253), calls=%async_computation.2 | async-start | bytes 163840 | tf_op jit(solution)/shard_map/all_to_all | solution.py:123
  143.5 6.8 %all-to-all-done.2 = f32[4,4,1280]{2,1,0:T(4,128)S(1)} async-done(((f32[4,4,1280]{2,1,0:T(4,128)}), f32[4,4,1280]{2,1,0:T(4,128)S(1)}, u32[]{:S(2)}, u32[]{:S(2)}) %all-to-all-start.2) | async-done | bytes 81952 | tf_op jit(solution)/shard_map/all_to_all | solution.py:123
  150.4 2.0 copy.43
  154.4 6.3 %fusion.2 = f32[2,4,1152]{1,0,2:T(2,128)} fusion(f32[2,2,4,1280]{2,1,0,3:T(2,128)} %bitcast.97, f32[2,2,4]{2,1,0:T(2,128)S(1)} %divide_bitcast_fusion), kind=kLoop, calls=%fused_computation.5 | loop fusion | flops 27648 | bytes 110656 | tf_op jit(solution)/shard_map/reduce_sum | solution.py:127
  160.8 1.6 copy.44
  162.4 1.4 fusion.32
  164.1 7.6 %psum.7 = f32[2,1152]{1,0:T(2,128)S(1)} all-reduce(f32[2,1152]{1,0:T(2,128)S(1)} %fusion.132), channel_id=1, replica_groups=mesh['dp'=128,'mp'=4] {'mp'}, use_global_device_ids=true, to_apply=%region_17.18 | all-reduce | flops 2304 | bytes 18432 | tf_op jit(solution)/shard_map/psum | solution.py:130
  173.1 12.9 %all-to-all-start.4 = ((bf16[128,2,1152]{2,1,0:T(2,128)(2,1)}), bf16[128,2,1152]{2,1,0:T(2,128)(2,1)S(1)}, u32[]{:S(2)}, u32[]{:S(2)}) async-start(bf16[128,2,1152]{2,1,0:T(2,128)(2,1)} %broadcast_in_dim.142), calls=%async_computation.4 | async-start | bytes 1179648 | tf_op jit(solution)/shard_map/all_to_all | solution.py:13
  187.5 18.6 %all-to-all-done.4 = bf16[128,2,1152]{2,1,0:T(2,128)(2,1)S(1)} async-done(((bf16[128,2,1152]{2,1,0:T(2,128)(2,1)}), bf16[128,2,1152]{2,1,0:T(2,128)(2,1)S(1)}, u32[]{:S(2)}, u32[]{:S(2)}) %all-to-all-start.4) | async-done | bytes 589856 | tf_op jit(solution)/shard_map/all_to_all | solution.py:13
  (111 shorter events, 27.5 us)
Async XLA Ops:
  7.2 52.6 %copy-start = (bf16[3,1152,288]{1,2,0:T(8,128)(2,1)S(1)}, bf16[3,1152,288]{1,2,0:T(8,128)(2,1)}, u32[]{:S(2)}) copy-start(bf16[3,1152,288]{1,2,0:T(8,128)(2,1)} %param.16) | copy-start | bytes 5971972
  7.2 13.7 %copy-start.10 = (f32[1152]{0:T(1024)S(1)}, f32[1152]{0:T(1024)}, u32[]{:S(2)}) copy-start(f32[1152]{0:T(1024)} %param.15) | copy-start | bytes 13828
  7.2 13.7 %copy-start.14 = (s32[2]{0:T(128)S(1)}, s32[2]{0:T(128)}, u32[]{:S(2)}) copy-start(s32[2]{0:T(128)} %param.23) | copy-start | bytes 28
  7.2 13.7 %copy-start.11 = (s32[2]{0:T(128)S(1)}, s32[2]{0:T(128)}, u32[]{:S(2)}) copy-start(s32[2]{0:T(128)} %param.14) | copy-start | bytes 28
  7.2 16.8 %copy-start.6 = (bf16[2,1152]{1,0:T(2,128)(2,1)S(1)}, bf16[2,1152]{1,0:T(2,128)(2,1)}, u32[]{:S(2)}) copy-start(bf16[2,1152]{1,0:T(2,128)(2,1)} %param.22) | copy-start | bytes 13828
  7.2 48.3 %all-gather.3.cloned.1.call-start = ((), (), s32[]{:S(2)}) async-start(), calls=%async_computation.5 | async-start | bytes 1474560 | tf_op jit(solution)/shard_map/all_gather | solution.py:73
  8.0 1.3 copy-start.7
  10.0 59.5 %all-to-all-start = ((bf16[4,2,4,1152]{3,2,1,0:T(4,128)(2,1)}), bf16[4,2,4,1152]{3,2,1,0:T(4,128)(2,1)S(1)}, u32[]{:S(2)}, u32[]{:S(2)}) async-start(bf16[4,2,4,1152]{3,2,1,0:T(4,128)(2,1)} %broadcast_in_dim.78), calls=%async_computation | async-start | bytes 147456 | tf_op jit(solution)/shard_map/all_to_all | solution.py:13
  55.5 2.9 %copy-start.1 = (bf16[8,288,256]{2,1,0:T(8,128)(2,1)S(1)}, bf16[8,288,256]{2,1,0:T(8,128)(2,1)}, u32[]{:S(2)}) copy-start(bf16[8,288,256]{2,1,0:T(8,128)(2,1)} %all-gather.3.cloned.1.call-done) | copy-start | bytes 3538948
  59.8 1.4 copy-start.13
  70.7 33.1 %all-to-all-start.3 = ((bf16[128,2,1280]{2,1,0:T(2,128)(2,1)}), bf16[128,2,1280]{2,1,0:T(2,128)(2,1)}, u32[]{:S(2)}, u32[]{:S(2)}) async-start(bf16[128,2,1280]{2,1,0:T(2,128)(2,1)} %broadcast_in_dim.88), calls=%async_computation.3 | async-start | bytes 1310720 | tf_op jit(solution)/shard_map/all_to_all | solution.py:13
  82.9 1.3 copy-start.12
  85.5 2.0 copy-start.5
  87.5 1.7 copy-start.3
  103.8 28.6 %all-to-all-start.1 = ((bf16[4,128,1152]{2,1,0:T(8,128)(2,1)}), bf16[4,128,1152]{2,1,0:T(8,128)(2,1)}, u32[]{:S(2)}, u32[]{:S(2)}) async-start(bf16[4,128,1152]{2,1,0:T(8,128)(2,1)} %pad_maximum_fusion), calls=%async_computation.1 | async-start | bytes 2359296 | tf_op jit(solution)/shard_map/all_to_all | solution.py:106
  134.0 0.7 copy-start.9
  134.2 9.2 %copy-start.2 = (bf16[256,1280]{1,0:T(8,128)(2,1)S(1)}, bf16[256,1280]{1,0:T(8,128)(2,1)}, u32[]{:S(2)}) copy-start(bf16[256,1280]{1,0:T(8,128)(2,1)} %reshape.257) | copy-start | bytes 1966084
  136.4 13.9 %all-to-all-start.2 = ((f32[4,4,1280]{2,1,0:T(4,128)}), f32[4,4,1280]{2,1,0:T(4,128)S(1)}, u32[]{:S(2)}, u32[]{:S(2)}) async-start(f32[4,4,1280]{2,1,0:T(4,128)} %reshape.253), calls=%async_computation.2 | async-start | bytes 163840 | tf_op jit(solution)/shard_map/all_to_all | solution.py:123
  160.8 3.1 %copy-start.8 = (pred[4,288]{1,0:T(4,128)(4,1)S(1)}, pred[4,288]{1,0:T(4,128)(4,1)}, u32[]{:S(2)}) copy-start(pred[4,288]{1,0:T(4,128)(4,1)} %copy-done.7) | copy-start | bytes 3460
  160.8 3.2 %copy-start.4 = (bf16[288,1152]{1,0:T(8,128)(2,1)S(1)}, bf16[288,1152]{1,0:T(8,128)(2,1)}, u32[]{:S(2)}) copy-start(bf16[288,1152]{1,0:T(8,128)(2,1)} %param.21) | copy-start | bytes 1990660
  172.0 14.3 %copy-start.15 = (s32[2]{0:T(128)S(1)}, s32[2]{0:T(128)}, u32[]{:S(2)}) copy-start(s32[2]{0:T(128)} %param.23) | copy-start | bytes 28
  173.1 33.0 %all-to-all-start.4 = ((bf16[128,2,1152]{2,1,0:T(2,128)(2,1)}), bf16[128,2,1152]{2,1,0:T(2,128)(2,1)S(1)}, u32[]{:S(2)}, u32[]{:S(2)}) async-start(bf16[128,2,1152]{2,1,0:T(2,128)(2,1)} %broadcast_in_dim.142), calls=%async_computation.4 | async-start | bytes 1179648 | tf_op jit(solution)/shard_map/all_to_all | solution.py:13
Sparse Core Ops, SparseCore 0:
  10.2 45.2 all-gather.2

commit v2 on v1

v2 whole, which is shorter than its diff:
```python
import math

import jax
import jax.numpy as jnp
from jax import lax
from jax.experimental import pallas as pl
from jax.experimental.pallas import tpu as pltpu
from jax.sharding import PartitionSpec as P

HDIM = 72


def spread_all(value, axis):
    count = lax.axis_size(axis)
    return lax.all_to_all(jnp.broadcast_to(value[None], (count,) + value.shape), axis, 0, 0)


def shift(value, steps):
    count = lax.axis_size("mp")
    pairs = [(source, (source + steps) % count) for source in range(count)]
    return lax.ppermute(value, "mp", pairs)


def layer_norm(values, gain_vec):
    floats = values.astype(jnp.float32)
    center = floats - jnp.mean(floats, axis=-1, keepdims=True)
    spread = jnp.mean(center * center, axis=-1, keepdims=True)
    return center * lax.rsqrt(spread + 1e-06) * gain_vec


def split_bf16(values, terms):
    pieces = []
    for _ in range(terms):
        top = values.astype(jnp.bfloat16)
        pieces.append(top)
        values = values - top.astype(jnp.float32)
    return pieces


def matmul(left, right, dims=(((1,), (0,)), ((), ()))):
    return lax.dot_general(left, right, dims, preferred_element_type=jnp.float32)


NT = (((1,), (1,)), ((), ()))


def attend_kernel(count_ref, x_ref, w_ref, out_w_ref, gain_ref, o_ref, ctx_ref):
    f32, bf16 = jnp.float32, jnp.bfloat16
    shards, dlocal, pmax = x_ref.shape
    width = shards * dlocal
    count = count_ref[0]
    floats = x_ref[...].reshape(width, pmax).astype(f32)
    center = floats - jnp.sum(floats, axis=0, keepdims=True) * (1.0 / width)
    spread = jnp.sum(center * center, axis=0, keepdims=True) * (1.0 / width)
    normed = (center * lax.rsqrt(spread + 1e-06) * gain_ref[...]).astype(bf16)
    proj = matmul(w_ref[...], normed)
    live = lax.broadcasted_iota(jnp.int32, (pmax, pmax), 0) < count
    for h in range(dlocal // HDIM):
        q, k, v = (proj[c * dlocal + h * HDIM : c * dlocal + (h + 1) * HDIM] for c in range(3))
        scores = matmul(k.T.astype(bf16), q.astype(bf16)) * (1.0 / math.sqrt(HDIM))
        scores = jnp.where(live, scores, -1e30)
        raised = jnp.exp(scores - jnp.max(scores, axis=0, keepdims=True))
        total = jnp.sum(raised, axis=0, keepdims=True)
        ctx_ref[h * HDIM : (h + 1) * HDIM] = matmul(v.astype(bf16), raised.astype(bf16)) / total
    context = ctx_ref[...].T.astype(bf16)
    o_ref[...] = matmul(context, out_w_ref[...]).astype(bf16)


def attend(count, slices, w_rows, w_out, gain):
    shards, dlocal, pmax = slices.shape
    width = w_rows.shape[1]
    flops = 2 * pmax * (3 * dlocal * width + 2 * dlocal * pmax + dlocal * width)
    return pl.pallas_call(
        attend_kernel,
        in_specs=[pl.BlockSpec(memory_space=pltpu.SMEM)] + [pl.BlockSpec(memory_space=pltpu.VMEM)] * 4,
        out_specs=pl.BlockSpec(memory_space=pltpu.VMEM),
        out_shape=jax.ShapeDtypeStruct((pmax, width), jnp.bfloat16),
        scratch_shapes=[pltpu.VMEM((dlocal, pmax), jnp.float32)],
        compiler_params=pltpu.CompilerParams(vmem_limit_bytes=40 * 1024 * 1024),
        cost_estimate=pl.CostEstimate(
            flops=flops, bytes_accessed=8 * width * dlocal + 4 * pmax * width, transcendentals=0
        ),
        name="attend",
    )(count.reshape(1), slices, w_rows, w_out, gain)


def pool_kernel(halves_ref, val_ref, out_w_ref, o_ref):
    f32, bf16 = jnp.float32, jnp.bfloat16
    dlocal, width = out_w_ref.shape
    heads = dlocal // HDIM
    images = halves_ref.shape[0] // (2 * heads)
    mixed = []
    for i in range(images):
        first = halves_ref[2 * i * heads : (2 * i + 1) * heads]
        second = halves_ref[(2 * i + 1) * heads : (2 * i + 2) * heads]
        lse_a, lse_b = first[:, width : width + 1], second[:, width : width + 1]
        top = jnp.maximum(lse_a, lse_b)
        raised_a, raised_b = jnp.exp(lse_a - top), jnp.exp(lse_b - top)
        total = raised_a + raised_b
        mixed.append(first[:, :width] * (raised_a / total) + second[:, :width] * (raised_b / total))
    mixed = jnp.concatenate(mixed, axis=0)
    rows = images * heads
    terms = []
    for _ in range(2):
        top = mixed.astype(bf16).astype(f32)
        terms.append(top)
        mixed = mixed - top
    vals = matmul(jnp.concatenate(terms, axis=0).astype(bf16), val_ref[0], NT)
    vals = vals[:rows] + vals[rows:]
    row = lax.broadcasted_iota(jnp.int32, (rows, dlocal), 0)
    lane = lax.broadcasted_iota(jnp.int32, (rows, dlocal), 1)
    start = (row % heads) * HDIM
    vals = jnp.where((lane >= start) & (lane < start + HDIM), vals, 0.0)
    pooled = [jnp.sum(vals[i * heads : (i + 1) * heads], axis=0, keepdims=True) for i in range(images)]
    pooled.append(jnp.zeros((16 - images, dlocal), f32))
    pooled = jnp.concatenate(pooled, axis=0).astype(bf16)
    o_ref[...] = matmul(pooled, out_w_ref[...])[:images]


def pool_embed(halves, pool_kv_rows, pool_out):
    dlocal, width = pool_out.shape
    images = halves.shape[0] // (2 * (dlocal // HDIM))
    return pl.pallas_call(
        pool_kernel,
        grid=(1,),
        in_specs=[
            pl.BlockSpec(halves.shape, lambda i: (0, 0)),
            pl.BlockSpec((1, dlocal, width), lambda i: (1, 0, 0)),
            pl.BlockSpec((dlocal, width), lambda i: (0, 0)),
        ],
        out_specs=pl.BlockSpec((images, width), lambda i: (0, 0)),
        out_shape=jax.ShapeDtypeStruct((images, width), jnp.float32),
        compiler_params=pltpu.CompilerParams(vmem_limit_bytes=24 * 1024 * 1024),
        name="pool_embed",
    )(halves, pool_kv_rows, pool_out)


def per_device(
    patches,
    patch_count,
    ln1_gain,
    w_qkv,
    w_out,
    ln2_gain,
    pool_kv,
    pool_query,
    pool_out,
    text_emb,
    image_pair,
    logit_scale,
    logit_bias,
):
    f32, bf16 = jnp.float32, jnp.bfloat16
    rows_img, pmax, dlocal = patches.shape
    width = w_out.shape[1]
    local_heads = dlocal // HDIM
    heads = width // HDIM
    shards = lax.axis_size("mp")
    me = lax.axis_index("mp")
    rank = lax.axis_index(("plane", "near"))
    half = pmax // 2
    nt = (((1,), (1,)), ((), ()))

    def dot(left, right, dims=(((1,), (0,)), ((), ()))):
        return lax.dot_general(left, right, dims, preferred_element_type=f32)

    def dot_exact(left, right, dims=(((1,), (0,)), ((), ()))):
        rows = left.shape[0]
        product = dot(jnp.concatenate(split_bf16(left, 3), axis=0), right, dims)
        return product[:rows] + product[rows : 2 * rows] + product[2 * rows :]

    my_image, my_half = me // 2, me % 2
    tall = patches.transpose(0, 2, 1)
    x_other = lax.all_to_all(jnp.stack([tall[1 - d // 2] for d in range(shards)]), "mp", 0, 0)
    x_mine = lax.all_to_all(jnp.stack([tall[d // 2] for d in range(shards)]), "mp", 0, 0)

    texts_pairs = jnp.concatenate(
        [text_emb, jnp.broadcast_to(image_pair.astype(bf16)[:, None], (rows_img, 128))], axis=1
    )
    texts_pairs, x_other = lax.optimization_barrier((texts_pairs, x_other))
    texts_pairs = spread_all(texts_pairs, ("plane", "near")).reshape(-1, width + 128)
    text_all, pair_all = texts_pairs[:, :width], texts_pairs[:, width].astype(jnp.int32)
    texts = text_all.astype(f32)
    inv_txt = lax.rsqrt(jnp.sum(texts * texts, axis=-1) + 1e-06)

    head_of = jnp.arange(dlocal, dtype=jnp.int32) // HDIM
    own_head = head_of[None, :] == jnp.arange(local_heads, dtype=jnp.int32)[:, None]
    probe = jnp.where(own_head, pool_query[None, :], 0).astype(bf16)
    probe_keys = dot(probe, pool_kv[0], nt) * (1.0 / math.sqrt(HDIM))
    probe_all = spread_all(jnp.stack(split_bf16(probe_keys, 2)), "mp")
    probe_all = probe_all.transpose(1, 0, 2, 3).reshape(2 * heads, width)

    w_rows = w_qkv.transpose(0, 2, 1).reshape(3 * dlocal, width)
    gain = ln1_gain[:, None]
    my_count = jnp.where(my_image == 0, patch_count[0], patch_count[1])
    other_count = jnp.where(my_image == 0, patch_count[1], patch_count[0])
    first = attend(other_count, x_other, w_rows, w_out, gain)
    second = attend(my_count, x_mine, w_rows, w_out, gain)

    quarter = half // 2
    far = lax.dynamic_slice(first, (my_half * half, 0), (half, width))
    far_after, far_before = shift(far[:quarter], 1), shift(far[quarter:], -1)
    even = my_half == 0
    after = jnp.where(even, second[half:], first[:half])
    before = jnp.where(even, first[half:], second[:half])
    own_part = jnp.where(even, second[:half], second[half:]).astype(f32)

    def added(left, right):
        return (left.astype(f32) + right.astype(f32)).astype(bf16)

    after = jnp.concatenate([added(after[:quarter], far_after), after[quarter:]], axis=0)
    before = jnp.concatenate([before[:quarter], added(before[quarter:], far_before)], axis=0)
    parts = own_part + shift(after, 1).astype(f32) + shift(before, -1).astype(f32)
    mine = x_mine.reshape(width, pmax)
    resid = jnp.where(my_half == 0, mine[:, :half], mine[:, half:]).T
    stream = (resid.astype(f32) + parts).astype(bf16)
    normed2 = layer_norm(stream, ln2_gain).astype(bf16)
    both = dot(probe_all, normed2, nt)
    pool_scores = both[:heads] + both[heads:]
    row_ids = my_half * half + jnp.arange(half, dtype=jnp.int32)
    pool_scores = jnp.where((row_ids < my_count)[None, :], pool_scores, -1e30)
    highest = jnp.max(pool_scores, axis=-1, keepdims=True)
    raised = jnp.exp(pool_scores - highest)
    total = jnp.sum(raised, axis=-1, keepdims=True)
    mixed = dot((raised / total).astype(bf16), normed2)
    lse = jnp.broadcast_to(highest + jnp.log(total), (heads, 128))
    send = jnp.concatenate([mixed, lse], axis=1).reshape(shards, local_heads, width + 128)
    halves = lax.all_to_all(send, "mp", 0, 0).reshape(shards * local_heads, width + 128)
    shares = pool_embed(halves, pool_kv.transpose(0, 2, 1), pool_out)

    shares = spread_all(shares, ("near", "mp"))
    embeds = jnp.sum(shares.reshape(-1, shards, rows_img, width), axis=1).reshape(-1, width)
    inv_img = lax.rsqrt(jnp.sum(embeds * embeds, axis=-1, keepdims=True) + 1e-06)
    zimg_near = embeds * inv_img
    start = lax.axis_index("near") * rows_img
    zimg_own = lax.dynamic_slice(zimg_near, (start, 0), (rows_img, width))
    inv_img_own = lax.dynamic_slice(inv_img, (start, 0), (rows_img, 1))
    zimg = spread_all(zimg_near.astype(bf16), "plane").reshape(-1, width)

    scale = jnp.exp(logit_scale)
    own_ids = rank * rows_img + jnp.arange(rows_img, dtype=jnp.int32)
    every = jnp.arange(zimg.shape[0], dtype=jnp.int32)
    text_own = text_emb.astype(f32)
    inv_txt_own = lax.rsqrt(jnp.sum(text_own * text_own, axis=-1, keepdims=True) + 1e-06)
    ztxt_own = text_own * inv_txt_own

    def slope(logits, is_pair):
        label = jnp.where(is_pair, 1.0, -1.0).astype(f32)
        return -label * jax.nn.sigmoid(-label * logits)

    logits_img = scale * dot_exact(zimg_own, text_all, nt) * inv_txt[None, :] + logit_bias
    dlog_img = slope(logits_img, image_pair[:, None] == every[None, :])
    logits_txt = scale * dot(text_emb, zimg, nt) * inv_txt_own + logit_bias
    dlog_txt = slope(logits_txt, pair_all[None, :] == own_ids[:, None])
    gimg = scale * dot_exact(dlog_img * inv_txt[None, :], text_all)
    gtxt = scale * dot_exact(dlog_txt, zimg)
    image_grad = (gimg - zimg_own * jnp.sum(zimg_own * gimg, axis=-1, keepdims=True)) * inv_img_own
    text_grad = (gtxt - ztxt_own * jnp.sum(ztxt_own * gtxt, axis=-1, keepdims=True)) * inv_txt_own
    return (image_grad, text_grad)


def solution(mesh):
    shards = mesh.shape["mp"]
    devices = mesh.devices.reshape(-1, 4, shards)
    fine = jax.sharding.Mesh(devices, ("plane", "near", "mp"))
    dp = ("plane", "near")
    placed = (
        P(dp, None, "mp"),
        P(dp),
        P(),
        P(None, None, "mp"),
        P("mp", None),
        P(),
        P(None, None, "mp"),
        P("mp"),
        P("mp", None),
        P(dp, None),
        P(dp),
        P(),
        P(),
    )
    return jax.shard_map(
        per_device,
        mesh=fine,
        in_specs=placed,
        out_specs=(P(dp, None), P(dp, None)),
        check_vma=False,
    )
```

time: 216 us -> 181 us (0.84)
  the two profiles are of different devices: /device:TPU:1 before, /device:TPU:8 now
where the time goes in v2:
time: 181 us; the launch traced here: 180 us
  waiting for transfers between devices  70.4 us (39%)
  starting transfers between devices  56.5 us (31%)
  blocking collectives  20.4 us (11%)
  local copies, waits for them, and re-layouts  11.3 us (6%)
  Pallas kernels  8 us (4%)
  other arithmetic  5.37 us (3%)
  between operations  5.11 us (3%)
  matrix products  2.69 us (1%)
    all_to_all x4, waiting for transfers between devices, spread_all(): lax.all_to_all(jnp.broadcast_to(value[None], (count,) + value.shape), axi...  51.8 us
    all_to_all x4, starting transfers between devices, spread_all(): lax.all_to_all(jnp.broadcast_to(value[None], (count,) + value.shape), axi...  32.9 us
    all_to_all x1, blocking collectives, per_device(): lax.all_to_all(jnp.stack([tall[1 - d // 2] for d in range(shards)]), 'mp'...  20.4 us
    ppermute x4, starting transfers between devices, shift(): return lax.ppermute(value, 'mp', pairs)  16 us
    ppermute x4, waiting for transfers between devices, shift(): return lax.ppermute(value, 'mp', pairs)  10.4 us
    all_to_all x1, waiting for transfers between devices, per_device(): lax.all_to_all(send, 'mp', 0, 0).reshape(shards * local_heads, width + 128)  8.21 us
    pallas_call x2, Pallas kernels, attend(): pl.pallas_call(attend_kernel, in_specs=[pl.BlockSpec(memory_space=pltpu.S...  7.31 us
    all_to_all x1, starting transfers between devices, per_device(): lax.all_to_all(send, 'mp', 0, 0).reshape(shards * local_heads, width + 128)  3.98 us
  transfers between devices with their start and end apart: 10, of which 8 were waited for; matrix products, arithmetic and copies ran while one was open for 4% of the time, Pallas kernels for 4%

profile of v2, /device:TPU:8, one launch (start us, length us, event | category | flops | bytes accessed | tf_op | source)
XLA Modules:
  0.0 179.7 jit_solution(5591067467171082991)
XLA Ops:
  0.7 1.4 convert_bitcast_fusion
  2.7 10.3 %all-to-all-start = ((bf16[4,2,4,1152]{3,2,1,0:T(4,128)(2,1)}), bf16[4,2,4,1152]{3,2,1,0:T(4,128)(2,1)S(1)}, u32[]{:S(2)}, u32[]{:S(2)}) async-start(bf16[4,2,4,1152]{3,2,1,0:T(4,128)(2,1)} %broadcast_in_dim.51), calls=%async_computation | async-start | bytes 147456 | tf_op jit(solution)/shard_map/all_to_all | solution.py:15
  14.9 6.5 %all-to-all-done = bf16[4,2,4,1152]{3,2,1,0:T(4,128)(2,1)S(1)} async-done(((bf16[4,2,4,1152]{3,2,1,0:T(4,128)(2,1)}), bf16[4,2,4,1152]{3,2,1,0:T(4,128)(2,1)S(1)}, u32[]{:S(2)}, u32[]{:S(2)}) %all-to-all-start) | async-done | bytes 73760 | tf_op jit(solution)/shard_map/all_to_all | solution.py:15
  21.5 20.4 %all_to_all.35.x_ref = bf16[4,288,256]{2,1,0:T(8,128)(2,1)} all-to-all(bf16[4,288,256]{2,1,0:T(8,128)(2,1)S(1)} %get-tuple-element.25), channel_id=1, replica_groups=mesh['plane'=32,'near'=4,'mp'=4] {'mp'}, dimensions={0} | all-to-all | bytes 1179648 | tf_op jit(solution)/shard_map/all_to_all | solution.py:174
  41.8 3.6 %all-to-all-start.1 = ((bf16[4,288,256]{2,1,0:T(8,128)(2,1)}), bf16[4,288,256]{2,1,0:T(8,128)(2,1)S(1)}, u32[]{:S(2)}, u32[]{:S(2)}) async-start(bf16[4,288,256]{2,1,0:T(8,128)(2,1)} %get-tuple-element.24), calls=%async_computation.1 | async-start | bytes 1179648 | tf_op jit(solution)/shard_map/all_to_all | solution.py:175
  51.7 3.7 %attend.3 = bf16[256,1152]{1,0:T(8,128)(2,1)S(1)} custom-call(s32[1]{0:T(128)} %bitcast.12.count_ref, bf16[4,288,256]{2,1,0:T(8,128)(2,1)S(1)} %copy-done.8, bf16[864,1152]{1,0:T(8,128)(2,1)S(1)} %bitcast.54, bf16[288,1152]{1,0:T(8,128)(2,1)S(1)} %copy-done.6, f32[1152,1]{1,0:T(8,128)S(1)} %broadcast_in_dim.61.gain_ref), custom_call_target="tpu_custom_call" | custom-call | flops 754974720 | bytes 3833856 | tf_op jit(solution)/shard_map/attend/pallas_call | solution.py:73
  56.3 6.0 %collective-permute-start.2 = (bf16[64,1152]{1,0:T(8,128)(2,1)}, bf16[64,1152]{1,0:T(8,128)(2,1)S(1)}, u32[]{:S(2)}, u32[]{:S(2)}) collective-permute-start(bf16[64,1152]{1,0:T(8,128)(2,1)} %get-tuple-element.23), channel_id=1, source_target_pairs={{0,3},{1,0},{2,1},{3,2},{4,7},{5,4},{6,5},{7,6},{8,11},{9,8},{10,9... | collective-permute-start | bytes 442376 | tf_op jit(solution)/shard_map/ppermute | solution.py:21
  62.3 1.1 copy-done.7
  63.4 3.7 %attend.2 = bf16[256,1152]{1,0:T(8,128)(2,1)S(1)} custom-call(s32[1]{0:T(128)} %bitcast.9.count_ref, bf16[4,288,256]{2,1,0:T(8,128)(2,1)S(1)} %all-to-all-done.1.x_ref, bf16[864,1152]{1,0:T(8,128)(2,1)S(1)} %bitcast.55, bf16[288,1152]{1,0:T(8,128)(2,1)S(1)} %copy-done.7, f32[1152,1]{1,0:T(8,128)S(1)} %broadcast_in_dim.61.gain_ref), custom_call_target="tpu_custom_call" | custom-call | flops 754974720 | bytes 3833856 | tf_op jit(solution)/shard_map/attend/pallas_call | solution.py:73
  67.2 1.9 %collective-permute-start = (bf16[64,1152]{1,0:T(8,128)(2,1)S(1)}, bf16[64,1152]{1,0:T(8,128)(2,1)S(1)}, u32[]{:S(2)}, u32[]{:S(2)}) collective-permute-start(bf16[64,1152]{1,0:T(8,128)(2,1)S(1)} %get-tuple-element.22), channel_id=1, source_target_pairs={{0,1},{1,2},{2,3},{3,0},{4,5},{5,6},{6,7},{7,4},{8,9},{9,10},{10,1... | collective-permute-start | bytes 442376 | tf_op jit(solution)/shard_map/ppermute | solution.py:21
  69.2 6.0 %collective-permute-start.3 = (bf16[128,1152]{1,0:T(8,128)(2,1)S(1)}, bf16[128,1152]{1,0:T(8,128)(2,1)S(1)}, u32[]{:S(2)}, u32[]{:S(2)}) collective-permute-start(bf16[128,1152]{1,0:T(8,128)(2,1)S(1)} %pad_maximum_fusion.3), channel_id=1, source_target_pairs={{0,3},{1,0},{2,1},{3,2},{4,7},{5,4},{6,5},{7,6},{8,11},{9,8},{10,9... | collective-permute-start | bytes 884744 | tf_op jit(solution)/shard_map/ppermute | solution.py:21
  75.2 2.0 %collective-permute-done = bf16[64,1152]{1,0:T(8,128)(2,1)S(1)} collective-permute-done((bf16[64,1152]{1,0:T(8,128)(2,1)S(1)}, bf16[64,1152]{1,0:T(8,128)(2,1)S(1)}, u32[]{:S(2)}, u32[]{:S(2)}) %collective-permute-start) | collective-permute-done | bytes 147488 | tf_op jit(solution)/shard_map/ppermute | solution.py:21
  77.3 2.1 %collective-permute-start.1 = (bf16[128,1152]{1,0:T(8,128)(2,1)S(1)}, bf16[128,1152]{1,0:T(8,128)(2,1)S(1)}, u32[]{:S(2)}, u32[]{:S(2)}) collective-permute-start(bf16[128,1152]{1,0:T(8,128)(2,1)S(1)} %pad_maximum_fusion.2), channel_id=1, source_target_pairs={{0,1},{1,2},{2,3},{3,0},{4,5},{5,6},{6,7},{7,4},{8,9},{9,10},{10,1... | collective-permute-start | bytes 884744 | tf_op jit(solution)/shard_map/ppermute | solution.py:21
  79.9 4.3 %collective-permute-done.3 = bf16[128,1152]{1,0:T(8,128)(2,1)S(1)} collective-permute-done((bf16[128,1152]{1,0:T(8,128)(2,1)S(1)}, bf16[128,1152]{1,0:T(8,128)(2,1)S(1)}, u32[]{:S(2)}, u32[]{:S(2)}) %collective-permute-start.3) | collective-permute-done | bytes 294944 | tf_op jit(solution)/shard_map/ppermute | solution.py:21
  84.2 4.1 %collective-permute-done.1 = bf16[128,1152]{1,0:T(8,128)(2,1)S(1)} collective-permute-done((bf16[128,1152]{1,0:T(8,128)(2,1)S(1)}, bf16[128,1152]{1,0:T(8,128)(2,1)S(1)}, u32[]{:S(2)}, u32[]{:S(2)}) %collective-permute-start.1) | collective-permute-done | bytes 294944 | tf_op jit(solution)/shard_map/ppermute | solution.py:21
  90.6 4.0 %all-to-all-start.3 = ((f32[4,4,1280]{2,1,0:T(4,128)}), f32[4,4,1280]{2,1,0:T(4,128)S(1)}, u32[]{:S(2)}, u32[]{:S(2)}) async-start(f32[4,4,1280]{2,1,0:T(4,128)} %reshape.154), calls=%async_computation.3 | async-start | bytes 163840 | tf_op jit(solution)/shard_map/all_to_all | solution.py:228
  94.7 8.2 %all-to-all-done.3 = f32[4,4,1280]{2,1,0:T(4,128)S(1)} async-done(((f32[4,4,1280]{2,1,0:T(4,128)}), f32[4,4,1280]{2,1,0:T(4,128)S(1)}, u32[]{:S(2)}, u32[]{:S(2)}) %all-to-all-start.3) | async-done | bytes 81952 | tf_op jit(solution)/shard_map/all_to_all | solution.py:228
  104.4 5.4 %all-to-all-start.4 = ((f32[16,2,1152]{2,1,0:T(2,128)}), f32[16,2,1152]{2,1,0:T(2,128)S(1)}, u32[]{:S(2)}, u32[]{:S(2)}) async-start(f32[16,2,1152]{2,1,0:T(2,128)} %broadcast_in_dim.58), calls=%async_computation.4 | async-start | bytes 294912 | tf_op jit(solution)/shard_map/all_to_all | solution.py:15
  111.2 7.3 %all-to-all-done.4 = f32[16,2,1152]{2,1,0:T(2,128)S(1)} async-done(((f32[16,2,1152]{2,1,0:T(2,128)}), f32[16,2,1152]{2,1,0:T(2,128)S(1)}, u32[]{:S(2)}, u32[]{:S(2)}) %all-to-all-start.4) | async-done | bytes 147488 | tf_op jit(solution)/shard_map/all_to_all | solution.py:15
  118.5 1.2 broadcast_in_dim.59
  119.7 12.3 %all-to-all-start.5 = ((bf16[128,2,1280]{2,1,0:T(2,128)(2,1)}), bf16[128,2,1280]{2,1,0:T(2,128)(2,1)S(1)}, u32[]{:S(2)}, u32[]{:S(2)}) async-start(bf16[128,2,1280]{2,1,0:T(2,128)(2,1)} %broadcast_in_dim.59), calls=%async_computation.5 | async-start | bytes 1310720 | tf_op jit(solution)/shard_map/all_to_all | solution.py:15
  132.6 20.8 %all-to-all-done.5 = bf16[128,2,1280]{2,1,0:T(2,128)(2,1)S(1)} async-done(((bf16[128,2,1280]{2,1,0:T(2,128)(2,1)}), bf16[128,2,1280]{2,1,0:T(2,128)(2,1)S(1)}, u32[]{:S(2)}, u32[]{:S(2)}) %all-to-all-start.5) | async-done | bytes 655392 | tf_op jit(solution)/shard_map/all_to_all | solution.py:15
  154.2 4.9 %all-to-all-start.6 = ((bf16[32,8,1152]{2,1,0:T(8,128)(2,1)}), bf16[32,8,1152]{2,1,0:T(8,128)(2,1)S(1)}, u32[]{:S(2)}, u32[]{:S(2)}) async-start(bf16[32,8,1152]{2,1,0:T(8,128)(2,1)} %broadcast_in_dim.60), calls=%async_computation.6 | async-start | bytes 1179648 | tf_op jit(solution)/shard_map/all_to_all | solution.py:15
  161.1 17.2 %all-to-all-done.6 = bf16[32,8,1152]{2,1,0:T(8,128)(2,1)S(1)} async-done(((bf16[32,8,1152]{2,1,0:T(8,128)(2,1)}), bf16[32,8,1152]{2,1,0:T(8,128)(2,1)S(1)}, u32[]{:S(2)}, u32[]{:S(2)}) %all-to-all-start.6) | async-done | bytes 589856 | tf_op jit(solution)/shard_map/all_to_all | solution.py:15
  (105 shorter events, 16.4 us)
Async XLA Ops:
  0.6 13.4 %copy-start.10 = (bf16[2,256,288]{1,2,0:T(8,128)(2,1)S(1)}, bf16[2,256,288]{1,2,0:T(8,128)(2,1)}, u32[]{:S(2)}) copy-start(bf16[2,256,288]{1,2,0:T(8,128)(2,1)} %param.13) | copy-start | bytes 884740
  2.7 18.8 %all-to-all-start = ((bf16[4,2,4,1152]{3,2,1,0:T(4,128)(2,1)}), bf16[4,2,4,1152]{3,2,1,0:T(4,128)(2,1)S(1)}, u32[]{:S(2)}, u32[]{:S(2)}) async-start(bf16[4,2,4,1152]{3,2,1,0:T(4,128)(2,1)} %broadcast_in_dim.51), calls=%async_computation | async-start | bytes 147456 | tf_op jit(solution)/shard_map/all_to_all | solution.py:15
  14.9 30.5 %copy-start.14 = (s32[2]{0:T(128)S(1)}, s32[2]{0:T(128)}, u32[]{:S(2)}) copy-start(s32[2]{0:T(128)} %param.14) | copy-start | bytes 28
  14.9 33.7 %copy-start.15 = (s32[2]{0:T(128)S(1)}, s32[2]{0:T(128)}, u32[]{:S(2)}) copy-start(s32[2]{0:T(128)} %param.23) | copy-start | bytes 28
  14.9 33.7 %copy-start.12 = (f32[1152]{0:T(1024)S(1)}, f32[1152]{0:T(1024)}, u32[]{:S(2)}) copy-start(f32[1152]{0:T(1024)} %param.15) | copy-start | bytes 13828
  21.5 28.0 %copy-start.11 = (bf16[2,1152]{1,0:T(2,128)(2,1)S(1)}, bf16[2,1152]{1,0:T(2,128)(2,1)}, u32[]{:S(2)}) copy-start(bf16[2,1152]{1,0:T(2,128)(2,1)} %param.22) | copy-start | bytes 13828
  41.8 7.8 %copy-start = (bf16[3,1152,288]{1,2,0:T(8,128)(2,1)S(1)}, bf16[3,1152,288]{1,2,0:T(8,128)(2,1)}, u32[]{:S(2)}) copy-start(bf16[3,1152,288]{1,2,0:T(8,128)(2,1)} %param.16) | copy-start | bytes 5971972
  41.8 20.4 %all-to-all-start.1 = ((bf16[4,288,256]{2,1,0:T(8,128)(2,1)}), bf16[4,288,256]{2,1,0:T(8,128)(2,1)S(1)}, u32[]{:S(2)}, u32[]{:S(2)}) async-start(bf16[4,288,256]{2,1,0:T(8,128)(2,1)} %get-tuple-element.24), calls=%async_computation.1 | async-start | bytes 1179648 | tf_op jit(solution)/shard_map/all_to_all | solution.py:175
  49.6 1.1 copy-start.6
  56.3 12.8 %collective-permute-start.2 = (bf16[64,1152]{1,0:T(8,128)(2,1)}, bf16[64,1152]{1,0:T(8,128)(2,1)S(1)}, u32[]{:S(2)}, u32[]{:S(2)}) collective-permute-start(bf16[64,1152]{1,0:T(8,128)(2,1)} %get-tuple-element.23), channel_id=1, source_target_pairs={{0,3},{1,0},{2,1},{3,2},{4,7},{5,4},{6,5},{7,6},{8,11},{9,8},{10,9... | collective-permute-start | bytes 442376 | tf_op jit(solution)/shard_map/ppermute | solution.py:21
  63.4 3.7 %copy-start.4 = (bf16[256,1152]{1,0:T(8,128)(2,1)S(1)}, bf16[256,1152]{1,0:T(8,128)(2,1)}, u32[]{:S(2)}) copy-start(bf16[256,1152]{1,0:T(8,128)(2,1)} %copy-done.3) | copy-start | bytes 1769476
  67.0 2.1 %copy-start.1 = (bf16[256,1152]{1,0:T(8,128)(2,1)}, bf16[256,1152]{1,0:T(8,128)(2,1)S(1)}, u32[]{:S(2)}) copy-start(bf16[256,1152]{1,0:T(8,128)(2,1)S(1)} %attend.2) | copy-start | bytes 1769476
  67.2 10.1 %collective-permute-start = (bf16[64,1152]{1,0:T(8,128)(2,1)S(1)}, bf16[64,1152]{1,0:T(8,128)(2,1)S(1)}, u32[]{:S(2)}, u32[]{:S(2)}) collective-permute-start(bf16[64,1152]{1,0:T(8,128)(2,1)S(1)} %get-tuple-element.22), channel_id=1, source_target_pairs={{0,1},{1,2},{2,3},{3,0},{4,5},{5,6},{6,7},{7,4},{8,9},{9,10},{10,1... | collective-permute-start | bytes 442376 | tf_op jit(solution)/shard_map/ppermute | solution.py:21
  69.2 15.0 %collective-permute-start.3 = (bf16[128,1152]{1,0:T(8,128)(2,1)S(1)}, bf16[128,1152]{1,0:T(8,128)(2,1)S(1)}, u32[]{:S(2)}, u32[]{:S(2)}) collective-permute-start(bf16[128,1152]{1,0:T(8,128)(2,1)S(1)} %pad_maximum_fusion.3), channel_id=1, source_target_pairs={{0,3},{1,0},{2,1},{3,2},{4,7},{5,4},{6,5},{7,6},{8,11},{9,8},{10,9... | collective-permute-start | bytes 884744 | tf_op jit(solution)/shard_map/ppermute | solution.py:21
  77.3 11.0 %copy-start.2 = (bf16[256,1152]{1,0:T(8,128)(2,1)S(1)}, bf16[256,1152]{1,0:T(8,128)(2,1)}, u32[]{:S(2)}) copy-start(bf16[256,1152]{1,0:T(8,128)(2,1)} %copy-done.1) | copy-start | bytes 1769476
  77.3 11.0 %collective-permute-start.1 = (bf16[128,1152]{1,0:T(8,128)(2,1)S(1)}, bf16[128,1152]{1,0:T(8,128)(2,1)S(1)}, u32[]{:S(2)}, u32[]{:S(2)}) collective-permute-start(bf16[128,1152]{1,0:T(8,128)(2,1)S(1)} %pad_maximum_fusion.2), channel_id=1, source_target_pairs={{0,1},{1,2},{2,3},{3,0},{4,5},{5,6},{6,7},{7,4},{8,9},{9,10},{10,1... | collective-permute-start | bytes 884744 | tf_op jit(solution)/shard_map/ppermute | solution.py:21
  79.8 9.0 %copy-start.13 = (f32[1152]{0:T(1024)S(1)}, f32[1152]{0:T(1024)}, u32[]{:S(2)}) copy-start(f32[1152]{0:T(1024)} %param.18) | copy-start | bytes 13828
  79.9 9.4 %copy-start.17 = (pred[128]{0:T(512)(128)(4,1)S(1)}, pred[128]{0:T(512)(128)(4,1)}, u32[]{:S(2)}) copy-start(pred[128]{0:T(512)(128)(4,1)} %add_compare_fusion) | copy-start | bytes 388
  88.6 14.4 %copy-start.5 = (bf16[2,1152,288]{1,2,0:T(8,128)(2,1)S(1)}, bf16[2,1152,288]{1,2,0:T(8,128)(2,1)}, u32[]{:S(2)}) copy-start(bf16[2,1152,288]{1,2,0:T(8,128)(2,1)} %param.19) | copy-start | bytes 3981316
  88.6 14.4 %copy-start.9 = (bf16[288,1152]{1,0:T(8,128)(2,1)S(1)}, bf16[288,1152]{1,0:T(8,128)(2,1)}, u32[]{:S(2)}) copy-start(bf16[288,1152]{1,0:T(8,128)(2,1)} %out_w_ref.5) | copy-start | bytes 1990660
  90.6 12.3 %all-to-all-start.3 = ((f32[4,4,1280]{2,1,0:T(4,128)}), f32[4,4,1280]{2,1,0:T(4,128)S(1)}, u32[]{:S(2)}, u32[]{:S(2)}) async-start(f32[4,4,1280]{2,1,0:T(4,128)} %reshape.154), calls=%async_computation.3 | async-start | bytes 163840 | tf_op jit(solution)/shard_map/all_to_all | solution.py:228
  104.4 14.1 %all-to-all-start.4 = ((f32[16,2,1152]{2,1,0:T(2,128)}), f32[16,2,1152]{2,1,0:T(2,128)S(1)}, u32[]{:S(2)}, u32[]{:S(2)}) async-start(f32[16,2,1152]{2,1,0:T(2,128)} %broadcast_in_dim.58), calls=%async_computation.4 | async-start | bytes 294912 | tf_op jit(solution)/shard_map/all_to_all | solution.py:15
  119.7 33.7 %all-to-all-start.5 = ((bf16[128,2,1280]{2,1,0:T(2,128)(2,1)}), bf16[128,2,1280]{2,1,0:T(2,128)(2,1)S(1)}, u32[]{:S(2)}, u32[]{:S(2)}) async-start(bf16[128,2,1280]{2,1,0:T(2,128)(2,1)} %broadcast_in_dim.59), calls=%async_computation.5 | async-start | bytes 1310720 | tf_op jit(solution)/shard_map/all_to_all | solution.py:15
  154.2 24.1 %all-to-all-start.6 = ((bf16[32,8,1152]{2,1,0:T(8,128)(2,1)}), bf16[32,8,1152]{2,1,0:T(8,128)(2,1)S(1)}, u32[]{:S(2)}, u32[]{:S(2)}) async-start(bf16[32,8,1152]{2,1,0:T(8,128)(2,1)} %broadcast_in_dim.60), calls=%async_computation.6 | async-start | bytes 1179648 | tf_op jit(solution)/shard_map/all_to_all | solution.py:15
  (4 other events, 3.7 us)

commit v3 on v2

--- a/solution.py
+++ b/solution.py
@@ -44,16 +44,25 @@
 NT = (((1,), (1,)), ((), ()))
 
 
-def attend_kernel(count_ref, x_ref, w_ref, out_w_ref, gain_ref, o_ref, ctx_ref):
+def attend_kernel(scalar_ref, own_ref, left_ref, right_ref, far_a_ref, far_b_ref, w_ref, out_w_ref, gain_ref,
+                  o_ref, x_ref, norm_ref, ctx_ref):
     f32, bf16 = jnp.float32, jnp.bfloat16
-    shards, dlocal, pmax = x_ref.shape
-    width = shards * dlocal
-    count = count_ref[0]
-    floats = x_ref[...].reshape(width, pmax).astype(f32)
-    center = floats - jnp.sum(floats, axis=0, keepdims=True) * (1.0 / width)
-    spread = jnp.sum(center * center, axis=0, keepdims=True) * (1.0 / width)
-    normed = (center * lax.rsqrt(spread + 1e-06) * gain_ref[...]).astype(bf16)
-    proj = matmul(w_ref[...], normed)
+    width, pmax = x_ref.shape
+    dlocal = out_w_ref.shape[0]
+    shards = width // dlocal
+    me, image, count = scalar_ref[0], scalar_ref[1], scalar_ref[2]
+    far = jnp.where(image == 0, far_a_ref[...].astype(f32), far_b_ref[...].astype(f32))
+    slices = [ref[...].astype(f32) for ref in (own_ref, left_ref, right_ref)] + [far]
+    mean = sum(jnp.sum(part, axis=0, keepdims=True) for part in slices) * (1.0 / width)
+    centers = [part - mean for part in slices]
+    spread = sum(jnp.sum(part * part, axis=0, keepdims=True) for part in centers) * (1.0 / width)
+    scale = lax.rsqrt(spread + 1e-06)
+    for part, center, steps in zip(slices, centers, (0, shards - 1, 1, 2)):
+        source = lax.rem(me + steps, shards)
+        place = pl.ds(pl.multiple_of(source * dlocal, 16), dlocal)
+        x_ref[place] = part.astype(bf16)
+        norm_ref[place] = (center * scale * gain_ref[place]).astype(bf16)
+    proj = matmul(w_ref[...], norm_ref[...])
     live = lax.broadcasted_iota(jnp.int32, (pmax, pmax), 0) < count
     for h in range(dlocal // HDIM):
         q, k, v = (proj[c * dlocal + h * HDIM : c * dlocal + (h + 1) * HDIM] for c in range(3))
@@ -66,22 +75,33 @@
     o_ref[...] = matmul(context, out_w_ref[...]).astype(bf16)
 
 
-def attend(count, slices, w_rows, w_out, gain):
-    shards, dlocal, pmax = slices.shape
-    width = w_rows.shape[1]
+def attend(scalars, slices, w_rows, w_out, gain):
+    pmax = slices[0].shape[1]
+    dlocal, width = w_out.shape
     flops = 2 * pmax * (3 * dlocal * width + 2 * dlocal * pmax + dlocal * width)
+    of_image = pl.BlockSpec((dlocal, pmax), lambda i, scalar_ref: (scalar_ref[1], 0))
+    whole = lambda *shape: pl.BlockSpec(shape, lambda i, scalar_ref: (0, 0))
     return pl.pallas_call(
         attend_kernel,
-        in_specs=[pl.BlockSpec(memory_space=pltpu.SMEM)] + [pl.BlockSpec(memory_space=pltpu.VMEM)] * 4,
-        out_specs=pl.BlockSpec(memory_space=pltpu.VMEM),
-        out_shape=jax.ShapeDtypeStruct((pmax, width), jnp.bfloat16),
-        scratch_shapes=[pltpu.VMEM((dlocal, pmax), jnp.float32)],
-        compiler_params=pltpu.CompilerParams(vmem_limit_bytes=40 * 1024 * 1024),
+        grid_spec=pltpu.PrefetchScalarGridSpec(
+            num_scalar_prefetch=1,
+            grid=(1,),
+            in_specs=[of_image] * 3
+            + [whole(dlocal, pmax)] * 2
+            + [whole(3 * dlocal, width), whole(dlocal, width), whole(width, 1)],
+            out_specs=[whole(pmax, width), whole(width, pmax)],
+            scratch_shapes=[pltpu.VMEM((width, pmax), jnp.bfloat16), pltpu.VMEM((dlocal, pmax), jnp.float32)],
+        ),
+        out_shape=[
+            jax.ShapeDtypeStruct((pmax, width), jnp.bfloat16),
+            jax.ShapeDtypeStruct((width, pmax), jnp.bfloat16),
+        ],
+        compiler_params=pltpu.CompilerParams(vmem_limit_bytes=32 * 1024 * 1024),
         cost_estimate=pl.CostEstimate(
-            flops=flops, bytes_accessed=8 * width * dlocal + 4 * pmax * width, transcendentals=0
+            flops=flops, bytes_accessed=8 * width * dlocal + 8 * pmax * width, transcendentals=0
         ),
         name="attend",
-    )(count.reshape(1), slices, w_rows, w_out, gain)
+    )(jnp.stack(scalars).astype(jnp.int32), *slices, w_rows, w_out, gain)
 
 
 def pool_kernel(halves_ref, val_ref, out_w_ref, o_ref):
@@ -130,7 +150,7 @@
         ],
         out_specs=pl.BlockSpec((images, width), lambda i: (0, 0)),
         out_shape=jax.ShapeDtypeStruct((images, width), jnp.float32),
-        compiler_params=pltpu.CompilerParams(vmem_limit_bytes=24 * 1024 * 1024),
+        compiler_params=pltpu.CompilerParams(vmem_limit_bytes=12 * 1024 * 1024),
         name="pool_embed",
     )(halves, pool_kv_rows, pool_out)
 
@@ -157,7 +177,6 @@
     heads = width // HDIM
     shards = lax.axis_size("mp")
     me = lax.axis_index("mp")
-    rank = lax.axis_index(("plane", "near"))
     half = pmax // 2
     nt = (((1,), (1,)), ((), ()))
 
@@ -169,49 +188,42 @@
         product = dot(jnp.concatenate(split_bf16(left, 3), axis=0), right, dims)
         return product[:rows] + product[rows : 2 * rows] + product[2 * rows :]
 
-    my_image, my_half = me // 2, me % 2
-    tall = patches.transpose(0, 2, 1)
-    x_other = lax.all_to_all(jnp.stack([tall[1 - d // 2] for d in range(shards)]), "mp", 0, 0)
-    x_mine = lax.all_to_all(jnp.stack([tall[d // 2] for d in range(shards)]), "mp", 0, 0)
-
-    texts_pairs = jnp.concatenate(
-        [text_emb, jnp.broadcast_to(image_pair.astype(bf16)[:, None], (rows_img, 128))], axis=1
-    )
-    texts_pairs, x_other = lax.optimization_barrier((texts_pairs, x_other))
-    texts_pairs = spread_all(texts_pairs, ("plane", "near")).reshape(-1, width + 128)
-    text_all, pair_all = texts_pairs[:, :width], texts_pairs[:, width].astype(jnp.int32)
-    texts = text_all.astype(f32)
-    inv_txt = lax.rsqrt(jnp.sum(texts * texts, axis=-1) + 1e-06)
-
     head_of = jnp.arange(dlocal, dtype=jnp.int32) // HDIM
     own_head = head_of[None, :] == jnp.arange(local_heads, dtype=jnp.int32)[:, None]
     probe = jnp.where(own_head, pool_query[None, :], 0).astype(bf16)
     probe_keys = dot(probe, pool_kv[0], nt) * (1.0 / math.sqrt(HDIM))
-    probe_all = spread_all(jnp.stack(split_bf16(probe_keys, 2)), "mp")
-    probe_all = probe_all.transpose(1, 0, 2, 3).reshape(2 * heads, width)
-
+    probe_keys = jnp.concatenate(split_bf16(probe_keys, 2), axis=0).reshape(-1, pmax)
+    probe_rows = probe_keys.shape[0]
+    padding = jnp.zeros((-probe_rows % 16, pmax), bf16)
+
+    own_x = jnp.concatenate([patches[0].T, patches[1].T, probe_keys, padding], axis=0)
+    left_x, right_x = shift(own_x, 1), shift(own_x, -1)
+
+    slot, side = me % 2, me // 2
+    texts = spread_all(jnp.where(slot == 0, text_emb[0], text_emb[1])[None], "plane").reshape(-1, width)
+    texts, left_x, right_x = lax.optimization_barrier((texts, left_x, right_x))
+    far_a, far_b = shift(left_x[:dlocal], 1), shift(right_x[dlocal:], -1)
+    came = [own_x[2 * dlocal :], right_x[2 * dlocal :], far_b[dlocal:], left_x[2 * dlocal :]]
+    came = [x[:probe_rows] for x in came]
+    probe_all = jnp.stack([lax.select_n((j - me) % shards, *came) for j in range(shards)])
+    probe_all = probe_all.reshape(shards, 2, local_heads, width).transpose(1, 0, 2, 3).reshape(2 * heads, width)
+
+    my_image, my_half = me // 2, me % 2
     w_rows = w_qkv.transpose(0, 2, 1).reshape(3 * dlocal, width)
     gain = ln1_gain[:, None]
     my_count = jnp.where(my_image == 0, patch_count[0], patch_count[1])
     other_count = jnp.where(my_image == 0, patch_count[1], patch_count[0])
-    first = attend(other_count, x_other, w_rows, w_out, gain)
-    second = attend(my_count, x_mine, w_rows, w_out, gain)
-
-    quarter = half // 2
-    far = lax.dynamic_slice(first, (my_half * half, 0), (half, width))
-    far_after, far_before = shift(far[:quarter], 1), shift(far[quarter:], -1)
+    slices = (own_x, left_x, right_x, far_a, far_b)
+    first, _ = attend((me, 1 - my_image, other_count), slices, w_rows, w_out, gain)
+    second, mine = attend((me, my_image, my_count), slices, w_rows, w_out, gain)
+
     even = my_half == 0
+    far = shift(jnp.where(even, first[:half], first[half:]), 1)
     after = jnp.where(even, second[half:], first[:half])
     before = jnp.where(even, first[half:], second[:half])
     own_part = jnp.where(even, second[:half], second[half:]).astype(f32)
-
-    def added(left, right):
-        return (left.astype(f32) + right.astype(f32)).astype(bf16)
-
-    after = jnp.concatenate([added(after[:quarter], far_after), after[quarter:]], axis=0)
-    before = jnp.concatenate([before[:quarter], added(before[quarter:], far_before)], axis=0)
+    after = (after.astype(f32) + far.astype(f32)).astype(bf16)
     parts = own_part + shift(after, 1).astype(f32) + shift(before, -1).astype(f32)
-    mine = x_mine.reshape(width, pmax)
     resid = jnp.where(my_half == 0, mine[:, :half], mine[:, half:]).T
     stream = (resid.astype(f32) + parts).astype(bf16)
     normed2 = layer_norm(stream, ln2_gain).astype(bf16)
@@ -228,40 +240,48 @@
     halves = lax.all_to_all(send, "mp", 0, 0).reshape(shards * local_heads, width + 128)
     shares = pool_embed(halves, pool_kv.transpose(0, 2, 1), pool_out)
 
-    shares = spread_all(shares, ("near", "mp"))
-    embeds = jnp.sum(shares.reshape(-1, shards, rows_img, width), axis=1).reshape(-1, width)
+
+    pairs = jnp.broadcast_to(image_pair.astype(f32)[:, None], (rows_img, 128))
+    column = spread_all(jnp.concatenate([shares, pairs], axis=1), ("near", "mp"))
+    column = column.reshape(-1, shards, rows_img, width + 128)
+    embeds = jnp.sum(column[..., :width], axis=1)
     inv_img = lax.rsqrt(jnp.sum(embeds * embeds, axis=-1, keepdims=True) + 1e-06)
-    zimg_near = embeds * inv_img
-    start = lax.axis_index("near") * rows_img
-    zimg_own = lax.dynamic_slice(zimg_near, (start, 0), (rows_img, width))
-    inv_img_own = lax.dynamic_slice(inv_img, (start, 0), (rows_img, 1))
-    zimg = spread_all(zimg_near.astype(bf16), "plane").reshape(-1, width)
+    zimg = embeds * inv_img
 
     scale = jnp.exp(logit_scale)
-    own_ids = rank * rows_img + jnp.arange(rows_img, dtype=jnp.int32)
-    every = jnp.arange(zimg.shape[0], dtype=jnp.int32)
+    planes, nears = texts.shape[0], embeds.shape[0]
+    near = lax.axis_index("near")
+    z_part = jnp.where(side == 0, zimg[:, 0], zimg[:, 1])
+    pair_part = jnp.where(side == 0, column[:, 0, 0, width], column[:, 0, 1, width])
+    text_ids = (jnp.arange(planes, dtype=jnp.int32) * nears + near) * rows_img + slot
+    texts_f32 = texts.astype(f32)
+    inv_txt = lax.rsqrt(jnp.sum(texts_f32 * texts_f32, axis=-1) + 1e-06)
+    logits = scale * dot_exact(z_part, texts, nt) * inv_txt[None, :] + logit_bias
+    is_pair = pair_part.astype(jnp.int32)[:, None] == text_ids[None, :]
+    label = jnp.where(is_pair, 1.0, -1.0).astype(f32)
+    dlog = -label * jax.nn.sigmoid(-label * logits) * scale
+    gimg = dot_exact(dlog * inv_txt[None, :], texts)
+    gtxt = sum(dlog[n][:, None] * z_part[n][None, :] for n in range(nears))
+
+    gtxt = jnp.sum(lax.all_to_all(gtxt, "plane", 0, 0, tiled=True), axis=0)
+    both = jnp.stack([gimg, jnp.broadcast_to(gtxt[None], gimg.shape)], axis=1)
+    both = jnp.broadcast_to(both[:, None], (nears, shards, 2, width)).reshape(-1, 2, width)
+    both = lax.all_to_all(both, ("near", "mp"), 0, 0).reshape(nears, rows_img, 2, 2, width)
+    gimg = jnp.sum(both[:, :, :, 0], axis=(0, 2))
+    gtxt = jnp.sum(lax.dynamic_index_in_dim(both, near, 0, False)[:, :, 1], axis=0)
+
+    zimg_own = lax.dynamic_index_in_dim(zimg, near, 0, False)
+    inv_img_own = lax.dynamic_index_in_dim(inv_img, near, 0, False)
     text_own = text_emb.astype(f32)
     inv_txt_own = lax.rsqrt(jnp.sum(text_own * text_own, axis=-1, keepdims=True) + 1e-06)
     ztxt_own = text_own * inv_txt_own
-
-    def slope(logits, is_pair):
-        label = jnp.where(is_pair, 1.0, -1.0).astype(f32)
-        return -label * jax.nn.sigmoid(-label * logits)
-
-    logits_img = scale * dot_exact(zimg_own, text_all, nt) * inv_txt[None, :] + logit_bias
-    dlog_img = slope(logits_img, image_pair[:, None] == every[None, :])
-    logits_txt = scale * dot(text_emb, zimg, nt) * inv_txt_own + logit_bias
-    dlog_txt = slope(logits_txt, pair_all[None, :] == own_ids[:, None])
-    gimg = scale * dot_exact(dlog_img * inv_txt[None, :], text_all)
-    gtxt = scale * dot_exact(dlog_txt, zimg)
     image_grad = (gimg - zimg_own * jnp.sum(zimg_own * gimg, axis=-1, keepdims=True)) * inv_img_own
     text_grad = (gtxt - ztxt_own * jnp.sum(ztxt_own * gtxt, axis=-1, keepdims=True)) * inv_txt_own
     return (image_grad, text_grad)
 
 
 def solution(mesh):
-    shards = mesh.shape["mp"]
-    devices = mesh.devices.reshape(-1, 4, shards)
+    devices = mesh.devices.reshape(-1, 4, mesh.shape["mp"])
     fine = jax.sharding.Mesh(devices, ("plane", "near", "mp"))
     dp = ("plane", "near")
     placed = (

time: 181 us -> 168 us (0.928)
  the two profiles are of different devices: /device:TPU:8 before, /device:TPU:1 now
where the time goes in v3:
time: 168 us; the launch traced here: 167 us
  waiting for transfers between devices  56.7 us (34%)
  starting transfers between devices  52.9 us (31%)
  blocking collectives  18.4 us (11%)
  local copies, waits for them, and re-layouts  13.2 us (8%)
  Pallas kernels  11.2 us (7%)
  other arithmetic  7.06 us (4%)
  between operations  5.1 us (3%)
  matrix products  2 us (1%)
    ppermute x7, starting transfers between devices, shift(): return lax.ppermute(value, 'mp', pairs)  29.1 us
    ppermute x7, waiting for transfers between devices, shift(): return lax.ppermute(value, 'mp', pairs)  22.6 us
    all_to_all x1, blocking collectives, spread_all(): lax.all_to_all(jnp.broadcast_to(value[None], (count,) + value.shape), axi...  18.4 us
    pallas_call x2, Pallas kernels, attend(): pl.pallas_call(attend_kernel, grid_spec=pltpu.PrefetchScalarGridSpec(num_...  10.6 us
    all_to_all x1, waiting for transfers between devices, per_device(): gtxt = jnp.sum(lax.all_to_all(gtxt, 'plane', 0, 0, tiled=True), axis=0)  9.95 us
    all_to_all x1, waiting for transfers between devices, spread_all(): lax.all_to_all(jnp.broadcast_to(value[None], (count,) + value.shape), axi...  9.4 us
    all_to_all x1, waiting for transfers between devices, per_device(): lax.all_to_all(both, ('near', 'mp'), 0, 0)  9.26 us
    all_to_all x1, starting transfers between devices, spread_all(): lax.all_to_all(jnp.broadcast_to(value[None], (count,) + value.shape), axi...  8.97 us
  transfers between devices with their start and end apart: 11, of which 7 were waited for; matrix products, arithmetic and copies ran while one was open for 5% of the time, Pallas kernels for 0%

profile of v3, /device:TPU:1, one launch (start us, length us, event | category | flops | bytes accessed | tf_op | source)
XLA Modules:
  0.0 166.6 jit_solution(9697728347892445785)
XLA Ops:
  0.7 1.3 subtract_convert_fusion.1
  3.3 6.8 %collective-permute-start = (bf16[624,256]{1,0:T(8,128)(2,1)S(1)}, bf16[624,256]{1,0:T(8,128)(2,1)S(1)}, u32[]{:S(2)}, u32[]{:S(2)}) collective-permute-start(bf16[624,256]{1,0:T(8,128)(2,1)S(1)} %maximum_maximum_fusion.own_ref), channel_id=1, source_target_pairs={{0,1},{1,2},{2,3},{3,0},{4,5},{5,6},{6,7},{7,4},{8,9},{9,10},{10,1... | collective-permute-start | bytes 958472 | tf_op jit(solution)/shard_map/ppermute | solution.py:21
  10.1 6.8 %collective-permute-start.1 = (bf16[624,256]{1,0:T(8,128)(2,1)S(1)}, bf16[624,256]{1,0:T(8,128)(2,1)S(1)}, u32[]{:S(2)}, u32[]{:S(2)}) collective-permute-start(bf16[624,256]{1,0:T(8,128)(2,1)S(1)} %maximum_maximum_fusion.own_ref), channel_id=1, source_target_pairs={{0,3},{1,0},{2,1},{3,2},{4,7},{5,4},{6,5},{7,6},{8,11},{9,8},{10,9... | collective-permute-start | bytes 958472 | tf_op jit(solution)/shard_map/ppermute | solution.py:21
  18.8 18.4 %all_to_all.26 = bf16[32,2,576]{2,1,0:T(2,128)(2,1)S(1)} all-to-all(bf16[32,2,576]{2,1,0:T(2,128)(2,1)S(1)} %reshape.408), channel_id=1, replica_groups=mesh['plane'=32,'near'=4,'mp'=4] {'plane'}, dimensions={0} | all-to-all | bytes 147456 | tf_op jit(solution)/shard_map/all_to_all | solution.py:15
  38.7 4.3 %collective-permute-start.2 = (bf16[336,256]{1,0:T(8,128)(2,1)}, bf16[336,256]{1,0:T(8,128)(2,1)}, u32[]{:S(2)}, u32[]{:S(2)}) collective-permute-start(bf16[336,256]{1,0:T(8,128)(2,1)} %slice.159), channel_id=1, source_target_pairs={{0,3},{1,0},{2,1},{3,2},{4,7},{5,4},{6,5},{7,6},{8,11},{9,8},{10,9... | collective-permute-start | bytes 516104 | tf_op jit(solution)/shard_map/ppermute | solution.py:21
  43.7 1.9 %collective-permute-start.3 = (bf16[288,256]{1,0:T(8,128)(2,1)}, bf16[288,256]{1,0:T(8,128)(2,1)}, u32[]{:S(2)}, u32[]{:S(2)}) collective-permute-start(bf16[288,256]{1,0:T(8,128)(2,1)} %slice.162), channel_id=1, source_target_pairs={{0,1},{1,2},{2,3},{3,0},{4,5},{5,6},{6,7},{7,4},{8,9},{9,10},{10,1... | collective-permute-start | bytes 442376 | tf_op jit(solution)/shard_map/ppermute | solution.py:21
  49.0 3.1 %collective-permute-done.3.far_a_ref = bf16[288,256]{1,0:T(8,128)(2,1)} collective-permute-done((bf16[288,256]{1,0:T(8,128)(2,1)}, bf16[288,256]{1,0:T(8,128)(2,1)}, u32[]{:S(2)}, u32[]{:S(2)}) %collective-permute-start.3) | collective-permute-done | bytes 147488 | tf_op jit(solution)/shard_map/ppermute | solution.py:21
  52.1 1.1 copy-done.2
  53.2 5.3 %attend.3 = (bf16[256,1152]{1,0:T(8,128)(2,1)S(1)}, bf16[1152,256]{1,0:T(8,128)(2,1)}) custom-call(s32[3]{0:T(128)S(1)} %get-tuple-element.44.scalar_ref, bf16[624,256]{1,0:T(8,128)(2,1)S(1)} %maximum_maximum_fusion.own_ref, bf16[624,256]{1,0:T(8,128)(2,1)S(1)} %collective-permute-done.left_ref, bf16[624,256]{1,0:T(8,128)(2,1)S(1)} %collective-permute-done.1.right_ref, ...), custom_call_target="tpu_custom_call" | custom-call | flops 754974720 | bytes 5013504 | tf_op jit(solution)/shard_map/attend/pallas_call | solution.py:84
  60.4 5.3 %attend.2 = (bf16[256,1152]{1,0:T(8,128)(2,1)S(1)}, bf16[1152,256]{1,0:T(8,128)(2,1)S(1)}) custom-call(s32[3]{0:T(128)S(1)} %get-tuple-element.43.scalar_ref, bf16[624,256]{1,0:T(8,128)(2,1)S(1)} %maximum_maximum_fusion.own_ref, bf16[624,256]{1,0:T(8,128)(2,1)S(1)} %copy-done.6, bf16[624,256]{1,0:T(8,128)(2,1)S(1)} %copy-done.4, ...), custom_call_target="tpu_custom_call" | custom-call | flops 754974720 | bytes 5013504 | tf_op jit(solution)/shard_map/attend/pallas_call | solution.py:84
  65.8 1.9 %collective-permute-start.4 = (bf16[128,1152]{1,0:T(8,128)(2,1)S(1)}, bf16[128,1152]{1,0:T(8,128)(2,1)S(1)}, u32[]{:S(2)}, u32[]{:S(2)}) collective-permute-start(bf16[128,1152]{1,0:T(8,128)(2,1)S(1)} %get-tuple-element.29), channel_id=1, source_target_pairs={{0,1},{1,2},{2,3},{3,0},{4,5},{5,6},{6,7},{7,4},{8,9},{9,10},{10,1... | collective-permute-start | bytes 884744 | tf_op jit(solution)/shard_map/ppermute | solution.py:21
  67.8 5.5 %collective-permute-start.6 = (bf16[128,1152]{1,0:T(8,128)(2,1)S(1)}, bf16[128,1152]{1,0:T(8,128)(2,1)S(1)}, u32[]{:S(2)}, u32[]{:S(2)}) collective-permute-start(bf16[128,1152]{1,0:T(8,128)(2,1)S(1)} %get-tuple-element.30), channel_id=1, source_target_pairs={{0,3},{1,0},{2,1},{3,2},{4,7},{5,4},{6,5},{7,6},{8,11},{9,8},{10,9... | collective-permute-start | bytes 884744 | tf_op jit(solution)/shard_map/ppermute | solution.py:21
  74.0 8.8 %collective-permute-done.4 = bf16[128,1152]{1,0:T(8,128)(2,1)S(1)} collective-permute-done((bf16[128,1152]{1,0:T(8,128)(2,1)S(1)}, bf16[128,1152]{1,0:T(8,128)(2,1)S(1)}, u32[]{:S(2)}, u32[]{:S(2)}) %collective-permute-start.4) | collective-permute-done | bytes 294944 | tf_op jit(solution)/shard_map/ppermute | solution.py:21
  82.9 1.9 %collective-permute-start.5 = (bf16[128,1152]{1,0:T(8,128)(2,1)S(1)}, bf16[128,1152]{1,0:T(8,128)(2,1)S(1)}, u32[]{:S(2)}, u32[]{:S(2)}) collective-permute-start(bf16[128,1152]{1,0:T(8,128)(2,1)S(1)} %add_convert_fusion), channel_id=1, source_target_pairs={{0,1},{1,2},{2,3},{3,0},{4,5},{5,6},{6,7},{7,4},{8,9},{9,10},{10,1... | collective-permute-start | bytes 884744 | tf_op jit(solution)/shard_map/ppermute | solution.py:21
  86.4 1.4 copy.93
  87.8 10.7 %collective-permute-done.5 = bf16[128,1152]{1,0:T(8,128)(2,1)S(1)} collective-permute-done((bf16[128,1152]{1,0:T(8,128)(2,1)S(1)}, bf16[128,1152]{1,0:T(8,128)(2,1)S(1)}, u32[]{:S(2)}, u32[]{:S(2)}) %collective-permute-start.5) | collective-permute-done | bytes 294944 | tf_op jit(solution)/shard_map/ppermute | solution.py:21
  100.9 3.3 %all-to-all-start.1 = ((f32[4,4,1280]{2,1,0:T(4,128)}), f32[4,4,1280]{2,1,0:T(4,128)S(1)}, u32[]{:S(2)}, u32[]{:S(2)}) async-start(f32[4,4,1280]{2,1,0:T(4,128)} %reshape.397), calls=%async_computation.1 | async-start | bytes 163840 | tf_op jit(solution)/shard_map/all_to_all | solution.py:240
  105.7 5.4 %all-to-all-done.1 = f32[4,4,1280]{2,1,0:T(4,128)S(1)} async-done(((f32[4,4,1280]{2,1,0:T(4,128)}), f32[4,4,1280]{2,1,0:T(4,128)S(1)}, u32[]{:S(2)}, u32[]{:S(2)}) %all-to-all-start.1) | async-done | bytes 81952 | tf_op jit(solution)/shard_map/all_to_all | solution.py:240
  112.7 9.0 %all-to-all-start.2 = ((f32[16,2,1280]{2,1,0:T(2,128)}), f32[16,2,1280]{2,1,0:T(2,128)S(1)}, u32[]{:S(2)}, u32[]{:S(2)}) async-start(f32[16,2,1280]{2,1,0:T(2,128)} %broadcast_in_dim.55), calls=%async_computation.2 | async-start | bytes 327680 | tf_op jit(solution)/shard_map/all_to_all | solution.py:15
  121.8 9.4 %all-to-all-done.2 = f32[16,2,1280]{2,1,0:T(2,128)S(1)} async-done(((f32[16,2,1280]{2,1,0:T(2,128)}), f32[16,2,1280]{2,1,0:T(2,128)S(1)}, u32[]{:S(2)}, u32[]{:S(2)}) %all-to-all-start.2) | async-done | bytes 163872 | tf_op jit(solution)/shard_map/all_to_all | solution.py:15
  132.9 7.8 %all-to-all-start.3 = ((f32[32,1,1152]{2,1,0:T(1,128)}), f32[32,1,1152]{2,1,0:T(1,128)S(1)}, u32[]{:S(2)}, u32[]{:S(2)}) async-start(f32[32,1,1152]{2,1,0:T(1,128)} %copy.96), calls=%async_computation.3 | async-start | bytes 294912 | tf_op jit(solution)/shard_map/all_to_all | solution.py:266
  140.9 9.9 %all-to-all-done.3 = f32[32,1,1152]{2,1,0:T(1,128)S(1)} async-done(((f32[32,1,1152]{2,1,0:T(1,128)}), f32[32,1,1152]{2,1,0:T(1,128)S(1)}, u32[]{:S(2)}, u32[]{:S(2)}) %all-to-all-start.3) | async-done | bytes 147488 | tf_op jit(solution)/shard_map/all_to_all | solution.py:266
  151.7 3.8 %all-to-all-start.4 = ((f32[16,2,1152]{2,1,0:T(2,128)}), f32[16,2,1152]{2,1,0:T(2,128)S(1)}, u32[]{:S(2)}, u32[]{:S(2)}) async-start(f32[16,2,1152]{2,1,0:T(2,128)} %bitcast.28), calls=%async_computation.4 | async-start | bytes 294912 | tf_op jit(solution)/shard_map/all_to_all | solution.py:269
  155.5 9.3 %all-to-all-done.4 = f32[16,2,1152]{2,1,0:T(2,128)S(1)} async-done(((f32[16,2,1152]{2,1,0:T(2,128)}), f32[16,2,1152]{2,1,0:T(2,128)S(1)}, u32[]{:S(2)}, u32[]{:S(2)}) %all-to-all-start.4) | async-done | bytes 147488 | tf_op jit(solution)/shard_map/all_to_all | solution.py:269
  (123 shorter events, 19.2 us)
Async XLA Ops:
  0.6 16.3 %copy-start.13 = (bf16[2,1152]{1,0:T(2,128)(2,1)S(1)}, bf16[2,1152]{1,0:T(2,128)(2,1)}, u32[]{:S(2)}) copy-start(bf16[2,1152]{1,0:T(2,128)(2,1)} %param.22) | copy-start | bytes 13828
  3.1 42.5 %copy-start.16 = (s32[2]{0:T(128)S(1)}, s32[2]{0:T(128)}, u32[]{:S(2)}) copy-start(s32[2]{0:T(128)} %param.14) | copy-start | bytes 28
  3.1 45.6 %copy-start.14 = (f32[1152]{0:T(1024)S(1)}, f32[1152]{0:T(1024)}, u32[]{:S(2)}) copy-start(f32[1152]{0:T(1024)} %param.15) | copy-start | bytes 13828
  3.3 48.8 %copy-start = (bf16[3,1152,288]{1,2,0:T(8,128)(2,1)S(1)}, bf16[3,1152,288]{1,2,0:T(8,128)(2,1)}, u32[]{:S(2)}) copy-start(bf16[3,1152,288]{1,2,0:T(8,128)(2,1)} %param.16) | copy-start | bytes 5971972
  3.3 34.6 %collective-permute-start = (bf16[624,256]{1,0:T(8,128)(2,1)S(1)}, bf16[624,256]{1,0:T(8,128)(2,1)S(1)}, u32[]{:S(2)}, u32[]{:S(2)}) collective-permute-start(bf16[624,256]{1,0:T(8,128)(2,1)S(1)} %maximum_maximum_fusion.own_ref), channel_id=1, source_target_pairs={{0,1},{1,2},{2,3},{3,0},{4,5},{5,6},{6,7},{7,4},{8,9},{9,10},{10,1... | collective-permute-start | bytes 958472 | tf_op jit(solution)/shard_map/ppermute | solution.py:21
  10.1 27.8 %collective-permute-start.1 = (bf16[624,256]{1,0:T(8,128)(2,1)S(1)}, bf16[624,256]{1,0:T(8,128)(2,1)S(1)}, u32[]{:S(2)}, u32[]{:S(2)}) collective-permute-start(bf16[624,256]{1,0:T(8,128)(2,1)S(1)} %maximum_maximum_fusion.own_ref), channel_id=1, source_target_pairs={{0,3},{1,0},{2,1},{3,2},{4,7},{5,4},{6,5},{7,6},{8,11},{9,8},{10,9... | collective-permute-start | bytes 958472 | tf_op jit(solution)/shard_map/ppermute | solution.py:21
  38.0 20.5 %copy-start.5 = (bf16[624,256]{1,0:T(8,128)(2,1)}, bf16[624,256]{1,0:T(8,128)(2,1)S(1)}, u32[]{:S(2)}) copy-start(bf16[624,256]{1,0:T(8,128)(2,1)S(1)} %collective-permute-done.left_ref) | copy-start | bytes 958468
  38.0 20.5 %copy-start.3 = (bf16[624,256]{1,0:T(8,128)(2,1)}, bf16[624,256]{1,0:T(8,128)(2,1)S(1)}, u32[]{:S(2)}) copy-start(bf16[624,256]{1,0:T(8,128)(2,1)S(1)} %collective-permute-done.1.right_ref) | copy-start | bytes 958468
  38.7 13.4 %collective-permute-start.2 = (bf16[336,256]{1,0:T(8,128)(2,1)}, bf16[336,256]{1,0:T(8,128)(2,1)}, u32[]{:S(2)}, u32[]{:S(2)}) collective-permute-start(bf16[336,256]{1,0:T(8,128)(2,1)} %slice.159), channel_id=1, source_target_pairs={{0,3},{1,0},{2,1},{3,2},{4,7},{5,4},{6,5},{7,6},{8,11},{9,8},{10,9... | collective-permute-start | bytes 516104 | tf_op jit(solution)/shard_map/ppermute | solution.py:21
  43.7 8.4 %collective-permute-start.3 = (bf16[288,256]{1,0:T(8,128)(2,1)}, bf16[288,256]{1,0:T(8,128)(2,1)}, u32[]{:S(2)}, u32[]{:S(2)}) collective-permute-start(bf16[288,256]{1,0:T(8,128)(2,1)} %slice.162), channel_id=1, source_target_pairs={{0,1},{1,2},{2,3},{3,0},{4,5},{5,6},{6,7},{7,4},{8,9},{9,10},{10,1... | collective-permute-start | bytes 442376 | tf_op jit(solution)/shard_map/ppermute | solution.py:21
  65.7 17.2 %copy-start.8 = (bf16[1152,256]{1,0:T(8,128)(2,1)}, bf16[1152,256]{1,0:T(8,128)(2,1)S(1)}, u32[]{:S(2)}) copy-start(bf16[1152,256]{1,0:T(8,128)(2,1)S(1)} %get-tuple-element.10) | copy-start | bytes 1769476
  65.7 7.5 %copy-start.11 = (bf16[36,256]{1,0:T(8,128)(2,1)S(1)}, bf16[36,256]{1,0:T(8,128)(2,1)}, u32[]{:S(2)}) copy-start(bf16[36,256]{1,0:T(8,128)(2,1)} %copy-done.10) | copy-start | bytes 55300
  65.8 17.0 %collective-permute-start.4 = (bf16[128,1152]{1,0:T(8,128)(2,1)S(1)}, bf16[128,1152]{1,0:T(8,128)(2,1)S(1)}, u32[]{:S(2)}, u32[]{:S(2)}) collective-permute-start(bf16[128,1152]{1,0:T(8,128)(2,1)S(1)} %get-tuple-element.29), channel_id=1, source_target_pairs={{0,1},{1,2},{2,3},{3,0},{4,5},{5,6},{6,7},{7,4},{8,9},{9,10},{10,1... | collective-permute-start | bytes 884744 | tf_op jit(solution)/shard_map/ppermute | solution.py:21
  67.8 20.0 %collective-permute-start.6 = (bf16[128,1152]{1,0:T(8,128)(2,1)S(1)}, bf16[128,1152]{1,0:T(8,128)(2,1)S(1)}, u32[]{:S(2)}, u32[]{:S(2)}) collective-permute-start(bf16[128,1152]{1,0:T(8,128)(2,1)S(1)} %get-tuple-element.30), channel_id=1, source_target_pairs={{0,3},{1,0},{2,1},{3,2},{4,7},{5,4},{6,5},{7,6},{8,11},{9,8},{10,9... | collective-permute-start | bytes 884744 | tf_op jit(solution)/shard_map/ppermute | solution.py:21
  82.9 15.6 %collective-permute-start.5 = (bf16[128,1152]{1,0:T(8,128)(2,1)S(1)}, bf16[128,1152]{1,0:T(8,128)(2,1)S(1)}, u32[]{:S(2)}, u32[]{:S(2)}) collective-permute-start(bf16[128,1152]{1,0:T(8,128)(2,1)S(1)} %add_convert_fusion), channel_id=1, source_target_pairs={{0,1},{1,2},{2,3},{3,0},{4,5},{5,6},{6,7},{7,4},{8,9},{9,10},{10,1... | collective-permute-start | bytes 884744 | tf_op jit(solution)/shard_map/ppermute | solution.py:21
  87.8 11.4 %copy-start.15 = (f32[1152]{0:T(1024)S(1)}, f32[1152]{0:T(1024)}, u32[]{:S(2)}) copy-start(f32[1152]{0:T(1024)} %param.18) | copy-start | bytes 13828
  87.8 11.6 %copy-start.12 = (bf16[32,1152]{1,0:T(8,128)(2,1)S(1)}, bf16[32,1152]{1,0:T(8,128)(2,1)}, u32[]{:S(2)}) copy-start(bf16[32,1152]{1,0:T(8,128)(2,1)} %reshape.395) | copy-start | bytes 221188
  98.8 12.3 %copy-start.1 = (bf16[2,1152,288]{1,2,0:T(8,128)(2,1)S(1)}, bf16[2,1152,288]{1,2,0:T(8,128)(2,1)}, u32[]{:S(2)}) copy-start(bf16[2,1152,288]{1,2,0:T(8,128)(2,1)} %param.19) | copy-start | bytes 3981316
  98.9 12.3 %copy-start.7 = (bf16[288,1152]{1,0:T(8,128)(2,1)S(1)}, bf16[288,1152]{1,0:T(8,128)(2,1)}, u32[]{:S(2)}) copy-start(bf16[288,1152]{1,0:T(8,128)(2,1)} %out_w_ref.5) | copy-start | bytes 1990660
  100.9 10.2 %all-to-all-start.1 = ((f32[4,4,1280]{2,1,0:T(4,128)}), f32[4,4,1280]{2,1,0:T(4,128)S(1)}, u32[]{:S(2)}, u32[]{:S(2)}) async-start(f32[4,4,1280]{2,1,0:T(4,128)} %reshape.397), calls=%async_computation.1 | async-start | bytes 163840 | tf_op jit(solution)/shard_map/all_to_all | solution.py:240
  111.2 10.5 %copy-start.9 = (bf16[32,1,1152]{2,0,1:T(8,128)(2,1)S(1)}, bf16[32,1,1152]{2,0,1:T(8,128)(2,1)}, u32[]{:S(2)}) copy-start(bf16[32,1,1152]{2,0,1:T(8,128)(2,1)} %copy.119) | copy-start | bytes 221188
  112.7 18.5 %all-to-all-start.2 = ((f32[16,2,1280]{2,1,0:T(2,128)}), f32[16,2,1280]{2,1,0:T(2,128)S(1)}, u32[]{:S(2)}, u32[]{:S(2)}) async-start(f32[16,2,1280]{2,1,0:T(2,128)} %broadcast_in_dim.55), calls=%async_computation.2 | async-start | bytes 327680 | tf_op jit(solution)/shard_map/all_to_all | solution.py:15
  132.9 17.9 %all-to-all-start.3 = ((f32[32,1,1152]{2,1,0:T(1,128)}), f32[32,1,1152]{2,1,0:T(1,128)S(1)}, u32[]{:S(2)}, u32[]{:S(2)}) async-start(f32[32,1,1152]{2,1,0:T(1,128)} %copy.96), calls=%async_computation.3 | async-start | bytes 294912 | tf_op jit(solution)/shard_map/all_to_all | solution.py:266
  151.7 13.1 %all-to-all-start.4 = ((f32[16,2,1152]{2,1,0:T(2,128)}), f32[16,2,1152]{2,1,0:T(2,128)S(1)}, u32[]{:S(2)}, u32[]{:S(2)}) async-start(f32[16,2,1152]{2,1,0:T(2,128)} %bitcast.28), calls=%async_computation.4 | async-start | bytes 294912 | tf_op jit(solution)/shard_map/all_to_all | solution.py:269
  (5 other events, 9.5 us)

commit v4 on v3

--- a/solution.py
+++ b/solution.py
@@ -15,10 +15,10 @@
     return lax.all_to_all(jnp.broadcast_to(value[None], (count,) + value.shape), axis, 0, 0)
 
 
-def shift(value, steps):
-    count = lax.axis_size("mp")
+def shift(value, steps, axis="mp"):
+    count = lax.axis_size(axis)
     pairs = [(source, (source + steps) % count) for source in range(count)]
-    return lax.ppermute(value, "mp", pairs)
+    return lax.ppermute(value, axis, pairs)
 
 
 def layer_norm(values, gain_vec):
@@ -199,8 +199,7 @@
     own_x = jnp.concatenate([patches[0].T, patches[1].T, probe_keys, padding], axis=0)
     left_x, right_x = shift(own_x, 1), shift(own_x, -1)
 
-    slot, side = me % 2, me // 2
-    texts = spread_all(jnp.where(slot == 0, text_emb[0], text_emb[1])[None], "plane").reshape(-1, width)
+    texts = spread_all(text_emb, "plane").reshape(-1, width)
     texts, left_x, right_x = lax.optimization_barrier((texts, left_x, right_x))
     far_a, far_b = shift(left_x[:dlocal], 1), shift(right_x[dlocal:], -1)
     came = [own_x[2 * dlocal :], right_x[2 * dlocal :], far_b[dlocal:], left_x[2 * dlocal :]]
@@ -217,12 +216,19 @@
     first, _ = attend((me, 1 - my_image, other_count), slices, w_rows, w_out, gain)
     second, mine = attend((me, my_image, my_count), slices, w_rows, w_out, gain)
 
+    quarter = half // 2
     even = my_half == 0
-    far = shift(jnp.where(even, first[:half], first[half:]), 1)
+    far = jnp.where(even, first[:half], first[half:])
+    far_after, far_before = shift(far[:quarter], 1), shift(far[quarter:], -1)
     after = jnp.where(even, second[half:], first[:half])
     before = jnp.where(even, first[half:], second[:half])
     own_part = jnp.where(even, second[:half], second[half:]).astype(f32)
-    after = (after.astype(f32) + far.astype(f32)).astype(bf16)
+
+    def added(left, right):
+        return (left.astype(f32) + right.astype(f32)).astype(bf16)
+
+    after = jnp.concatenate([added(after[:quarter], far_after), after[quarter:]], axis=0)
+    before = jnp.concatenate([before[:quarter], added(before[quarter:], far_before)], axis=0)
     parts = own_part + shift(after, 1).astype(f32) + shift(before, -1).astype(f32)
     resid = jnp.where(my_half == 0, mine[:, :half], mine[:, half:]).T
     stream = (resid.astype(f32) + parts).astype(bf16)
@@ -249,26 +255,26 @@
     zimg = embeds * inv_img
 
     scale = jnp.exp(logit_scale)
-    planes, nears = texts.shape[0], embeds.shape[0]
+    planes, nears = texts.shape[0] // rows_img, embeds.shape[0]
     near = lax.axis_index("near")
-    z_part = jnp.where(side == 0, zimg[:, 0], zimg[:, 1])
-    pair_part = jnp.where(side == 0, column[:, 0, 0, width], column[:, 0, 1, width])
-    text_ids = (jnp.arange(planes, dtype=jnp.int32) * nears + near) * rows_img + slot
+    z_part = zimg.reshape(-1, width)
+    pair_part = column[:, 0, :, width].reshape(-1)
+    plane_ids = jnp.arange(planes, dtype=jnp.int32)[:, None] * nears + near
+    text_ids = (plane_ids * rows_img + jnp.arange(rows_img, dtype=jnp.int32)[None, :]).reshape(-1)
     texts_f32 = texts.astype(f32)
     inv_txt = lax.rsqrt(jnp.sum(texts_f32 * texts_f32, axis=-1) + 1e-06)
     logits = scale * dot_exact(z_part, texts, nt) * inv_txt[None, :] + logit_bias
     is_pair = pair_part.astype(jnp.int32)[:, None] == text_ids[None, :]
     label = jnp.where(is_pair, 1.0, -1.0).astype(f32)
     dlog = -label * jax.nn.sigmoid(-label * logits) * scale
-    gimg = dot_exact(dlog * inv_txt[None, :], texts)
-    gtxt = sum(dlog[n][:, None] * z_part[n][None, :] for n in range(nears))
-
-    gtxt = jnp.sum(lax.all_to_all(gtxt, "plane", 0, 0, tiled=True), axis=0)
-    both = jnp.stack([gimg, jnp.broadcast_to(gtxt[None], gimg.shape)], axis=1)
-    both = jnp.broadcast_to(both[:, None], (nears, shards, 2, width)).reshape(-1, 2, width)
-    both = lax.all_to_all(both, ("near", "mp"), 0, 0).reshape(nears, rows_img, 2, 2, width)
-    gimg = jnp.sum(both[:, :, :, 0], axis=(0, 2))
-    gtxt = jnp.sum(lax.dynamic_index_in_dim(both, near, 0, False)[:, :, 1], axis=0)
+    gimg = dot_exact(dlog * inv_txt[None, :], texts).reshape(nears, rows_img, width)
+    gtxt = jnp.dot(dlog.T, z_part, precision=lax.Precision.HIGHEST).reshape(planes, rows_img, width)
+
+    gtxt = jnp.sum(lax.all_to_all(gtxt, "plane", 0, 0), axis=0)
+    gimg_own = lax.dynamic_index_in_dim(gimg, near, 0, False)
+    for k in range(1, nears):
+        gimg_own += shift(lax.dynamic_index_in_dim(gimg, (near + k) % nears, 0, False), k, "near")
+    gimg = gimg_own
 
     zimg_own = lax.dynamic_index_in_dim(zimg, near, 0, False)
     inv_img_own = lax.dynamic_index_in_dim(inv_img, near, 0, False)

time: 168 us -> 161 us (0.958)
  starting transfers between devices: 52.9 us -> 73.8 us
  blocking collectives: 18.4 us -> 0 us
  waiting for transfers between devices: 56.7 us -> 44 us
    all_to_all x1 -> x0, blocking collectives: 18.4 us -> none  [spread_all(): lax.all_to_all(jnp.broadcast_to(value[None], (count,) + value.shape), axi...]
    ppermute x7 -> x11, starting transfers between devices: 29.1 us -> 43.1 us  [shift(): return lax.ppermute(value, axis, pairs)]
    ppermute x7 -> x11, waiting for transfers between devices: 22.6 us -> 11.4 us  [shift(): return lax.ppermute(value, axis, pairs)]
    all_to_all x1 -> x2, starting transfers between devices: 8.97 us -> 18.9 us  [spread_all(): lax.all_to_all(jnp.broadcast_to(value[None], (count,) + value.shape), axi...]
    all_to_all x2 -> x1, waiting for transfers between devices: 19.2 us -> 10.8 us  [per_device(): gtxt = jnp.sum(lax.all_to_all(gtxt, 'plane', 0, 0), axis=0)]
    all_to_all x1 -> x2, waiting for transfers between devices: 9.4 us -> 14.6 us  [spread_all(): lax.all_to_all(jnp.broadcast_to(value[None], (count,) + value.shape), axi...]
    all_to_all x2 -> x1, starting transfers between devices: 11.6 us -> 8.11 us  [per_device(): gtxt = jnp.sum(lax.all_to_all(gtxt, 'plane', 0, 0), axis=0)]
    all_to_all x1, waiting for transfers between devices: 5.45 us -> 7.18 us  [per_device(): lax.all_to_all(send, 'mp', 0, 0).reshape(shards * local_heads, width + 128)]
  transfers between devices with their start and end apart: 11 -> 15, of which waited for: 7 -> 7; matrix products, arithmetic and copies ran while one was open for 5% -> 8% of each run, Pallas kernels for 0% -> 0%
where the time goes in v4:
time: 161 us; the launch traced here: 159 us
  starting transfers between devices  73.8 us (46%)
  waiting for transfers between devices  44 us (27%)
  local copies, waits for them, and re-layouts  14.6 us (9%)
  Pallas kernels  11.2 us (7%)
  other arithmetic  8.04 us (5%)
  between operations  5.29 us (3%)
  matrix products  2.38 us (1%)
    ppermute x11, starting transfers between devices, shift(): return lax.ppermute(value, axis, pairs)  43.1 us
    all_to_all x2, starting transfers between devices, spread_all(): lax.all_to_all(jnp.broadcast_to(value[None], (count,) + value.shape), axi...  18.9 us
    all_to_all x2, waiting for transfers between devices, spread_all(): lax.all_to_all(jnp.broadcast_to(value[None], (count,) + value.shape), axi...  14.6 us
    ppermute x11, waiting for transfers between devices, shift(): return lax.ppermute(value, axis, pairs)  11.4 us
    all_to_all x1, waiting for transfers between devices, per_device(): gtxt = jnp.sum(lax.all_to_all(gtxt, 'plane', 0, 0), axis=0)  10.8 us
    pallas_call x2, Pallas kernels, attend(): pl.pallas_call(attend_kernel, grid_spec=pltpu.PrefetchScalarGridSpec(num_...  10.5 us
    all_to_all x1, starting transfers between devices, per_device(): gtxt = jnp.sum(lax.all_to_all(gtxt, 'plane', 0, 0), axis=0)  8.11 us
    all_to_all x1, waiting for transfers between devices, per_device(): lax.all_to_all(send, 'mp', 0, 0).reshape(shards * local_heads, width + 128)  7.18 us
  transfers between devices with their start and end apart: 15, of which 7 were waited for; matrix products, arithmetic and copies ran while one was open for 8% of the time, Pallas kernels for 0%

profile of v4, /device:TPU:1, one launch (start us, length us, event | category | flops | bytes accessed | tf_op | source)
XLA Modules:
  0.0 159.3 jit_solution(4663636909483608371)
XLA Ops:
  3.3 6.8 %collective-permute-start = (bf16[624,256]{1,0:T(8,128)(2,1)S(1)}, bf16[624,256]{1,0:T(8,128)(2,1)S(1)}, u32[]{:S(2)}, u32[]{:S(2)}) collective-permute-start(bf16[624,256]{1,0:T(8,128)(2,1)S(1)} %maximum_maximum_fusion.own_ref), channel_id=1, source_target_pairs={{0,1},{1,2},{2,3},{3,0},{4,5},{5,6},{6,7},{7,4},{8,9},{9,10},{10,1... | collective-permute-start | bytes 958472 | tf_op jit(solution)/shard_map/ppermute | solution.py:21
  10.1 6.8 %collective-permute-start.1 = (bf16[624,256]{1,0:T(8,128)(2,1)S(1)}, bf16[624,256]{1,0:T(8,128)(2,1)S(1)}, u32[]{:S(2)}, u32[]{:S(2)}) collective-permute-start(bf16[624,256]{1,0:T(8,128)(2,1)S(1)} %maximum_maximum_fusion.own_ref), channel_id=1, source_target_pairs={{0,3},{1,0},{2,1},{3,2},{4,7},{5,4},{6,5},{7,6},{8,11},{9,8},{10,9... | collective-permute-start | bytes 958472 | tf_op jit(solution)/shard_map/ppermute | solution.py:21
  17.6 9.7 %all-to-all-start = ((bf16[32,2,1152]{2,1,0:T(2,128)(2,1)}), bf16[32,2,1152]{2,1,0:T(2,128)(2,1)S(1)}, u32[]{:S(2)}, u32[]{:S(2)}) async-start(bf16[32,2,1152]{2,1,0:T(2,128)(2,1)} %broadcast_in_dim.45), calls=%async_computation | async-start | bytes 294912 | tf_op jit(solution)/shard_map/all_to_all | solution.py:15
  31.4 5.1 %all-to-all-done = bf16[32,2,1152]{2,1,0:T(2,128)(2,1)S(1)} async-done(((bf16[32,2,1152]{2,1,0:T(2,128)(2,1)}), bf16[32,2,1152]{2,1,0:T(2,128)(2,1)S(1)}, u32[]{:S(2)}, u32[]{:S(2)}) %all-to-all-start) | async-done | bytes 147488 | tf_op jit(solution)/shard_map/all_to_all | solution.py:15
  38.0 4.2 %collective-permute-start.2 = (bf16[336,256]{1,0:T(8,128)(2,1)}, bf16[336,256]{1,0:T(8,128)(2,1)}, u32[]{:S(2)}, u32[]{:S(2)}) collective-permute-start(bf16[336,256]{1,0:T(8,128)(2,1)} %slice.118), channel_id=1, source_target_pairs={{0,3},{1,0},{2,1},{3,2},{4,7},{5,4},{6,5},{7,6},{8,11},{9,8},{10,9... | collective-permute-start | bytes 516104 | tf_op jit(solution)/shard_map/ppermute | solution.py:21
  42.9 1.9 %collective-permute-start.3 = (bf16[288,256]{1,0:T(8,128)(2,1)}, bf16[288,256]{1,0:T(8,128)(2,1)}, u32[]{:S(2)}, u32[]{:S(2)}) collective-permute-start(bf16[288,256]{1,0:T(8,128)(2,1)} %slice.121), channel_id=1, source_target_pairs={{0,1},{1,2},{2,3},{3,0},{4,5},{5,6},{6,7},{7,4},{8,9},{9,10},{10,1... | collective-permute-start | bytes 442376 | tf_op jit(solution)/shard_map/ppermute | solution.py:21
  48.1 1.4 add.218
  52.4 5.3 %attend.3 = (bf16[256,1152]{1,0:T(8,128)(2,1)S(1)}, bf16[1152,256]{1,0:T(8,128)(2,1)}) custom-call(s32[3]{0:T(128)S(1)} %get-tuple-element.45.scalar_ref, bf16[624,256]{1,0:T(8,128)(2,1)S(1)} %maximum_maximum_fusion.own_ref, bf16[624,256]{1,0:T(8,128)(2,1)S(1)} %collective-permute-done.left_ref, bf16[624,256]{1,0:T(8,128)(2,1)S(1)} %collective-permute-done.1.right_ref, ...), custom_call_target="tpu_custom_call" | custom-call | flops 754974720 | bytes 5013504 | tf_op jit(solution)/shard_map/attend/pallas_call | solution.py:84
  59.7 5.3 %attend.2 = (bf16[256,1152]{1,0:T(8,128)(2,1)S(1)}, bf16[1152,256]{1,0:T(8,128)(2,1)S(1)}) custom-call(s32[3]{0:T(128)S(1)} %get-tuple-element.44.scalar_ref, bf16[624,256]{1,0:T(8,128)(2,1)S(1)} %maximum_maximum_fusion.own_ref, bf16[624,256]{1,0:T(8,128)(2,1)S(1)} %copy-done.6, bf16[624,256]{1,0:T(8,128)(2,1)S(1)} %copy-done.4, ...), custom_call_target="tpu_custom_call" | custom-call | flops 754974720 | bytes 5013504 | tf_op jit(solution)/shard_map/attend/pallas_call | solution.py:84
  65.7 4.3 %collective-permute-start.6 = (bf16[64,1152]{1,0:T(8,128)(2,1)S(1)}, bf16[64,1152]{1,0:T(8,128)(2,1)S(1)}, u32[]{:S(2)}, u32[]{:S(2)}) collective-permute-start(bf16[64,1152]{1,0:T(8,128)(2,1)S(1)} %get-tuple-element.31), channel_id=1, source_target_pairs={{0,3},{1,0},{2,1},{3,2},{4,7},{5,4},{6,5},{7,6},{8,11},{9,8},{10,9... | collective-permute-start | bytes 442376 | tf_op jit(solution)/shard_map/ppermute | solution.py:21
  70.1 1.9 %collective-permute-start.4 = (bf16[64,1152]{1,0:T(8,128)(2,1)S(1)}, bf16[64,1152]{1,0:T(8,128)(2,1)S(1)}, u32[]{:S(2)}, u32[]{:S(2)}) collective-permute-start(bf16[64,1152]{1,0:T(8,128)(2,1)S(1)} %get-tuple-element.30), channel_id=1, source_target_pairs={{0,1},{1,2},{2,3},{3,0},{4,5},{5,6},{6,7},{7,4},{8,9},{9,10},{10,1... | collective-permute-start | bytes 442376 | tf_op jit(solution)/shard_map/ppermute | solution.py:21
  72.9 6.9 %collective-permute-start.7 = (bf16[128,1152]{1,0:T(8,128)(2,1)S(1)}, bf16[128,1152]{1,0:T(8,128)(2,1)S(1)}, u32[]{:S(2)}, u32[]{:S(2)}) collective-permute-start(bf16[128,1152]{1,0:T(8,128)(2,1)S(1)} %pad_maximum_fusion.1), channel_id=1, source_target_pairs={{0,3},{1,0},{2,1},{3,2},{4,7},{5,4},{6,5},{7,6},{8,11},{9,8},{10,9... | collective-permute-start | bytes 884744 | tf_op jit(solution)/shard_map/ppermute | solution.py:21
  79.9 1.9 %collective-permute-start.5 = (bf16[128,1152]{1,0:T(8,128)(2,1)S(1)}, bf16[128,1152]{1,0:T(8,128)(2,1)S(1)}, u32[]{:S(2)}, u32[]{:S(2)}) collective-permute-start(bf16[128,1152]{1,0:T(8,128)(2,1)S(1)} %pad_maximum_fusion), channel_id=1, source_target_pairs={{0,1},{1,2},{2,3},{3,0},{4,5},{5,6},{6,7},{7,4},{8,9},{9,10},{10,1... | collective-permute-start | bytes 884744 | tf_op jit(solution)/shard_map/ppermute | solution.py:21
  83.7 4.1 %collective-permute-done.7 = bf16[128,1152]{1,0:T(8,128)(2,1)S(1)} collective-permute-done((bf16[128,1152]{1,0:T(8,128)(2,1)S(1)}, bf16[128,1152]{1,0:T(8,128)(2,1)S(1)}, u32[]{:S(2)}, u32[]{:S(2)}) %collective-permute-start.7) | collective-permute-done | bytes 294944 | tf_op jit(solution)/shard_map/ppermute | solution.py:21
  87.8 6.0 %collective-permute-done.5 = bf16[128,1152]{1,0:T(8,128)(2,1)S(1)} collective-permute-done((bf16[128,1152]{1,0:T(8,128)(2,1)S(1)}, bf16[128,1152]{1,0:T(8,128)(2,1)S(1)}, u32[]{:S(2)}, u32[]{:S(2)}) %collective-permute-start.5) | collective-permute-done | bytes 294944 | tf_op jit(solution)/shard_map/ppermute | solution.py:21
  96.2 3.6 %all-to-all-start.1 = ((f32[4,4,1280]{2,1,0:T(4,128)}), f32[4,4,1280]{2,1,0:T(4,128)S(1)}, u32[]{:S(2)}, u32[]{:S(2)}) async-start(f32[4,4,1280]{2,1,0:T(4,128)} %reshape.185), calls=%async_computation.1 | async-start | bytes 163840 | tf_op jit(solution)/shard_map/all_to_all | solution.py:246
  99.9 7.2 %all-to-all-done.1 = f32[4,4,1280]{2,1,0:T(4,128)S(1)} async-done(((f32[4,4,1280]{2,1,0:T(4,128)}), f32[4,4,1280]{2,1,0:T(4,128)S(1)}, u32[]{:S(2)}, u32[]{:S(2)}) %all-to-all-start.1) | async-done | bytes 81952 | tf_op jit(solution)/shard_map/all_to_all | solution.py:246
  108.6 9.3 %all-to-all-start.2 = ((f32[16,2,1280]{2,1,0:T(2,128)}), f32[16,2,1280]{2,1,0:T(2,128)S(1)}, u32[]{:S(2)}, u32[]{:S(2)}) async-start(f32[16,2,1280]{2,1,0:T(2,128)} %broadcast_in_dim.53), calls=%async_computation.2 | async-start | bytes 327680 | tf_op jit(solution)/shard_map/all_to_all | solution.py:15
  118.0 9.5 %all-to-all-done.2 = f32[16,2,1280]{2,1,0:T(2,128)S(1)} async-done(((f32[16,2,1280]{2,1,0:T(2,128)}), f32[16,2,1280]{2,1,0:T(2,128)S(1)}, u32[]{:S(2)}, u32[]{:S(2)}) %all-to-all-start.2) | async-done | bytes 163872 | tf_op jit(solution)/shard_map/all_to_all | solution.py:15
  128.7 1.9 %collective-permute-start.10 = (f32[2,1152]{1,0:T(2,128)S(1)}, f32[2,1152]{1,0:T(2,128)S(1)}, u32[]{:S(2)}, u32[]{:S(2)}) collective-permute-start(f32[2,1152]{1,0:T(2,128)S(1)} %get-tuple-element.38), channel_id=1, source_target_pairs={{0,12},{4,0},{8,4},{12,8},{1,13},{5,1},{9,5},{13,9},{2,14},{6,2},{... | collective-permute-start | bytes 27656 | tf_op jit(solution)/shard_map/ppermute | solution.py:21
  130.6 2.5 %collective-permute-start.9 = (f32[2,1152]{1,0:T(2,128)S(1)}, f32[2,1152]{1,0:T(2,128)S(1)}, u32[]{:S(2)}, u32[]{:S(2)}) collective-permute-start(f32[2,1152]{1,0:T(2,128)S(1)} %get-tuple-element.39), channel_id=1, source_target_pairs={{0,8},{4,12},{8,0},{12,4},{1,9},{5,13},{9,1},{13,5},{2,10},{6,14},... | collective-permute-start | bytes 27656 | tf_op jit(solution)/shard_map/ppermute | solution.py:21
  133.1 3.9 %collective-permute-start.8 = (f32[2,1152]{1,0:T(2,128)S(1)}, f32[2,1152]{1,0:T(2,128)S(1)}, u32[]{:S(2)}, u32[]{:S(2)}) collective-permute-start(f32[2,1152]{1,0:T(2,128)S(1)} %get-tuple-element.37), channel_id=1, source_target_pairs={{0,4},{4,8},{8,12},{12,0},{1,5},{5,9},{9,13},{13,1},{2,6},{6,10},{... | collective-permute-start | bytes 27656 | tf_op jit(solution)/shard_map/ppermute | solution.py:21
  138.5 8.1 %all-to-all-start.3 = ((f32[32,2,1152]{2,1,0:T(2,128)}), f32[32,2,1152]{2,1,0:T(2,128)S(1)}, u32[]{:S(2)}, u32[]{:S(2)}) async-start(f32[32,2,1152]{2,1,0:T(2,128)} %copy.49), calls=%async_computation.3 | async-start | bytes 589824 | tf_op jit(solution)/shard_map/all_to_all | solution.py:273
  147.5 10.8 %all-to-all-done.3 = f32[32,2,1152]{2,1,0:T(2,128)S(1)} async-done(((f32[32,2,1152]{2,1,0:T(2,128)}), f32[32,2,1152]{2,1,0:T(2,128)S(1)}, u32[]{:S(2)}, u32[]{:S(2)}) %all-to-all-start.3) | async-done | bytes 294944 | tf_op jit(solution)/shard_map/all_to_all | solution.py:273
  (137 shorter events, 25.6 us)
Async XLA Ops:
  0.6 16.3 %copy-start.14 = (bf16[2,1152]{1,0:T(2,128)(2,1)S(1)}, bf16[2,1152]{1,0:T(2,128)(2,1)}, u32[]{:S(2)}) copy-start(bf16[2,1152]{1,0:T(2,128)(2,1)} %param.22) | copy-start | bytes 13828
  0.6 26.7 %copy-start.16 = (s32[2]{0:T(128)S(1)}, s32[2]{0:T(128)}, u32[]{:S(2)}) copy-start(s32[2]{0:T(128)} %param.14) | copy-start | bytes 28
  2.1 40.8 %copy-start.11 = (bf16[36,256]{1,0:T(8,128)(2,1)}, bf16[36,256]{1,0:T(8,128)(2,1)S(1)}, u32[]{:S(2)}) copy-start(bf16[36,256]{1,0:T(8,128)(2,1)S(1)} %reshape.181) | copy-start | bytes 55300
  2.1 43.3 %copy-start.20 = (s32[2]{0:T(128)S(1)}, s32[2]{0:T(128)}, u32[]{:S(2)}) copy-start(s32[2]{0:T(128)} %param.23) | copy-start | bytes 28
  3.2 48.1 %copy-start = (bf16[3,1152,288]{1,2,0:T(8,128)(2,1)S(1)}, bf16[3,1152,288]{1,2,0:T(8,128)(2,1)}, u32[]{:S(2)}) copy-start(bf16[3,1152,288]{1,2,0:T(8,128)(2,1)} %param.16) | copy-start | bytes 5971972
  3.3 33.9 %collective-permute-start = (bf16[624,256]{1,0:T(8,128)(2,1)S(1)}, bf16[624,256]{1,0:T(8,128)(2,1)S(1)}, u32[]{:S(2)}, u32[]{:S(2)}) collective-permute-start(bf16[624,256]{1,0:T(8,128)(2,1)S(1)} %maximum_maximum_fusion.own_ref), channel_id=1, source_target_pairs={{0,1},{1,2},{2,3},{3,0},{4,5},{5,6},{6,7},{7,4},{8,9},{9,10},{10,1... | collective-permute-start | bytes 958472 | tf_op jit(solution)/shard_map/ppermute | solution.py:21
  10.1 27.1 %collective-permute-start.1 = (bf16[624,256]{1,0:T(8,128)(2,1)S(1)}, bf16[624,256]{1,0:T(8,128)(2,1)S(1)}, u32[]{:S(2)}, u32[]{:S(2)}) collective-permute-start(bf16[624,256]{1,0:T(8,128)(2,1)S(1)} %maximum_maximum_fusion.own_ref), channel_id=1, source_target_pairs={{0,3},{1,0},{2,1},{3,2},{4,7},{5,4},{6,5},{7,6},{8,11},{9,8},{10,9... | collective-permute-start | bytes 958472 | tf_op jit(solution)/shard_map/ppermute | solution.py:21
  17.6 18.9 %all-to-all-start = ((bf16[32,2,1152]{2,1,0:T(2,128)(2,1)}), bf16[32,2,1152]{2,1,0:T(2,128)(2,1)S(1)}, u32[]{:S(2)}, u32[]{:S(2)}) async-start(bf16[32,2,1152]{2,1,0:T(2,128)(2,1)} %broadcast_in_dim.45), calls=%async_computation | async-start | bytes 294912 | tf_op jit(solution)/shard_map/all_to_all | solution.py:15
  37.2 20.5 %copy-start.5 = (bf16[624,256]{1,0:T(8,128)(2,1)}, bf16[624,256]{1,0:T(8,128)(2,1)S(1)}, u32[]{:S(2)}) copy-start(bf16[624,256]{1,0:T(8,128)(2,1)S(1)} %collective-permute-done.left_ref) | copy-start | bytes 958468
  37.2 20.5 %copy-start.3 = (bf16[624,256]{1,0:T(8,128)(2,1)}, bf16[624,256]{1,0:T(8,128)(2,1)S(1)}, u32[]{:S(2)}) copy-start(bf16[624,256]{1,0:T(8,128)(2,1)S(1)} %collective-permute-done.1.right_ref) | copy-start | bytes 958468
  38.0 13.4 %collective-permute-start.2 = (bf16[336,256]{1,0:T(8,128)(2,1)}, bf16[336,256]{1,0:T(8,128)(2,1)}, u32[]{:S(2)}, u32[]{:S(2)}) collective-permute-start(bf16[336,256]{1,0:T(8,128)(2,1)} %slice.118), channel_id=1, source_target_pairs={{0,3},{1,0},{2,1},{3,2},{4,7},{5,4},{6,5},{7,6},{8,11},{9,8},{10,9... | collective-permute-start | bytes 516104 | tf_op jit(solution)/shard_map/ppermute | solution.py:21
  42.9 8.4 %collective-permute-start.3 = (bf16[288,256]{1,0:T(8,128)(2,1)}, bf16[288,256]{1,0:T(8,128)(2,1)}, u32[]{:S(2)}, u32[]{:S(2)}) collective-permute-start(bf16[288,256]{1,0:T(8,128)(2,1)} %slice.121), channel_id=1, source_target_pairs={{0,1},{1,2},{2,3},{3,0},{4,5},{5,6},{6,7},{7,4},{8,9},{9,10},{10,1... | collective-permute-start | bytes 442376 | tf_op jit(solution)/shard_map/ppermute | solution.py:21
  65.7 7.0 %collective-permute-start.6 = (bf16[64,1152]{1,0:T(8,128)(2,1)S(1)}, bf16[64,1152]{1,0:T(8,128)(2,1)S(1)}, u32[]{:S(2)}, u32[]{:S(2)}) collective-permute-start(bf16[64,1152]{1,0:T(8,128)(2,1)S(1)} %get-tuple-element.31), channel_id=1, source_target_pairs={{0,3},{1,0},{2,1},{3,2},{4,7},{5,4},{6,5},{7,6},{8,11},{9,8},{10,9... | collective-permute-start | bytes 442376 | tf_op jit(solution)/shard_map/ppermute | solution.py:21
  70.1 9.7 %collective-permute-start.4 = (bf16[64,1152]{1,0:T(8,128)(2,1)S(1)}, bf16[64,1152]{1,0:T(8,128)(2,1)S(1)}, u32[]{:S(2)}, u32[]{:S(2)}) collective-permute-start(bf16[64,1152]{1,0:T(8,128)(2,1)S(1)} %get-tuple-element.30), channel_id=1, source_target_pairs={{0,1},{1,2},{2,3},{3,0},{4,5},{5,6},{6,7},{7,4},{8,9},{9,10},{10,1... | collective-permute-start | bytes 442376 | tf_op jit(solution)/shard_map/ppermute | solution.py:21
  72.9 15.0 %collective-permute-start.7 = (bf16[128,1152]{1,0:T(8,128)(2,1)S(1)}, bf16[128,1152]{1,0:T(8,128)(2,1)S(1)}, u32[]{:S(2)}, u32[]{:S(2)}) collective-permute-start(bf16[128,1152]{1,0:T(8,128)(2,1)S(1)} %pad_maximum_fusion.1), channel_id=1, source_target_pairs={{0,3},{1,0},{2,1},{3,2},{4,7},{5,4},{6,5},{7,6},{8,11},{9,8},{10,9... | collective-permute-start | bytes 884744 | tf_op jit(solution)/shard_map/ppermute | solution.py:21
  79.9 14.0 %collective-permute-start.5 = (bf16[128,1152]{1,0:T(8,128)(2,1)S(1)}, bf16[128,1152]{1,0:T(8,128)(2,1)S(1)}, u32[]{:S(2)}, u32[]{:S(2)}) collective-permute-start(bf16[128,1152]{1,0:T(8,128)(2,1)S(1)} %pad_maximum_fusion), channel_id=1, source_target_pairs={{0,1},{1,2},{2,3},{3,0},{4,5},{5,6},{6,7},{7,4},{8,9},{9,10},{10,1... | collective-permute-start | bytes 884744 | tf_op jit(solution)/shard_map/ppermute | solution.py:21
  94.2 12.9 %copy-start.1 = (bf16[2,1152,288]{1,2,0:T(8,128)(2,1)S(1)}, bf16[2,1152,288]{1,2,0:T(8,128)(2,1)}, u32[]{:S(2)}) copy-start(bf16[2,1152,288]{1,2,0:T(8,128)(2,1)} %param.19) | copy-start | bytes 3981316
  96.2 10.8 %all-to-all-start.1 = ((f32[4,4,1280]{2,1,0:T(4,128)}), f32[4,4,1280]{2,1,0:T(4,128)S(1)}, u32[]{:S(2)}, u32[]{:S(2)}) async-start(f32[4,4,1280]{2,1,0:T(4,128)} %reshape.185), calls=%async_computation.1 | async-start | bytes 163840 | tf_op jit(solution)/shard_map/all_to_all | solution.py:246
  107.1 21.2 %copy-start.17 = (s32[64]{0:T(128)S(1)}, s32[64]{0:T(128)}, u32[]{:S(2)}) copy-start(s32[64]{0:T(128)} %add.218) | copy-start | bytes 772
  108.6 18.9 %all-to-all-start.2 = ((f32[16,2,1280]{2,1,0:T(2,128)}), f32[16,2,1280]{2,1,0:T(2,128)S(1)}, u32[]{:S(2)}, u32[]{:S(2)}) async-start(f32[16,2,1280]{2,1,0:T(2,128)} %broadcast_in_dim.53), calls=%async_computation.2 | async-start | bytes 327680 | tf_op jit(solution)/shard_map/all_to_all | solution.py:15
  128.7 18.0 %collective-permute-start.10 = (f32[2,1152]{1,0:T(2,128)S(1)}, f32[2,1152]{1,0:T(2,128)S(1)}, u32[]{:S(2)}, u32[]{:S(2)}) collective-permute-start(f32[2,1152]{1,0:T(2,128)S(1)} %get-tuple-element.38), channel_id=1, source_target_pairs={{0,12},{4,0},{8,4},{12,8},{1,13},{5,1},{9,5},{13,9},{2,14},{6,2},{... | collective-permute-start | bytes 27656 | tf_op jit(solution)/shard_map/ppermute | solution.py:21
  130.6 16.1 %collective-permute-start.9 = (f32[2,1152]{1,0:T(2,128)S(1)}, f32[2,1152]{1,0:T(2,128)S(1)}, u32[]{:S(2)}, u32[]{:S(2)}) collective-permute-start(f32[2,1152]{1,0:T(2,128)S(1)} %get-tuple-element.39), channel_id=1, source_target_pairs={{0,8},{4,12},{8,0},{12,4},{1,9},{5,13},{9,1},{13,5},{2,10},{6,14},... | collective-permute-start | bytes 27656 | tf_op jit(solution)/shard_map/ppermute | solution.py:21
  133.1 13.5 %collective-permute-start.8 = (f32[2,1152]{1,0:T(2,128)S(1)}, f32[2,1152]{1,0:T(2,128)S(1)}, u32[]{:S(2)}, u32[]{:S(2)}) collective-permute-start(f32[2,1152]{1,0:T(2,128)S(1)} %get-tuple-element.37), channel_id=1, source_target_pairs={{0,4},{4,8},{8,12},{12,0},{1,5},{5,9},{9,13},{13,1},{2,6},{6,10},{... | collective-permute-start | bytes 27656 | tf_op jit(solution)/shard_map/ppermute | solution.py:21
  138.5 19.8 %all-to-all-start.3 = ((f32[32,2,1152]{2,1,0:T(2,128)}), f32[32,2,1152]{2,1,0:T(2,128)S(1)}, u32[]{:S(2)}, u32[]{:S(2)}) async-start(f32[32,2,1152]{2,1,0:T(2,128)} %copy.49), calls=%async_computation.3 | async-start | bytes 589824 | tf_op jit(solution)/shard_map/all_to_all | solution.py:273
  (13 other events, 96.2 us)

commit v5 on v4

--- a/solution.py
+++ b/solution.py
@@ -78,7 +78,7 @@
 def attend(scalars, slices, w_rows, w_out, gain):
     pmax = slices[0].shape[1]
     dlocal, width = w_out.shape
-    flops = 2 * pmax * (3 * dlocal * width + 2 * dlocal * pmax + dlocal * width)
+    flops = 16 * pmax * (3 * dlocal * width + 2 * dlocal * pmax + dlocal * width)
     of_image = pl.BlockSpec((dlocal, pmax), lambda i, scalar_ref: (scalar_ref[1], 0))
     whole = lambda *shape: pl.BlockSpec(shape, lambda i, scalar_ref: (0, 0))
     return pl.pallas_call(
@@ -102,6 +102,50 @@
         ),
         name="attend",
     )(jnp.stack(scalars).astype(jnp.int32), *slices, w_rows, w_out, gain)
+
+
+def mix_kernel(scalar_ref, own_ref, after_ref, before_ref, x_ref, gain_ref, probe_ref, o_ref):
+    f32, bf16 = jnp.float32, jnp.bfloat16
+    half, width = own_ref.shape
+    heads = probe_ref.shape[0] // 2
+    stream = x_ref[...].astype(f32).T + (
+        own_ref[...].astype(f32) + after_ref[:half].astype(f32) + before_ref[...].astype(f32)
+    )
+    normed = layer_norm(stream.astype(bf16), gain_ref[...]).astype(bf16)
+    scores = matmul(probe_ref[...], normed, NT)
+    scores = scores[:heads] + scores[heads:]
+    row = scalar_ref[0] * half + lax.broadcasted_iota(jnp.int32, (heads, half), 1)
+    scores = jnp.where(row < scalar_ref[1], scores, -1e30)
+    highest = jnp.max(scores, axis=1, keepdims=True)
+    raised = jnp.exp(scores - highest)
+    total = jnp.sum(raised, axis=1, keepdims=True)
+    o_ref[:, :width] = matmul((raised / total).astype(bf16), normed)
+    o_ref[:, width:] = jnp.broadcast_to(highest + jnp.log(total), (heads, o_ref.shape[1] - width))
+
+
+def mix_rows(my_half, count, second, after, before, mine, gain, probe_all):
+    half, width = before.shape
+    heads = probe_all.shape[0] // 2
+    whole = lambda *shape: pl.BlockSpec(shape, lambda i, scalar_ref: (0, 0))
+    return pl.pallas_call(
+        mix_kernel,
+        grid_spec=pltpu.PrefetchScalarGridSpec(
+            num_scalar_prefetch=1,
+            grid=(1,),
+            in_specs=[
+                pl.BlockSpec((half, width), lambda i, scalar_ref: (scalar_ref[0], 0)),
+                whole(*after.shape),
+                whole(half, width),
+                pl.BlockSpec((width, half), lambda i, scalar_ref: (0, scalar_ref[0])),
+                whole(1, width),
+                whole(2 * heads, width),
+            ],
+            out_specs=whole(heads, width + 128),
+        ),
+        out_shape=jax.ShapeDtypeStruct((heads, width + 128), jnp.float32),
+        compiler_params=pltpu.CompilerParams(vmem_limit_bytes=16 * 1024 * 1024),
+        name="mix_rows",
+    )(jnp.stack([my_half, count]).astype(jnp.int32), second, after, before, mine, gain, probe_all)
 
 
 def pool_kernel(halves_ref, val_ref, out_w_ref, o_ref):
@@ -192,20 +236,14 @@
     own_head = head_of[None, :] == jnp.arange(local_heads, dtype=jnp.int32)[:, None]
     probe = jnp.where(own_head, pool_query[None, :], 0).astype(bf16)
     probe_keys = dot(probe, pool_kv[0], nt) * (1.0 / math.sqrt(HDIM))
-    probe_keys = jnp.concatenate(split_bf16(probe_keys, 2), axis=0).reshape(-1, pmax)
+    probe_keys = jnp.concatenate(split_bf16(probe_keys, 2), axis=0)
     probe_rows = probe_keys.shape[0]
-    padding = jnp.zeros((-probe_rows % 16, pmax), bf16)
-
-    own_x = jnp.concatenate([patches[0].T, patches[1].T, probe_keys, padding], axis=0)
+
+    own_x = patches.transpose(0, 2, 1).reshape(rows_img * dlocal, pmax)
     left_x, right_x = shift(own_x, 1), shift(own_x, -1)
-
     texts = spread_all(text_emb, "plane").reshape(-1, width)
     texts, left_x, right_x = lax.optimization_barrier((texts, left_x, right_x))
     far_a, far_b = shift(left_x[:dlocal], 1), shift(right_x[dlocal:], -1)
-    came = [own_x[2 * dlocal :], right_x[2 * dlocal :], far_b[dlocal:], left_x[2 * dlocal :]]
-    came = [x[:probe_rows] for x in came]
-    probe_all = jnp.stack([lax.select_n((j - me) % shards, *came) for j in range(shards)])
-    probe_all = probe_all.reshape(shards, 2, local_heads, width).transpose(1, 0, 2, 3).reshape(2 * heads, width)
 
     my_image, my_half = me // 2, me % 2
     w_rows = w_qkv.transpose(0, 2, 1).reshape(3 * dlocal, width)
@@ -219,37 +257,32 @@
     quarter = half // 2
     even = my_half == 0
     far = jnp.where(even, first[:half], first[half:])
-    far_after, far_before = shift(far[:quarter], 1), shift(far[quarter:], -1)
+    tail = jnp.concatenate([probe_keys, jnp.zeros((-probe_rows % 16, width), bf16)], axis=0)
+    far_after = shift(jnp.concatenate([far[:quarter], tail], axis=0), 1)
+    far_before = shift(jnp.concatenate([far[quarter:], tail], axis=0), -1)
+    left_keys, right_keys = far_after[quarter:], far_before[quarter:]
+    far_after, far_before = far_after[:quarter], far_before[:quarter]
     after = jnp.where(even, second[half:], first[:half])
     before = jnp.where(even, first[half:], second[:half])
-    own_part = jnp.where(even, second[:half], second[half:]).astype(f32)
 
     def added(left, right):
         return (left.astype(f32) + right.astype(f32)).astype(bf16)
 
-    after = jnp.concatenate([added(after[:quarter], far_after), after[quarter:]], axis=0)
+    after = jnp.concatenate([added(after[:quarter], far_after), after[quarter:], left_keys], axis=0)
     before = jnp.concatenate([before[:quarter], added(before[quarter:], far_before)], axis=0)
-    parts = own_part + shift(after, 1).astype(f32) + shift(before, -1).astype(f32)
-    resid = jnp.where(my_half == 0, mine[:, :half], mine[:, half:]).T
-    stream = (resid.astype(f32) + parts).astype(bf16)
-    normed2 = layer_norm(stream, ln2_gain).astype(bf16)
-    both = dot(probe_all, normed2, nt)
-    pool_scores = both[:heads] + both[heads:]
-    row_ids = my_half * half + jnp.arange(half, dtype=jnp.int32)
-    pool_scores = jnp.where((row_ids < my_count)[None, :], pool_scores, -1e30)
-    highest = jnp.max(pool_scores, axis=-1, keepdims=True)
-    raised = jnp.exp(pool_scores - highest)
-    total = jnp.sum(raised, axis=-1, keepdims=True)
-    mixed = dot((raised / total).astype(bf16), normed2)
-    lse = jnp.broadcast_to(highest + jnp.log(total), (heads, 128))
-    send = jnp.concatenate([mixed, lse], axis=1).reshape(shards, local_heads, width + 128)
+    after, before = shift(after, 1), shift(before, -1)
+    came = [x[:probe_rows] for x in (tail, right_keys, after[half:], left_keys)]
+    keys = [lax.select_n((j - me) % shards, *came) for j in range(shards)]
+    probe_all = jnp.concatenate([k[:local_heads] for k in keys] + [k[local_heads:] for k in keys], axis=0)
+    send = mix_rows(my_half, my_count, second, after, before, mine, ln2_gain[None], probe_all)
+    send = send.reshape(shards, local_heads, width + 128)
     halves = lax.all_to_all(send, "mp", 0, 0).reshape(shards * local_heads, width + 128)
     shares = pool_embed(halves, pool_kv.transpose(0, 2, 1), pool_out)
 
 
-    pairs = jnp.broadcast_to(image_pair.astype(f32)[:, None], (rows_img, 128))
-    column = spread_all(jnp.concatenate([shares, pairs], axis=1), ("near", "mp"))
-    column = column.reshape(-1, shards, rows_img, width + 128)
+    pairs = jnp.broadcast_to(image_pair.astype(bf16)[:, None], (rows_img, 128))
+    column = spread_all(jnp.concatenate([shares.astype(bf16), pairs], axis=1), ("near", "mp"))
+    column = column.reshape(-1, shards, rows_img, width + 128).astype(f32)
     embeds = jnp.sum(column[..., :width], axis=1)
     inv_img = lax.rsqrt(jnp.sum(embeds * embeds, axis=-1, keepdims=True) + 1e-06)
     zimg = embeds * inv_img
@@ -270,8 +303,9 @@
     gimg = dot_exact(dlog * inv_txt[None, :], texts).reshape(nears, rows_img, width)
     gtxt = jnp.dot(dlog.T, z_part, precision=lax.Precision.HIGHEST).reshape(planes, rows_img, width)
 
-    gtxt = jnp.sum(lax.all_to_all(gtxt, "plane", 0, 0), axis=0)
+    gtxt = jnp.sum(lax.all_to_all(gtxt.astype(bf16), "plane", 0, 0).astype(f32), axis=0)
     gimg_own = lax.dynamic_index_in_dim(gimg, near, 0, False)
+    gimg_own, gtxt = lax.optimization_barrier((gimg_own, gtxt))
     for k in range(1, nears):
         gimg_own += shift(lax.dynamic_index_in_dim(gimg, (near + k) % nears, 0, False), k, "near")
     gimg = gimg_own

time: 161 us -> 147 us (0.913)
  waiting for transfers between devices: 44 us -> 31.9 us
  other arithmetic: 8.04 us -> 4.91 us
    all_to_all x1, waiting for transfers between devices: 10.8 us -> 1.18 us  [per_device(): lax.all_to_all(gtxt.astype(bf16), 'plane', 0, 0).astype(f32)]
    ppermute x11, waiting for transfers between devices: 11.4 us -> 14.9 us  [shift(): return lax.ppermute(value, axis, pairs)]
    all_to_all x2, starting transfers between devices: 18.9 us -> 22.4 us  [spread_all(): lax.all_to_all(jnp.broadcast_to(value[None], (count,) + value.shape), axi...]
    all_to_all x2, waiting for transfers between devices: 14.6 us -> 11.4 us  [spread_all(): lax.all_to_all(jnp.broadcast_to(value[None], (count,) + value.shape), axi...]
    all_to_all x1, waiting for transfers between devices: 7.18 us -> 4.45 us  [per_device(): lax.all_to_all(send, 'mp', 0, 0).reshape(shards * local_heads, width + 128)]
    concatenate x1 -> x2, local copies, waits for them, and re-layouts: 0.08 us -> 2.58 us  [the longest x1 2.51 us: per_device(): jnp.concatenate([k[:local_heads] for k in keys] + [k[local_heads:] for k...]
    pallas_call x2, Pallas kernels: 10.5 us -> 8.55 us  [attend(): pl.pallas_call(attend_kernel, grid_spec=pltpu.PrefetchScalarGridSpec(num_...]
    unnamed x44 -> x34, local copies, waits for them, and re-layouts: 3.8 us -> 5.75 us
  transfers between devices with their start and end apart: 15 -> 15, of which waited for: 7 -> 10; matrix products, arithmetic and copies ran while one was open for 8% -> 8% of each run, Pallas kernels for 0% -> 0%
where the time goes in v5:
time: 147 us; the launch traced here: 145 us
  starting transfers between devices  74.8 us (51%)
  waiting for transfers between devices  31.9 us (22%)
  local copies, waits for them, and re-layouts  15.8 us (11%)
  Pallas kernels  10.8 us (7%)
  between operations  5.11 us (3%)
  other arithmetic  4.91 us (3%)
  matrix products  1.95 us (1%)
    ppermute x11, starting transfers between devices, shift(): return lax.ppermute(value, axis, pairs)  41.9 us
    all_to_all x2, starting transfers between devices, spread_all(): lax.all_to_all(jnp.broadcast_to(value[None], (count,) + value.shape), axi...  22.4 us
    ppermute x11, waiting for transfers between devices, shift(): return lax.ppermute(value, axis, pairs)  14.9 us
    all_to_all x2, waiting for transfers between devices, spread_all(): lax.all_to_all(jnp.broadcast_to(value[None], (count,) + value.shape), axi...  11.4 us
    pallas_call x2, Pallas kernels, attend(): pl.pallas_call(attend_kernel, grid_spec=pltpu.PrefetchScalarGridSpec(num_...  8.55 us
    all_to_all x1, starting transfers between devices, per_device(): lax.all_to_all(gtxt.astype(bf16), 'plane', 0, 0).astype(f32)  6.75 us
    unnamed x34, local copies, waits for them, and re-layouts  5.75 us
    all_to_all x1, waiting for transfers between devices, per_device(): lax.all_to_all(send, 'mp', 0, 0).reshape(shards * local_heads, width + 128)  4.45 us
  transfers between devices with their start and end apart: 15, of which 10 were waited for; matrix products, arithmetic and copies ran while one was open for 8% of the time, Pallas kernels for 0%

profile of v5, /device:TPU:1, one launch (start us, length us, event | category | flops | bytes accessed | tf_op | source)
XLA Modules:
  0.0 145.3 jit_solution(16633115756707932375)
XLA Ops:
  0.6 6.6 %collective-permute-start = (bf16[576,256]{1,0:T(8,128)(2,1)}, bf16[576,256]{1,0:T(8,128)(2,1)S(1)}, u32[]{:S(2)}, u32[]{:S(2)}) collective-permute-start(bf16[576,256]{1,0:T(8,128)(2,1)} %bitcast.50), channel_id=1, source_target_pairs={{0,1},{1,2},{2,3},{3,0},{4,5},{5,6},{6,7},{7,4},{8,9},{9,10},{10,1... | collective-permute-start | bytes 884744 | tf_op jit(solution)/shard_map/ppermute | solution.py:21
  7.3 6.8 %collective-permute-start.1 = (bf16[576,256]{1,0:T(8,128)(2,1)}, bf16[576,256]{1,0:T(8,128)(2,1)S(1)}, u32[]{:S(2)}, u32[]{:S(2)}) collective-permute-start(bf16[576,256]{1,0:T(8,128)(2,1)} %bitcast.51), channel_id=1, source_target_pairs={{0,3},{1,0},{2,1},{3,2},{4,7},{5,4},{6,5},{7,6},{8,11},{9,8},{10,9... | collective-permute-start | bytes 884744 | tf_op jit(solution)/shard_map/ppermute | solution.py:21
  15.5 9.8 %all-to-all-start = ((bf16[32,2,1152]{2,1,0:T(2,128)(2,1)}), bf16[32,2,1152]{2,1,0:T(2,128)(2,1)S(1)}, u32[]{:S(2)}, u32[]{:S(2)}) async-start(bf16[32,2,1152]{2,1,0:T(2,128)(2,1)} %broadcast_in_dim.30), calls=%async_computation | async-start | bytes 294912 | tf_op jit(solution)/shard_map/all_to_all | solution.py:15
  31.3 3.2 %all-to-all-done = bf16[32,2,1152]{2,1,0:T(2,128)(2,1)S(1)} async-done(((bf16[32,2,1152]{2,1,0:T(2,128)(2,1)}), bf16[32,2,1152]{2,1,0:T(2,128)(2,1)S(1)}, u32[]{:S(2)}, u32[]{:S(2)}) %all-to-all-start) | async-done | bytes 147488 | tf_op jit(solution)/shard_map/all_to_all | solution.py:15
  35.3 2.2 %collective-permute-start.2 = (bf16[288,256]{1,0:T(8,128)(2,1)S(1)}, bf16[288,256]{1,0:T(8,128)(2,1)S(1)}, u32[]{:S(2)}, u32[]{:S(2)}) collective-permute-start(bf16[288,256]{1,0:T(8,128)(2,1)S(1)} %slice.122), channel_id=1, source_target_pairs={{0,1},{1,2},{2,3},{3,0},{4,5},{5,6},{6,7},{7,4},{8,9},{9,10},{10,1... | collective-permute-start | bytes 442376 | tf_op jit(solution)/shard_map/ppermute | solution.py:21
  37.5 5.2 %collective-permute-start.3 = (bf16[288,256]{1,0:T(8,128)(2,1)S(1)}, bf16[288,256]{1,0:T(8,128)(2,1)S(1)}, u32[]{:S(2)}, u32[]{:S(2)}) collective-permute-start(bf16[288,256]{1,0:T(8,128)(2,1)S(1)} %slice.123), channel_id=1, source_target_pairs={{0,3},{1,0},{2,1},{3,2},{4,7},{5,4},{6,5},{7,6},{8,11},{9,8},{10,9... | collective-permute-start | bytes 442376 | tf_op jit(solution)/shard_map/ppermute | solution.py:21
  43.4 4.0 %collective-permute-done.3.far_b_ref = bf16[288,256]{1,0:T(8,128)(2,1)S(1)} collective-permute-done((bf16[288,256]{1,0:T(8,128)(2,1)S(1)}, bf16[288,256]{1,0:T(8,128)(2,1)S(1)}, u32[]{:S(2)}, u32[]{:S(2)}) %collective-permute-start.3) | collective-permute-done | bytes 147488 | tf_op jit(solution)/shard_map/ppermute | solution.py:21
  49.0 4.3 %attend.3 = (bf16[256,1152]{1,0:T(8,128)(2,1)S(1)}, bf16[1152,256]{1,0:T(8,128)(2,1)}) custom-call(s32[3]{0:T(128)S(1)} %get-tuple-element.55.scalar_ref, bf16[576,256]{1,0:T(8,128)(2,1)S(1)} %bitcast.52, bf16[576,256]{1,0:T(8,128)(2,1)S(1)} %collective-permute-done.left_ref, bf16[576,256]{1,0:T(8,128)(2,1)S(1)} %collective-permute-done.1.right_ref, ...), custom_call_target="tpu_custom_call" | custom-call | flops 6039797760 | bytes 5013504 | tf_op jit(solution)/shard_map/attend/pallas_call | solution.py:84
  54.2 4.3 %attend.2 = (bf16[256,1152]{1,0:T(8,128)(2,1)S(1)}, bf16[1152,256]{1,0:T(8,128)(2,1)S(1)}) custom-call(s32[3]{0:T(128)S(1)} %get-tuple-element.54.scalar_ref, bf16[576,256]{1,0:T(8,128)(2,1)S(1)} %bitcast.53, bf16[576,256]{1,0:T(8,128)(2,1)S(1)} %collective-permute-done.left_ref, bf16[576,256]{1,0:T(8,128)(2,1)S(1)} %collective-permute-done.1.right_ref, ...), custom_call_target="tpu_custom_call" | custom-call | flops 6039797760 | bytes 5013504 | tf_op jit(solution)/shard_map/attend/pallas_call | solution.py:84
  58.7 5.2 %collective-permute-start.4 = (bf16[80,1152]{1,0:T(8,128)(2,1)S(1)}, bf16[80,1152]{1,0:T(8,128)(2,1)S(1)}, u32[]{:S(2)}, u32[]{:S(2)}) collective-permute-start(bf16[80,1152]{1,0:T(8,128)(2,1)S(1)} %get-tuple-element.39), channel_id=1, source_target_pairs={{0,1},{1,2},{2,3},{3,0},{4,5},{5,6},{6,7},{7,4},{8,9},{9,10},{10,1... | collective-permute-start | bytes 552968 | tf_op jit(solution)/shard_map/ppermute | solution.py:21
  63.9 2.2 %collective-permute-start.6 = (bf16[80,1152]{1,0:T(8,128)(2,1)S(1)}, bf16[80,1152]{1,0:T(8,128)(2,1)S(1)}, u32[]{:S(2)}, u32[]{:S(2)}) collective-permute-start(bf16[80,1152]{1,0:T(8,128)(2,1)S(1)} %get-tuple-element.38), channel_id=1, source_target_pairs={{0,3},{1,0},{2,1},{3,2},{4,7},{5,4},{6,5},{7,6},{8,11},{9,8},{10,9... | collective-permute-start | bytes 552968 | tf_op jit(solution)/shard_map/ppermute | solution.py:21
  66.2 3.0 %collective-permute-done.4 = bf16[80,1152]{1,0:T(8,128)(2,1)S(1)} collective-permute-done((bf16[80,1152]{1,0:T(8,128)(2,1)S(1)}, bf16[80,1152]{1,0:T(8,128)(2,1)S(1)}, u32[]{:S(2)}, u32[]{:S(2)}) %collective-permute-start.4) | collective-permute-done | bytes 184352 | tf_op jit(solution)/shard_map/ppermute | solution.py:21
  69.3 2.4 %collective-permute-start.5 = (bf16[144,1152]{1,0:T(8,128)(2,1)S(1)}, bf16[144,1152]{1,0:T(8,128)(2,1)S(1)}, u32[]{:S(2)}, u32[]{:S(2)}) collective-permute-start(bf16[144,1152]{1,0:T(8,128)(2,1)S(1)} %pad_maximum_fusion), channel_id=1, source_target_pairs={{0,1},{1,2},{2,3},{3,0},{4,5},{5,6},{6,7},{7,4},{8,9},{9,10},{10,1... | collective-permute-start | bytes 995336 | tf_op jit(solution)/shard_map/ppermute | solution.py:21
  73.2 3.6 %collective-permute-start.7 = (bf16[128,1152]{1,0:T(8,128)(2,1)S(1)}, bf16[128,1152]{1,0:T(8,128)(2,1)S(1)}, u32[]{:S(2)}, u32[]{:S(2)}) collective-permute-start(bf16[128,1152]{1,0:T(8,128)(2,1)S(1)} %pad_maximum_fusion.1), channel_id=1, source_target_pairs={{0,3},{1,0},{2,1},{3,2},{4,7},{5,4},{6,5},{7,6},{8,11},{9,8},{10,9... | collective-permute-start | bytes 884744 | tf_op jit(solution)/shard_map/ppermute | solution.py:21
  76.8 6.1 %collective-permute-done.5.after_ref = bf16[144,1152]{1,0:T(8,128)(2,1)S(1)} collective-permute-done((bf16[144,1152]{1,0:T(8,128)(2,1)S(1)}, bf16[144,1152]{1,0:T(8,128)(2,1)S(1)}, u32[]{:S(2)}, u32[]{:S(2)}) %collective-permute-start.5) | collective-permute-done | bytes 331808 | tf_op jit(solution)/shard_map/ppermute | solution.py:21
  83.1 2.5 %concatenate.36.probe_ref = bf16[32,1152]{1,0:T(8,128)(2,1)} concatenate(bf16[4,1152]{1,0:T(4,128)(2,1)S(1)} %get-tuple-element.47, bf16[4,1152]{1,0:T(4,128)(2,1)S(1)} %get-tuple-element.45, bf16[4,1152]{1,0:T(4,128)(2,1)S(1)} %get-tuple-element.43, bf16[4,1152]{1,0:T(4,128)(2,1)S(1)} %get-tuple-element.41, bf16[4,1152]{1,0:T(4,128)(2,1)S(1)} %get-tuple-element.46, ...), dimensions={0} | concatenate | bytes 147456 | tf_op jit(solution)/shard_map/concatenate | solution.py:276
  91.9 3.7 %all-to-all-start.1 = ((f32[4,4,1280]{2,1,0:T(4,128)}), f32[4,4,1280]{2,1,0:T(4,128)S(1)}, u32[]{:S(2)}, u32[]{:S(2)}) async-start(f32[4,4,1280]{2,1,0:T(4,128)} %reshape.144), calls=%async_computation.1 | async-start | bytes 163840 | tf_op jit(solution)/shard_map/all_to_all | solution.py:279
  98.1 4.5 %all-to-all-done.1 = f32[4,4,1280]{2,1,0:T(4,128)S(1)} async-done(((f32[4,4,1280]{2,1,0:T(4,128)}), f32[4,4,1280]{2,1,0:T(4,128)S(1)}, u32[]{:S(2)}, u32[]{:S(2)}) %all-to-all-start.1) | async-done | bytes 81952 | tf_op jit(solution)/shard_map/all_to_all | solution.py:279
  104.1 12.6 %all-to-all-start.2 = ((bf16[16,2,1280]{2,1,0:T(2,128)(2,1)}), bf16[16,2,1280]{2,1,0:T(2,128)(2,1)S(1)}, u32[]{:S(2)}, u32[]{:S(2)}) async-start(bf16[16,2,1280]{2,1,0:T(2,128)(2,1)} %broadcast_in_dim.66), calls=%async_computation.2 | async-start | bytes 163840 | tf_op jit(solution)/shard_map/all_to_all | solution.py:15
  116.7 8.2 %all-to-all-done.2 = bf16[16,2,1280]{2,1,0:T(2,128)(2,1)S(1)} async-done(((bf16[16,2,1280]{2,1,0:T(2,128)(2,1)}), bf16[16,2,1280]{2,1,0:T(2,128)(2,1)S(1)}, u32[]{:S(2)}, u32[]{:S(2)}) %all-to-all-start.2) | async-done | bytes 81952 | tf_op jit(solution)/shard_map/all_to_all | solution.py:15
  127.2 6.7 %all-to-all-start.3 = ((bf16[32,2,1152]{2,1,0:T(2,128)(2,1)}), bf16[32,2,1152]{2,1,0:T(2,128)(2,1)S(1)}, u32[]{:S(2)}, u32[]{:S(2)}) async-start(bf16[32,2,1152]{2,1,0:T(2,128)(2,1)} %copy.29), calls=%async_computation.3 | async-start | bytes 294912 | tf_op jit(solution)/shard_map/all_to_all | solution.py:306
  134.2 2.4 %collective-permute-start.10 = (f32[2,1152]{1,0:T(2,128)S(1)}, f32[2,1152]{1,0:T(2,128)S(1)}, u32[]{:S(2)}, u32[]{:S(2)}) collective-permute-start(f32[2,1152]{1,0:T(2,128)S(1)} %get-tuple-element.35), channel_id=1, source_target_pairs={{0,12},{4,0},{8,4},{12,8},{1,13},{5,1},{9,5},{13,9},{2,14},{6,2},{... | collective-permute-start | bytes 27656 | tf_op jit(solution)/shard_map/ppermute | solution.py:21
  136.5 3.2 %collective-permute-start.8 = (f32[2,1152]{1,0:T(2,128)S(1)}, f32[2,1152]{1,0:T(2,128)S(1)}, u32[]{:S(2)}, u32[]{:S(2)}) collective-permute-start(f32[2,1152]{1,0:T(2,128)S(1)} %get-tuple-element.34), channel_id=1, source_target_pairs={{0,4},{4,8},{8,12},{12,0},{1,5},{5,9},{9,13},{13,1},{2,6},{6,10},{... | collective-permute-start | bytes 27656 | tf_op jit(solution)/shard_map/ppermute | solution.py:21
  139.7 2.2 %collective-permute-start.9 = (f32[2,1152]{1,0:T(2,128)S(1)}, f32[2,1152]{1,0:T(2,128)S(1)}, u32[]{:S(2)}, u32[]{:S(2)}) collective-permute-start(f32[2,1152]{1,0:T(2,128)S(1)} %get-tuple-element.36), channel_id=1, source_target_pairs={{0,8},{4,12},{8,0},{12,4},{1,9},{5,13},{9,1},{13,5},{2,10},{6,14},... | collective-permute-start | bytes 27656 | tf_op jit(solution)/shard_map/ppermute | solution.py:21
  (115 shorter events, 25.4 us)
Async XLA Ops:
  0.6 42.2 %copy-start.14 = (f32[1152]{0:T(1024)S(1)}, f32[1152]{0:T(1024)}, u32[]{:S(2)}) copy-start(f32[1152]{0:T(1024)} %param.15) | copy-start | bytes 13828
  0.6 34.6 %collective-permute-start = (bf16[576,256]{1,0:T(8,128)(2,1)}, bf16[576,256]{1,0:T(8,128)(2,1)S(1)}, u32[]{:S(2)}, u32[]{:S(2)}) collective-permute-start(bf16[576,256]{1,0:T(8,128)(2,1)} %bitcast.50), channel_id=1, source_target_pairs={{0,1},{1,2},{2,3},{3,0},{4,5},{5,6},{6,7},{7,4},{8,9},{9,10},{10,1... | collective-permute-start | bytes 884744 | tf_op jit(solution)/shard_map/ppermute | solution.py:21
  7.3 28.0 %collective-permute-start.1 = (bf16[576,256]{1,0:T(8,128)(2,1)}, bf16[576,256]{1,0:T(8,128)(2,1)S(1)}, u32[]{:S(2)}, u32[]{:S(2)}) collective-permute-start(bf16[576,256]{1,0:T(8,128)(2,1)} %bitcast.51), channel_id=1, source_target_pairs={{0,3},{1,0},{2,1},{3,2},{4,7},{5,4},{6,5},{7,6},{8,11},{9,8},{10,9... | collective-permute-start | bytes 884744 | tf_op jit(solution)/shard_map/ppermute | solution.py:21
  15.5 27.5 %copy-start.15 = (f32[1152]{0:T(1024)S(1)}, f32[1152]{0:T(1024)}, u32[]{:S(2)}) copy-start(f32[1152]{0:T(1024)} %param.18) | copy-start | bytes 13828
  15.5 27.7 %copy-start.12 = (bf16[2,1152]{1,0:T(2,128)(2,1)S(1)}, bf16[2,1152]{1,0:T(2,128)(2,1)}, u32[]{:S(2)}) copy-start(bf16[2,1152]{1,0:T(2,128)(2,1)} %param.22) | copy-start | bytes 13828
  15.5 31.8 %copy-start.7 = (bf16[288,1152]{1,0:T(8,128)(2,1)S(1)}, bf16[288,1152]{1,0:T(8,128)(2,1)}, u32[]{:S(2)}) copy-start(bf16[288,1152]{1,0:T(8,128)(2,1)} %out_w_ref.4) | copy-start | bytes 1990660
  15.5 31.8 %copy-start.8 = (bf16[2,256,288]{1,2,0:T(8,128)(2,1)S(1)}, bf16[2,256,288]{1,2,0:T(8,128)(2,1)}, u32[]{:S(2)}) copy-start(bf16[2,256,288]{1,2,0:T(8,128)(2,1)} %param.13) | copy-start | bytes 884740
  15.5 19.0 %all-to-all-start = ((bf16[32,2,1152]{2,1,0:T(2,128)(2,1)}), bf16[32,2,1152]{2,1,0:T(2,128)(2,1)S(1)}, u32[]{:S(2)}, u32[]{:S(2)}) async-start(bf16[32,2,1152]{2,1,0:T(2,128)(2,1)} %broadcast_in_dim.30), calls=%async_computation | async-start | bytes 294912 | tf_op jit(solution)/shard_map/all_to_all | solution.py:15
  35.3 8.1 %collective-permute-start.2 = (bf16[288,256]{1,0:T(8,128)(2,1)S(1)}, bf16[288,256]{1,0:T(8,128)(2,1)S(1)}, u32[]{:S(2)}, u32[]{:S(2)}) collective-permute-start(bf16[288,256]{1,0:T(8,128)(2,1)S(1)} %slice.122), channel_id=1, source_target_pairs={{0,1},{1,2},{2,3},{3,0},{4,5},{5,6},{6,7},{7,4},{8,9},{9,10},{10,1... | collective-permute-start | bytes 442376 | tf_op jit(solution)/shard_map/ppermute | solution.py:21
  37.5 9.9 %collective-permute-start.3 = (bf16[288,256]{1,0:T(8,128)(2,1)S(1)}, bf16[288,256]{1,0:T(8,128)(2,1)S(1)}, u32[]{:S(2)}, u32[]{:S(2)}) collective-permute-start(bf16[288,256]{1,0:T(8,128)(2,1)S(1)} %slice.123), channel_id=1, source_target_pairs={{0,3},{1,0},{2,1},{3,2},{4,7},{5,4},{6,5},{7,6},{8,11},{9,8},{10,9... | collective-permute-start | bytes 442376 | tf_op jit(solution)/shard_map/ppermute | solution.py:21
  58.7 10.4 %collective-permute-start.4 = (bf16[80,1152]{1,0:T(8,128)(2,1)S(1)}, bf16[80,1152]{1,0:T(8,128)(2,1)S(1)}, u32[]{:S(2)}, u32[]{:S(2)}) collective-permute-start(bf16[80,1152]{1,0:T(8,128)(2,1)S(1)} %get-tuple-element.39), channel_id=1, source_target_pairs={{0,1},{1,2},{2,3},{3,0},{4,5},{5,6},{6,7},{7,4},{8,9},{9,10},{10,1... | collective-permute-start | bytes 552968 | tf_op jit(solution)/shard_map/ppermute | solution.py:21
  63.9 9.2 %collective-permute-start.6 = (bf16[80,1152]{1,0:T(8,128)(2,1)S(1)}, bf16[80,1152]{1,0:T(8,128)(2,1)S(1)}, u32[]{:S(2)}, u32[]{:S(2)}) collective-permute-start(bf16[80,1152]{1,0:T(8,128)(2,1)S(1)} %get-tuple-element.38), channel_id=1, source_target_pairs={{0,3},{1,0},{2,1},{3,2},{4,7},{5,4},{6,5},{7,6},{8,11},{9,8},{10,9... | collective-permute-start | bytes 552968 | tf_op jit(solution)/shard_map/ppermute | solution.py:21
  69.3 13.6 %collective-permute-start.5 = (bf16[144,1152]{1,0:T(8,128)(2,1)S(1)}, bf16[144,1152]{1,0:T(8,128)(2,1)S(1)}, u32[]{:S(2)}, u32[]{:S(2)}) collective-permute-start(bf16[144,1152]{1,0:T(8,128)(2,1)S(1)} %pad_maximum_fusion), channel_id=1, source_target_pairs={{0,1},{1,2},{2,3},{3,0},{4,5},{5,6},{6,7},{7,4},{8,9},{9,10},{10,1... | collective-permute-start | bytes 995336 | tf_op jit(solution)/shard_map/ppermute | solution.py:21
  73.2 12.4 %collective-permute-start.7 = (bf16[128,1152]{1,0:T(8,128)(2,1)S(1)}, bf16[128,1152]{1,0:T(8,128)(2,1)S(1)}, u32[]{:S(2)}, u32[]{:S(2)}) collective-permute-start(bf16[128,1152]{1,0:T(8,128)(2,1)S(1)} %pad_maximum_fusion.1), channel_id=1, source_target_pairs={{0,3},{1,0},{2,1},{3,2},{4,7},{5,4},{6,5},{7,6},{8,11},{9,8},{10,9... | collective-permute-start | bytes 884744 | tf_op jit(solution)/shard_map/ppermute | solution.py:21
  83.0 12.6 %copy-start.16 = (s32[2]{0:T(128)S(1)}, s32[2]{0:T(128)}, u32[]{:S(2)}) copy-start(s32[2]{0:T(128)} %param.23) | copy-start | bytes 28
  88.1 14.4 %copy-start = (bf16[2,1152,288]{1,2,0:T(8,128)(2,1)S(1)}, bf16[2,1152,288]{1,2,0:T(8,128)(2,1)}, u32[]{:S(2)}) copy-start(bf16[2,1152,288]{1,2,0:T(8,128)(2,1)} %param.19) | copy-start | bytes 3981316
  88.1 14.4 %copy-start.1 = (bf16[288,1152]{1,0:T(8,128)(2,1)S(1)}, bf16[288,1152]{1,0:T(8,128)(2,1)}, u32[]{:S(2)}) copy-start(bf16[288,1152]{1,0:T(8,128)(2,1)} %out_w_ref.5) | copy-start | bytes 1990660
  91.9 10.6 %all-to-all-start.1 = ((f32[4,4,1280]{2,1,0:T(4,128)}), f32[4,4,1280]{2,1,0:T(4,128)S(1)}, u32[]{:S(2)}, u32[]{:S(2)}) async-start(f32[4,4,1280]{2,1,0:T(4,128)} %reshape.144), calls=%async_computation.1 | async-start | bytes 163840 | tf_op jit(solution)/shard_map/all_to_all | solution.py:279
  102.6 23.1 %copy-start.11 = (bf16[64,1152]{1,0:T(8,128)(2,1)S(1)}, bf16[64,1152]{1,0:T(8,128)(2,1)}, u32[]{:S(2)}) copy-start(bf16[64,1152]{1,0:T(8,128)(2,1)} %reshape.142) | copy-start | bytes 442372
  104.1 20.8 %all-to-all-start.2 = ((bf16[16,2,1280]{2,1,0:T(2,128)(2,1)}), bf16[16,2,1280]{2,1,0:T(2,128)(2,1)S(1)}, u32[]{:S(2)}, u32[]{:S(2)}) async-start(bf16[16,2,1280]{2,1,0:T(2,128)(2,1)} %broadcast_in_dim.66), calls=%async_computation.2 | async-start | bytes 163840 | tf_op jit(solution)/shard_map/all_to_all | solution.py:15
  127.2 16.0 %all-to-all-start.3 = ((bf16[32,2,1152]{2,1,0:T(2,128)(2,1)}), bf16[32,2,1152]{2,1,0:T(2,128)(2,1)S(1)}, u32[]{:S(2)}, u32[]{:S(2)}) async-start(bf16[32,2,1152]{2,1,0:T(2,128)(2,1)} %copy.29), calls=%async_computation.3 | async-start | bytes 294912 | tf_op jit(solution)/shard_map/all_to_all | solution.py:306
  134.2 10.0 %collective-permute-start.10 = (f32[2,1152]{1,0:T(2,128)S(1)}, f32[2,1152]{1,0:T(2,128)S(1)}, u32[]{:S(2)}, u32[]{:S(2)}) collective-permute-start(f32[2,1152]{1,0:T(2,128)S(1)} %get-tuple-element.35), channel_id=1, source_target_pairs={{0,12},{4,0},{8,4},{12,8},{1,13},{5,1},{9,5},{13,9},{2,14},{6,2},{... | collective-permute-start | bytes 27656 | tf_op jit(solution)/shard_map/ppermute | solution.py:21
  136.5 7.6 %collective-permute-start.8 = (f32[2,1152]{1,0:T(2,128)S(1)}, f32[2,1152]{1,0:T(2,128)S(1)}, u32[]{:S(2)}, u32[]{:S(2)}) collective-permute-start(f32[2,1152]{1,0:T(2,128)S(1)} %get-tuple-element.34), channel_id=1, source_target_pairs={{0,4},{4,8},{8,12},{12,0},{1,5},{5,9},{9,13},{13,1},{2,6},{6,10},{... | collective-permute-start | bytes 27656 | tf_op jit(solution)/shard_map/ppermute | solution.py:21
  139.7 4.7 %collective-permute-start.9 = (f32[2,1152]{1,0:T(2,128)S(1)}, f32[2,1152]{1,0:T(2,128)S(1)}, u32[]{:S(2)}, u32[]{:S(2)}) collective-permute-start(f32[2,1152]{1,0:T(2,128)S(1)} %get-tuple-element.36), channel_id=1, source_target_pairs={{0,8},{4,12},{8,0},{12,4},{1,9},{5,13},{9,1},{13,5},{2,10},{6,14},... | collective-permute-start | bytes 27656 | tf_op jit(solution)/shard_map/ppermute | solution.py:21
  (8 other events, 24.2 us)

commit v6 on v5

--- a/solution.py
+++ b/solution.py
@@ -45,7 +45,7 @@
 
 
 def attend_kernel(scalar_ref, own_ref, left_ref, right_ref, far_a_ref, far_b_ref, w_ref, out_w_ref, gain_ref,
-                  o_ref, x_ref, norm_ref, ctx_ref):
+                  o_ref, base_ref, x_ref, norm_ref, ctx_ref):
     f32, bf16 = jnp.float32, jnp.bfloat16
     width, pmax = x_ref.shape
     dlocal = out_w_ref.shape[0]
@@ -72,7 +72,12 @@
         total = jnp.sum(raised, axis=0, keepdims=True)
         ctx_ref[h * HDIM : (h + 1) * HDIM] = matmul(v.astype(bf16), raised.astype(bf16)) / total
     context = ctx_ref[...].T.astype(bf16)
-    o_ref[...] = matmul(context, out_w_ref[...]).astype(bf16)
+    out = matmul(context, out_w_ref[...])
+    o_ref[...] = out.astype(bf16)
+    half = pmax // 2
+    first_half = scalar_ref[3] == 0
+    resid = jnp.where(first_half, x_ref[:, :half].astype(f32), x_ref[:, half:].astype(f32))
+    base_ref[...] = resid.T + jnp.where(first_half, out[:half], out[half:])
 
 
 def attend(scalars, slices, w_rows, w_out, gain):
@@ -89,12 +94,16 @@
             in_specs=[of_image] * 3
             + [whole(dlocal, pmax)] * 2
             + [whole(3 * dlocal, width), whole(dlocal, width), whole(width, 1)],
-            out_specs=[whole(pmax, width), whole(width, pmax)],
-            scratch_shapes=[pltpu.VMEM((width, pmax), jnp.bfloat16), pltpu.VMEM((dlocal, pmax), jnp.float32)],
+            out_specs=[whole(pmax, width), whole(pmax // 2, width)],
+            scratch_shapes=[
+                pltpu.VMEM((width, pmax), jnp.bfloat16),
+                pltpu.VMEM((width, pmax), jnp.bfloat16),
+                pltpu.VMEM((dlocal, pmax), jnp.float32),
+            ],
         ),
         out_shape=[
             jax.ShapeDtypeStruct((pmax, width), jnp.bfloat16),
-            jax.ShapeDtypeStruct((width, pmax), jnp.bfloat16),
+            jax.ShapeDtypeStruct((pmax // 2, width), jnp.float32),
         ],
         compiler_params=pltpu.CompilerParams(vmem_limit_bytes=32 * 1024 * 1024),
         cost_estimate=pl.CostEstimate(
@@ -104,48 +113,48 @@
     )(jnp.stack(scalars).astype(jnp.int32), *slices, w_rows, w_out, gain)
 
 
-def mix_kernel(scalar_ref, own_ref, after_ref, before_ref, x_ref, gain_ref, probe_ref, o_ref):
+def mix_kernel(scalar_ref, base_ref, after_ref, before_ref, gain_ref, own_ref, right_ref, left_ref, o_ref):
     f32, bf16 = jnp.float32, jnp.bfloat16
-    half, width = own_ref.shape
-    heads = probe_ref.shape[0] // 2
-    stream = x_ref[...].astype(f32).T + (
-        own_ref[...].astype(f32) + after_ref[:half].astype(f32) + before_ref[...].astype(f32)
+    half, width = base_ref.shape
+    shards, local = o_ref.shape[:2]
+    heads, block = shards * local, own_ref.shape[0]
+    stream = base_ref[...] + after_ref[:half].astype(f32) + before_ref[...].astype(f32)
+    normed = layer_norm(stream.astype(bf16), gain_ref[...]).astype(bf16)
+    keys = jnp.concatenate([own_ref[...], right_ref[...], after_ref[half:], left_ref[...]], axis=0)
+    both = matmul(keys, normed, NT)
+    scores = jnp.concatenate(
+        [both[k * block : k * block + local] + both[k * block + local : k * block + 2 * local] for k in range(shards)],
+        axis=0,
     )
-    normed = layer_norm(stream.astype(bf16), gain_ref[...]).astype(bf16)
-    scores = matmul(probe_ref[...], normed, NT)
-    scores = scores[:heads] + scores[heads:]
     row = scalar_ref[0] * half + lax.broadcasted_iota(jnp.int32, (heads, half), 1)
     scores = jnp.where(row < scalar_ref[1], scores, -1e30)
     highest = jnp.max(scores, axis=1, keepdims=True)
     raised = jnp.exp(scores - highest)
     total = jnp.sum(raised, axis=1, keepdims=True)
-    o_ref[:, :width] = matmul((raised / total).astype(bf16), normed)
-    o_ref[:, width:] = jnp.broadcast_to(highest + jnp.log(total), (heads, o_ref.shape[1] - width))
-
-
-def mix_rows(my_half, count, second, after, before, mine, gain, probe_all):
+    mixed = matmul((raised / total).astype(bf16), normed)
+    lse = jnp.broadcast_to(highest + jnp.log(total), (heads, o_ref.shape[2] - width))
+    for k in range(shards):
+        source = lax.rem(scalar_ref[2] + k, shards)
+        o_ref[source, :, :width] = mixed[k * local : (k + 1) * local]
+        o_ref[source, :, width:] = lse[k * local : (k + 1) * local]
+
+
+def mix_rows(scalars, base, after, before, gain, own_keys, right_keys, left_keys, shards, local):
     half, width = before.shape
-    heads = probe_all.shape[0] // 2
-    whole = lambda *shape: pl.BlockSpec(shape, lambda i, scalar_ref: (0, 0))
+    whole = lambda *shape: pl.BlockSpec(shape, lambda i, scalar_ref: (0,) * len(shape))
+    operands = (base, after, before, gain, own_keys, right_keys, left_keys)
     return pl.pallas_call(
         mix_kernel,
         grid_spec=pltpu.PrefetchScalarGridSpec(
             num_scalar_prefetch=1,
             grid=(1,),
-            in_specs=[
-                pl.BlockSpec((half, width), lambda i, scalar_ref: (scalar_ref[0], 0)),
-                whole(*after.shape),
-                whole(half, width),
-                pl.BlockSpec((width, half), lambda i, scalar_ref: (0, scalar_ref[0])),
-                whole(1, width),
-                whole(2 * heads, width),
-            ],
-            out_specs=whole(heads, width + 128),
+            in_specs=[whole(*x.shape) for x in operands],
+            out_specs=whole(shards, local, width + 128),
         ),
-        out_shape=jax.ShapeDtypeStruct((heads, width + 128), jnp.float32),
+        out_shape=jax.ShapeDtypeStruct((shards, local, width + 128), jnp.float32),
         compiler_params=pltpu.CompilerParams(vmem_limit_bytes=16 * 1024 * 1024),
         name="mix_rows",
-    )(jnp.stack([my_half, count]).astype(jnp.int32), second, after, before, mine, gain, probe_all)
+    )(jnp.stack(scalars).astype(jnp.int32), *operands)
 
 
 def pool_kernel(halves_ref, val_ref, out_w_ref, o_ref):
@@ -242,8 +251,8 @@
     own_x = patches.transpose(0, 2, 1).reshape(rows_img * dlocal, pmax)
     left_x, right_x = shift(own_x, 1), shift(own_x, -1)
     texts = spread_all(text_emb, "plane").reshape(-1, width)
-    texts, left_x, right_x = lax.optimization_barrier((texts, left_x, right_x))
     far_a, far_b = shift(left_x[:dlocal], 1), shift(right_x[dlocal:], -1)
+    texts, far_a, far_b = lax.optimization_barrier((texts, far_a, far_b))
 
     my_image, my_half = me // 2, me % 2
     w_rows = w_qkv.transpose(0, 2, 1).reshape(3 * dlocal, width)
@@ -251,15 +260,15 @@
     my_count = jnp.where(my_image == 0, patch_count[0], patch_count[1])
     other_count = jnp.where(my_image == 0, patch_count[1], patch_count[0])
     slices = (own_x, left_x, right_x, far_a, far_b)
-    first, _ = attend((me, 1 - my_image, other_count), slices, w_rows, w_out, gain)
-    second, mine = attend((me, my_image, my_count), slices, w_rows, w_out, gain)
-
+    first, _ = attend((me, 1 - my_image, other_count, my_half), slices, w_rows, w_out, gain)
     quarter = half // 2
     even = my_half == 0
     far = jnp.where(even, first[:half], first[half:])
     tail = jnp.concatenate([probe_keys, jnp.zeros((-probe_rows % 16, width), bf16)], axis=0)
     far_after = shift(jnp.concatenate([far[:quarter], tail], axis=0), 1)
     far_before = shift(jnp.concatenate([far[quarter:], tail], axis=0), -1)
+    my_count, far_after = lax.optimization_barrier((my_count, far_after))
+    second, base = attend((me, my_image, my_count, my_half), slices, w_rows, w_out, gain)
     left_keys, right_keys = far_after[quarter:], far_before[quarter:]
     far_after, far_before = far_after[:quarter], far_before[:quarter]
     after = jnp.where(even, second[half:], first[:half])
@@ -271,14 +280,11 @@
     after = jnp.concatenate([added(after[:quarter], far_after), after[quarter:], left_keys], axis=0)
     before = jnp.concatenate([before[:quarter], added(before[quarter:], far_before)], axis=0)
     after, before = shift(after, 1), shift(before, -1)
-    came = [x[:probe_rows] for x in (tail, right_keys, after[half:], left_keys)]
-    keys = [lax.select_n((j - me) % shards, *came) for j in range(shards)]
-    probe_all = jnp.concatenate([k[:local_heads] for k in keys] + [k[local_heads:] for k in keys], axis=0)
-    send = mix_rows(my_half, my_count, second, after, before, mine, ln2_gain[None], probe_all)
-    send = send.reshape(shards, local_heads, width + 128)
+    send = mix_rows(
+        (my_half, my_count, me), base, after, before, ln2_gain[None], tail, right_keys, left_keys, shards, local_heads
+    )
     halves = lax.all_to_all(send, "mp", 0, 0).reshape(shards * local_heads, width + 128)
     shares = pool_embed(halves, pool_kv.transpose(0, 2, 1), pool_out)
-
 
     pairs = jnp.broadcast_to(image_pair.astype(bf16)[:, None], (rows_img, 128))
     column = spread_all(jnp.concatenate([shares.astype(bf16), pairs], axis=1), ("near", "mp"))

time: 147 us -> 139 us (0.946)
  local copies, waits for them, and re-layouts: 15.8 us -> 6.74 us
  starting transfers between devices: 74.8 us -> 76.8 us
  other arithmetic: 4.91 us -> 3.39 us
    unnamed x34 -> x20, local copies, waits for them, and re-layouts: 5.75 us -> 1.6 us
    all_to_all x2, waiting for transfers between devices: 11.4 us -> 8.19 us  [spread_all(): lax.all_to_all(jnp.broadcast_to(value[None], (count,) + value.shape), axi...]
    concatenate x2 -> x0, local copies, waits for them, and re-layouts: 2.58 us -> none  [the longest x1 2.51 us: per_device(): jnp.concatenate([k[:local_heads] for k in keys] + [k[local_heads:] for k...]
    ppermute x11, starting transfers between devices: 41.9 us -> 44 us  [shift(): return lax.ppermute(value, axis, pairs)]
    ppermute x11, waiting for transfers between devices: 14.9 us -> 16.8 us  [shift(): return lax.ppermute(value, axis, pairs)]
    all_to_all x1, starting transfers between devices: 6.75 us -> 8.39 us  [per_device(): lax.all_to_all(gtxt.astype(bf16), 'plane', 0, 0).astype(f32)]
    reshape x1 -> x0, local copies, waits for them, and re-layouts: 1.55 us -> none  [per_device(): send = send.reshape(shards, local_heads, width + 128)]
  transfers between devices with their start and end apart: 15 -> 15, of which waited for: 10 -> 7; matrix products, arithmetic and copies ran while one was open for 8% -> 5% of each run, Pallas kernels for 0% -> 3%
where the time goes in v6:
time: 139 us; the launch traced here: 138 us
  starting transfers between devices  76.8 us (55%)
  waiting for transfers between devices  31.5 us (23%)
  Pallas kernels  12.2 us (9%)
  local copies, waits for them, and re-layouts  6.74 us (5%)
  between operations  5.1 us (4%)
  other arithmetic  3.39 us (2%)
  matrix products  1.96 us (1%)
    ppermute x11, starting transfers between devices, shift(): return lax.ppermute(value, axis, pairs)  44 us
    all_to_all x2, starting transfers between devices, spread_all(): lax.all_to_all(jnp.broadcast_to(value[None], (count,) + value.shape), axi...  21.1 us
    ppermute x11, waiting for transfers between devices, shift(): return lax.ppermute(value, axis, pairs)  16.8 us
    pallas_call x2, Pallas kernels, attend(): pl.pallas_call(attend_kernel, grid_spec=pltpu.PrefetchScalarGridSpec(num_...  9.39 us
    all_to_all x1, starting transfers between devices, per_device(): lax.all_to_all(gtxt.astype(bf16), 'plane', 0, 0).astype(f32)  8.39 us
    all_to_all x2, waiting for transfers between devices, spread_all(): lax.all_to_all(jnp.broadcast_to(value[None], (count,) + value.shape), axi...  8.19 us
    all_to_all x1, waiting for transfers between devices, per_device(): lax.all_to_all(send, 'mp', 0, 0).reshape(shards * local_heads, width + 128)  5.35 us
    all_to_all x1, starting transfers between devices, per_device(): lax.all_to_all(send, 'mp', 0, 0).reshape(shards * local_heads, width + 128)  3.29 us
  transfers between devices with their start and end apart: 15, of which 7 were waited for; matrix products, arithmetic and copies ran while one was open for 5% of the time, Pallas kernels for 3%

profile of v6, /device:TPU:1, one launch (start us, length us, event | category | flops | bytes accessed | tf_op | source)
XLA Modules:
  0.0 137.6 jit_solution(4290602449124979775)
XLA Ops:
  0.7 6.8 %collective-permute-start = (bf16[576,256]{1,0:T(8,128)(2,1)}, bf16[576,256]{1,0:T(8,128)(2,1)S(1)}, u32[]{:S(2)}, u32[]{:S(2)}) collective-permute-start(bf16[576,256]{1,0:T(8,128)(2,1)} %bitcast.50), channel_id=1, source_target_pairs={{0,1},{1,2},{2,3},{3,0},{4,5},{5,6},{6,7},{7,4},{8,9},{9,10},{10,1... | collective-permute-start | bytes 884744 | tf_op jit(solution)/shard_map/ppermute | solution.py:21
  7.4 6.8 %collective-permute-start.1 = (bf16[576,256]{1,0:T(8,128)(2,1)}, bf16[576,256]{1,0:T(8,128)(2,1)S(1)}, u32[]{:S(2)}, u32[]{:S(2)}) collective-permute-start(bf16[576,256]{1,0:T(8,128)(2,1)} %bitcast.51), channel_id=1, source_target_pairs={{0,3},{1,0},{2,1},{3,2},{4,7},{5,4},{6,5},{7,6},{8,11},{9,8},{10,9... | collective-permute-start | bytes 884744 | tf_op jit(solution)/shard_map/ppermute | solution.py:21
  15.7 9.8 %all-to-all-start = ((bf16[32,2,1152]{2,1,0:T(2,128)(2,1)}), bf16[32,2,1152]{2,1,0:T(2,128)(2,1)S(1)}, u32[]{:S(2)}, u32[]{:S(2)}) async-start(bf16[32,2,1152]{2,1,0:T(2,128)(2,1)} %broadcast_in_dim.30), calls=%async_computation | async-start | bytes 294912 | tf_op jit(solution)/shard_map/all_to_all | solution.py:15
  29.5 2.2 %collective-permute-start.2 = (bf16[288,256]{1,0:T(8,128)(2,1)S(1)}, bf16[288,256]{1,0:T(8,128)(2,1)S(1)}, u32[]{:S(2)}, u32[]{:S(2)}) collective-permute-start(bf16[288,256]{1,0:T(8,128)(2,1)S(1)} %slice.112), channel_id=1, source_target_pairs={{0,1},{1,2},{2,3},{3,0},{4,5},{5,6},{6,7},{7,4},{8,9},{9,10},{10,1... | collective-permute-start | bytes 442376 | tf_op jit(solution)/shard_map/ppermute | solution.py:21
  31.7 5.2 %collective-permute-start.3 = (bf16[288,256]{1,0:T(8,128)(2,1)S(1)}, bf16[288,256]{1,0:T(8,128)(2,1)S(1)}, u32[]{:S(2)}, u32[]{:S(2)}) collective-permute-start(bf16[288,256]{1,0:T(8,128)(2,1)S(1)} %slice.113), channel_id=1, source_target_pairs={{0,3},{1,0},{2,1},{3,2},{4,7},{5,4},{6,5},{7,6},{8,11},{9,8},{10,9... | collective-permute-start | bytes 442376 | tf_op jit(solution)/shard_map/ppermute | solution.py:21
  38.7 3.8 %collective-permute-done.3.far_b_ref = bf16[288,256]{1,0:T(8,128)(2,1)S(1)} collective-permute-done((bf16[288,256]{1,0:T(8,128)(2,1)S(1)}, bf16[288,256]{1,0:T(8,128)(2,1)S(1)}, u32[]{:S(2)}, u32[]{:S(2)}) %collective-permute-start.3) | collective-permute-done | bytes 147488 | tf_op jit(solution)/shard_map/ppermute | solution.py:21
  44.1 5.1 %attend.2 = (bf16[256,1152]{1,0:T(8,128)(2,1)S(1)}, f32[128,1152]{1,0:T(8,128)}) custom-call(s32[4]{0:T(128)S(1)} %add_add_fusion.1.scalar_ref, bf16[576,256]{1,0:T(8,128)(2,1)S(1)} %bitcast.52, bf16[576,256]{1,0:T(8,128)(2,1)S(1)} %collective-permute-done.left_ref, bf16[576,256]{1,0:T(8,128)(2,1)S(1)} %collective-permute-done.1.right_ref, ...), custom_call_target="tpu_custom_call" | custom-call | flops 6039797760 | bytes 5013504 | tf_op jit(solution)/shard_map/attend/pallas_call | solution.py:89
  49.4 4.1 %collective-permute-start.4 = (bf16[80,1152]{1,0:T(8,128)(2,1)S(1)}, bf16[80,1152]{1,0:T(8,128)(2,1)S(1)}, u32[]{:S(2)}, u32[]{:S(2)}) collective-permute-start(bf16[80,1152]{1,0:T(8,128)(2,1)S(1)} %get-tuple-element.40), channel_id=1, source_target_pairs={{0,1},{1,2},{2,3},{3,0},{4,5},{5,6},{6,7},{7,4},{8,9},{9,10},{10,1... | collective-permute-start | bytes 552968 | tf_op jit(solution)/shard_map/ppermute | solution.py:21
  53.5 3.4 %collective-permute-start.6 = (bf16[80,1152]{1,0:T(8,128)(2,1)S(1)}, bf16[80,1152]{1,0:T(8,128)(2,1)S(1)}, u32[]{:S(2)}, u32[]{:S(2)}) collective-permute-start(bf16[80,1152]{1,0:T(8,128)(2,1)S(1)} %get-tuple-element.39), channel_id=1, source_target_pairs={{0,3},{1,0},{2,1},{3,2},{4,7},{5,4},{6,5},{7,6},{8,11},{9,8},{10,9... | collective-permute-start | bytes 552968 | tf_op jit(solution)/shard_map/ppermute | solution.py:21
  57.0 2.5 %collective-permute-done.4 = bf16[80,1152]{1,0:T(8,128)(2,1)S(1)} collective-permute-done((bf16[80,1152]{1,0:T(8,128)(2,1)S(1)}, bf16[80,1152]{1,0:T(8,128)(2,1)S(1)}, u32[]{:S(2)}, u32[]{:S(2)}) %collective-permute-start.4) | collective-permute-done | bytes 184352 | tf_op jit(solution)/shard_map/ppermute | solution.py:21
  59.6 4.3 %attend.3 = (bf16[256,1152]{1,0:T(8,128)(2,1)S(1)}, f32[128,1152]{1,0:T(8,128)S(1)}) custom-call(s32[4]{0:T(128)S(1)} %add_add_fusion.2.scalar_ref, bf16[576,256]{1,0:T(8,128)(2,1)S(1)} %bitcast.53, bf16[576,256]{1,0:T(8,128)(2,1)S(1)} %collective-permute-done.left_ref, bf16[576,256]{1,0:T(8,128)(2,1)S(1)} %collective-permute-done.1.right_ref, ...), custom_call_target="tpu_custom_call" | custom-call | flops 6039797760 | bytes 5013504 | tf_op jit(solution)/shard_map/attend/pallas_call | solution.py:89
  64.0 2.5 %collective-permute-start.5 = (bf16[144,1152]{1,0:T(8,128)(2,1)S(1)}, bf16[144,1152]{1,0:T(8,128)(2,1)S(1)}, u32[]{:S(2)}, u32[]{:S(2)}) collective-permute-start(bf16[144,1152]{1,0:T(8,128)(2,1)S(1)} %pad_maximum_fusion), channel_id=1, source_target_pairs={{0,1},{1,2},{2,3},{3,0},{4,5},{5,6},{6,7},{7,4},{8,9},{9,10},{10,1... | collective-permute-start | bytes 995336 | tf_op jit(solution)/shard_map/ppermute | solution.py:21
  66.7 5.0 %collective-permute-start.7 = (bf16[128,1152]{1,0:T(8,128)(2,1)S(1)}, bf16[128,1152]{1,0:T(8,128)(2,1)S(1)}, u32[]{:S(2)}, u32[]{:S(2)}) collective-permute-start(bf16[128,1152]{1,0:T(8,128)(2,1)S(1)} %pad_maximum_fusion.1), channel_id=1, source_target_pairs={{0,3},{1,0},{2,1},{3,2},{4,7},{5,4},{6,5},{7,6},{8,11},{9,8},{10,9... | collective-permute-start | bytes 884744 | tf_op jit(solution)/shard_map/ppermute | solution.py:21
  71.8 6.7 %collective-permute-done.7.before_ref = bf16[128,1152]{1,0:T(8,128)(2,1)S(1)} collective-permute-done((bf16[128,1152]{1,0:T(8,128)(2,1)S(1)}, bf16[128,1152]{1,0:T(8,128)(2,1)S(1)}, u32[]{:S(2)}, u32[]{:S(2)}) %collective-permute-start.7) | collective-permute-done | bytes 294944 | tf_op jit(solution)/shard_map/ppermute | solution.py:21
  78.6 3.7 %collective-permute-done.5.after_ref = bf16[144,1152]{1,0:T(8,128)(2,1)S(1)} collective-permute-done((bf16[144,1152]{1,0:T(8,128)(2,1)S(1)}, bf16[144,1152]{1,0:T(8,128)(2,1)S(1)}, u32[]{:S(2)}, u32[]{:S(2)}) %collective-permute-start.5) | collective-permute-done | bytes 331808 | tf_op jit(solution)/shard_map/ppermute | solution.py:21
  82.3 2.1 %mix_rows.1 = f32[4,4,1280]{2,1,0:T(4,128)} custom-call(s32[3]{0:T(128)S(1)} %pad_add_fusion.scalar_ref, f32[128,1152]{1,0:T(8,128)S(1)} %get-tuple-element.16.base_ref, bf16[144,1152]{1,0:T(8,128)(2,1)S(1)} %collective-permute-done.5.after_ref, bf16[128,1152]{1,0:T(8,128)(2,1)S(1)} %collective-permute-done.7.before_ref, ...), custom_call_target="tpu_custom_call" | custom-call | tf_op jit(solution)/shard_map/mix_rows/pallas_call | solution.py:146
  84.4 3.3 %all-to-all-start.1 = ((f32[4,4,1280]{2,1,0:T(4,128)}), f32[4,4,1280]{2,1,0:T(4,128)S(1)}, u32[]{:S(2)}, u32[]{:S(2)}) async-start(f32[4,4,1280]{2,1,0:T(4,128)} %mix_rows.1), calls=%async_computation.1 | async-start | bytes 163840 | tf_op jit(solution)/shard_map/all_to_all | solution.py:286
  89.3 5.4 %all-to-all-done.1 = f32[4,4,1280]{2,1,0:T(4,128)S(1)} async-done(((f32[4,4,1280]{2,1,0:T(4,128)}), f32[4,4,1280]{2,1,0:T(4,128)S(1)}, u32[]{:S(2)}, u32[]{:S(2)}) %all-to-all-start.1) | async-done | bytes 81952 | tf_op jit(solution)/shard_map/all_to_all | solution.py:286
  96.2 11.3 %all-to-all-start.2 = ((bf16[16,2,1280]{2,1,0:T(2,128)(2,1)}), bf16[16,2,1280]{2,1,0:T(2,128)(2,1)S(1)}, u32[]{:S(2)}, u32[]{:S(2)}) async-start(bf16[16,2,1280]{2,1,0:T(2,128)(2,1)} %broadcast_in_dim.66), calls=%async_computation.2 | async-start | bytes 163840 | tf_op jit(solution)/shard_map/all_to_all | solution.py:15
  107.5 8.2 %all-to-all-done.2 = bf16[16,2,1280]{2,1,0:T(2,128)(2,1)S(1)} async-done(((bf16[16,2,1280]{2,1,0:T(2,128)(2,1)}), bf16[16,2,1280]{2,1,0:T(2,128)(2,1)S(1)}, u32[]{:S(2)}, u32[]{:S(2)}) %all-to-all-start.2) | async-done | bytes 81952 | tf_op jit(solution)/shard_map/all_to_all | solution.py:15
  118.2 8.4 %all-to-all-start.3 = ((bf16[32,2,1152]{2,1,0:T(2,128)(2,1)}), bf16[32,2,1152]{2,1,0:T(2,128)(2,1)S(1)}, u32[]{:S(2)}, u32[]{:S(2)}) async-start(bf16[32,2,1152]{2,1,0:T(2,128)(2,1)} %copy.29), calls=%async_computation.3 | async-start | bytes 294912 | tf_op jit(solution)/shard_map/all_to_all | solution.py:312
  126.6 2.4 %collective-permute-start.10 = (f32[2,1152]{1,0:T(2,128)S(1)}, f32[2,1152]{1,0:T(2,128)S(1)}, u32[]{:S(2)}, u32[]{:S(2)}) collective-permute-start(f32[2,1152]{1,0:T(2,128)S(1)} %get-tuple-element.36), channel_id=1, source_target_pairs={{0,12},{4,0},{8,4},{12,8},{1,13},{5,1},{9,5},{13,9},{2,14},{6,2},{... | collective-permute-start | bytes 27656 | tf_op jit(solution)/shard_map/ppermute | solution.py:21
  129.0 2.3 %collective-permute-start.9 = (f32[2,1152]{1,0:T(2,128)S(1)}, f32[2,1152]{1,0:T(2,128)S(1)}, u32[]{:S(2)}, u32[]{:S(2)}) collective-permute-start(f32[2,1152]{1,0:T(2,128)S(1)} %get-tuple-element.37), channel_id=1, source_target_pairs={{0,8},{4,12},{8,0},{12,4},{1,9},{5,13},{9,1},{13,5},{2,10},{6,14},... | collective-permute-start | bytes 27656 | tf_op jit(solution)/shard_map/ppermute | solution.py:21
  131.3 3.4 %collective-permute-start.8 = (f32[2,1152]{1,0:T(2,128)S(1)}, f32[2,1152]{1,0:T(2,128)S(1)}, u32[]{:S(2)}, u32[]{:S(2)}) collective-permute-start(f32[2,1152]{1,0:T(2,128)S(1)} %get-tuple-element.35), channel_id=1, source_target_pairs={{0,4},{4,8},{8,12},{12,0},{1,5},{5,9},{9,13},{13,1},{2,6},{6,10},{... | collective-permute-start | bytes 27656 | tf_op jit(solution)/shard_map/ppermute | solution.py:21
  (96 shorter events, 13.9 us)
Async XLA Ops:
  0.6 37.9 %copy-start.6 = (bf16[2,1152]{1,0:T(2,128)(2,1)S(1)}, bf16[2,1152]{1,0:T(2,128)(2,1)}, u32[]{:S(2)}) copy-start(bf16[2,1152]{1,0:T(2,128)(2,1)} %param.22) | copy-start | bytes 13828
  0.6 37.6 %copy-start.7 = (f32[1152]{0:T(1024)S(1)}, f32[1152]{0:T(1024)}, u32[]{:S(2)}) copy-start(f32[1152]{0:T(1024)} %param.15) | copy-start | bytes 13828
  0.7 37.9 %copy-start.8 = (f32[1152]{0:T(1024)S(1)}, f32[1152]{0:T(1024)}, u32[]{:S(2)}) copy-start(f32[1152]{0:T(1024)} %param.18) | copy-start | bytes 13828
  0.7 28.8 %collective-permute-start = (bf16[576,256]{1,0:T(8,128)(2,1)}, bf16[576,256]{1,0:T(8,128)(2,1)S(1)}, u32[]{:S(2)}, u32[]{:S(2)}) collective-permute-start(bf16[576,256]{1,0:T(8,128)(2,1)} %bitcast.50), channel_id=1, source_target_pairs={{0,1},{1,2},{2,3},{3,0},{4,5},{5,6},{6,7},{7,4},{8,9},{9,10},{10,1... | collective-permute-start | bytes 884744 | tf_op jit(solution)/shard_map/ppermute | solution.py:21
  7.4 24.2 %collective-permute-start.1 = (bf16[576,256]{1,0:T(8,128)(2,1)}, bf16[576,256]{1,0:T(8,128)(2,1)S(1)}, u32[]{:S(2)}, u32[]{:S(2)}) collective-permute-start(bf16[576,256]{1,0:T(8,128)(2,1)} %bitcast.51), channel_id=1, source_target_pairs={{0,3},{1,0},{2,1},{3,2},{4,7},{5,4},{6,5},{7,6},{8,11},{9,8},{10,9... | collective-permute-start | bytes 884744 | tf_op jit(solution)/shard_map/ppermute | solution.py:21
  15.7 26.9 %copy-start.4 = (bf16[288,1152]{1,0:T(8,128)(2,1)S(1)}, bf16[288,1152]{1,0:T(8,128)(2,1)}, u32[]{:S(2)}) copy-start(bf16[288,1152]{1,0:T(8,128)(2,1)} %out_w_ref.4) | copy-start | bytes 1990660
  15.7 26.9 %copy-start.5 = (bf16[2,256,288]{1,2,0:T(8,128)(2,1)S(1)}, bf16[2,256,288]{1,2,0:T(8,128)(2,1)}, u32[]{:S(2)}) copy-start(bf16[2,256,288]{1,2,0:T(8,128)(2,1)} %param.13) | copy-start | bytes 884740
  15.7 23.0 %all-to-all-start = ((bf16[32,2,1152]{2,1,0:T(2,128)(2,1)}), bf16[32,2,1152]{2,1,0:T(2,128)(2,1)S(1)}, u32[]{:S(2)}, u32[]{:S(2)}) async-start(bf16[32,2,1152]{2,1,0:T(2,128)(2,1)} %broadcast_in_dim.30), calls=%async_computation | async-start | bytes 294912 | tf_op jit(solution)/shard_map/all_to_all | solution.py:15
  29.5 9.2 %collective-permute-start.2 = (bf16[288,256]{1,0:T(8,128)(2,1)S(1)}, bf16[288,256]{1,0:T(8,128)(2,1)S(1)}, u32[]{:S(2)}, u32[]{:S(2)}) collective-permute-start(bf16[288,256]{1,0:T(8,128)(2,1)S(1)} %slice.112), channel_id=1, source_target_pairs={{0,1},{1,2},{2,3},{3,0},{4,5},{5,6},{6,7},{7,4},{8,9},{9,10},{10,1... | collective-permute-start | bytes 442376 | tf_op jit(solution)/shard_map/ppermute | solution.py:21
  31.7 10.9 %collective-permute-start.3 = (bf16[288,256]{1,0:T(8,128)(2,1)S(1)}, bf16[288,256]{1,0:T(8,128)(2,1)S(1)}, u32[]{:S(2)}, u32[]{:S(2)}) collective-permute-start(bf16[288,256]{1,0:T(8,128)(2,1)S(1)} %slice.113), channel_id=1, source_target_pairs={{0,3},{1,0},{2,1},{3,2},{4,7},{5,4},{6,5},{7,6},{8,11},{9,8},{10,9... | collective-permute-start | bytes 442376 | tf_op jit(solution)/shard_map/ppermute | solution.py:21
  49.2 10.3 %copy-start.3 = (bf16[3,1152,288]{1,2,0:T(8,128)(2,1)S(1)}, bf16[3,1152,288]{1,2,0:T(8,128)(2,1)}, u32[]{:S(2)}) copy-start(bf16[3,1152,288]{1,2,0:T(8,128)(2,1)} %param.16) | copy-start | bytes 5971972
  49.4 10.1 %collective-permute-start.4 = (bf16[80,1152]{1,0:T(8,128)(2,1)S(1)}, bf16[80,1152]{1,0:T(8,128)(2,1)S(1)}, u32[]{:S(2)}, u32[]{:S(2)}) collective-permute-start(bf16[80,1152]{1,0:T(8,128)(2,1)S(1)} %get-tuple-element.40), channel_id=1, source_target_pairs={{0,1},{1,2},{2,3},{3,0},{4,5},{5,6},{6,7},{7,4},{8,9},{9,10},{10,1... | collective-permute-start | bytes 552968 | tf_op jit(solution)/shard_map/ppermute | solution.py:21
  53.5 13.1 %collective-permute-start.6 = (bf16[80,1152]{1,0:T(8,128)(2,1)S(1)}, bf16[80,1152]{1,0:T(8,128)(2,1)S(1)}, u32[]{:S(2)}, u32[]{:S(2)}) collective-permute-start(bf16[80,1152]{1,0:T(8,128)(2,1)S(1)} %get-tuple-element.39), channel_id=1, source_target_pairs={{0,3},{1,0},{2,1},{3,2},{4,7},{5,4},{6,5},{7,6},{8,11},{9,8},{10,9... | collective-permute-start | bytes 552968 | tf_op jit(solution)/shard_map/ppermute | solution.py:21
  64.0 18.2 %collective-permute-start.5 = (bf16[144,1152]{1,0:T(8,128)(2,1)S(1)}, bf16[144,1152]{1,0:T(8,128)(2,1)S(1)}, u32[]{:S(2)}, u32[]{:S(2)}) collective-permute-start(bf16[144,1152]{1,0:T(8,128)(2,1)S(1)} %pad_maximum_fusion), channel_id=1, source_target_pairs={{0,1},{1,2},{2,3},{3,0},{4,5},{5,6},{6,7},{7,4},{8,9},{9,10},{10,1... | collective-permute-start | bytes 995336 | tf_op jit(solution)/shard_map/ppermute | solution.py:21
  66.6 21.1 %copy-start.9 = (s32[2]{0:T(128)S(1)}, s32[2]{0:T(128)}, u32[]{:S(2)}) copy-start(s32[2]{0:T(128)} %param.23) | copy-start | bytes 28
  66.7 28.0 %copy-start = (bf16[2,1152,288]{1,2,0:T(8,128)(2,1)S(1)}, bf16[2,1152,288]{1,2,0:T(8,128)(2,1)}, u32[]{:S(2)}) copy-start(bf16[2,1152,288]{1,2,0:T(8,128)(2,1)} %param.19) | copy-start | bytes 3981316
  66.7 28.0 %copy-start.1 = (bf16[288,1152]{1,0:T(8,128)(2,1)S(1)}, bf16[288,1152]{1,0:T(8,128)(2,1)}, u32[]{:S(2)}) copy-start(bf16[288,1152]{1,0:T(8,128)(2,1)} %out_w_ref.5) | copy-start | bytes 1990660
  66.7 11.9 %collective-permute-start.7 = (bf16[128,1152]{1,0:T(8,128)(2,1)S(1)}, bf16[128,1152]{1,0:T(8,128)(2,1)S(1)}, u32[]{:S(2)}, u32[]{:S(2)}) collective-permute-start(bf16[128,1152]{1,0:T(8,128)(2,1)S(1)} %pad_maximum_fusion.1), channel_id=1, source_target_pairs={{0,3},{1,0},{2,1},{3,2},{4,7},{5,4},{6,5},{7,6},{8,11},{9,8},{10,9... | collective-permute-start | bytes 884744 | tf_op jit(solution)/shard_map/ppermute | solution.py:21
  84.4 10.3 %all-to-all-start.1 = ((f32[4,4,1280]{2,1,0:T(4,128)}), f32[4,4,1280]{2,1,0:T(4,128)S(1)}, u32[]{:S(2)}, u32[]{:S(2)}) async-start(f32[4,4,1280]{2,1,0:T(4,128)} %mix_rows.1), calls=%async_computation.1 | async-start | bytes 163840 | tf_op jit(solution)/shard_map/all_to_all | solution.py:286
  96.2 19.5 %all-to-all-start.2 = ((bf16[16,2,1280]{2,1,0:T(2,128)(2,1)}), bf16[16,2,1280]{2,1,0:T(2,128)(2,1)S(1)}, u32[]{:S(2)}, u32[]{:S(2)}) async-start(bf16[16,2,1280]{2,1,0:T(2,128)(2,1)} %broadcast_in_dim.66), calls=%async_computation.2 | async-start | bytes 163840 | tf_op jit(solution)/shard_map/all_to_all | solution.py:15
  118.2 17.6 %all-to-all-start.3 = ((bf16[32,2,1152]{2,1,0:T(2,128)(2,1)}), bf16[32,2,1152]{2,1,0:T(2,128)(2,1)S(1)}, u32[]{:S(2)}, u32[]{:S(2)}) async-start(bf16[32,2,1152]{2,1,0:T(2,128)(2,1)} %copy.29), calls=%async_computation.3 | async-start | bytes 294912 | tf_op jit(solution)/shard_map/all_to_all | solution.py:312
  126.6 10.2 %collective-permute-start.10 = (f32[2,1152]{1,0:T(2,128)S(1)}, f32[2,1152]{1,0:T(2,128)S(1)}, u32[]{:S(2)}, u32[]{:S(2)}) collective-permute-start(f32[2,1152]{1,0:T(2,128)S(1)} %get-tuple-element.36), channel_id=1, source_target_pairs={{0,12},{4,0},{8,4},{12,8},{1,13},{5,1},{9,5},{13,9},{2,14},{6,2},{... | collective-permute-start | bytes 27656 | tf_op jit(solution)/shard_map/ppermute | solution.py:21
  129.0 7.8 %collective-permute-start.9 = (f32[2,1152]{1,0:T(2,128)S(1)}, f32[2,1152]{1,0:T(2,128)S(1)}, u32[]{:S(2)}, u32[]{:S(2)}) collective-permute-start(f32[2,1152]{1,0:T(2,128)S(1)} %get-tuple-element.37), channel_id=1, source_target_pairs={{0,8},{4,12},{8,0},{12,4},{1,9},{5,13},{9,1},{13,5},{2,10},{6,14},... | collective-permute-start | bytes 27656 | tf_op jit(solution)/shard_map/ppermute | solution.py:21
  131.3 5.5 %collective-permute-start.8 = (f32[2,1152]{1,0:T(2,128)S(1)}, f32[2,1152]{1,0:T(2,128)S(1)}, u32[]{:S(2)}, u32[]{:S(2)}) collective-permute-start(f32[2,1152]{1,0:T(2,128)S(1)} %get-tuple-element.35), channel_id=1, source_target_pairs={{0,4},{4,8},{8,12},{12,0},{1,5},{5,9},{9,13},{13,1},{2,6},{6,10},{... | collective-permute-start | bytes 27656 | tf_op jit(solution)/shard_map/ppermute | solution.py:21
  (1 other events, 1.6 us)

commit v7 on v6

--- a/solution.py
+++ b/solution.py
@@ -44,15 +44,14 @@
 NT = (((1,), (1,)), ((), ()))
 
 
-def attend_kernel(scalar_ref, own_ref, left_ref, right_ref, far_a_ref, far_b_ref, w_ref, out_w_ref, gain_ref,
+def attend_kernel(scalar_ref, own_ref, left_ref, right_ref, far_ref, w_ref, out_w_ref, gain_ref,
                   o_ref, base_ref, x_ref, norm_ref, ctx_ref):
     f32, bf16 = jnp.float32, jnp.bfloat16
     width, pmax = x_ref.shape
     dlocal = out_w_ref.shape[0]
     shards = width // dlocal
-    me, image, count = scalar_ref[0], scalar_ref[1], scalar_ref[2]
-    far = jnp.where(image == 0, far_a_ref[...].astype(f32), far_b_ref[...].astype(f32))
-    slices = [ref[...].astype(f32) for ref in (own_ref, left_ref, right_ref)] + [far]
+    me, count = scalar_ref[0], scalar_ref[2]
+    slices = [ref[...].astype(f32) for ref in (own_ref, left_ref, right_ref, far_ref)]
     mean = sum(jnp.sum(part, axis=0, keepdims=True) for part in slices) * (1.0 / width)
     centers = [part - mean for part in slices]
     spread = sum(jnp.sum(part * part, axis=0, keepdims=True) for part in centers) * (1.0 / width)
@@ -92,7 +91,7 @@
             num_scalar_prefetch=1,
             grid=(1,),
             in_specs=[of_image] * 3
-            + [whole(dlocal, pmax)] * 2
+            + [whole(dlocal, pmax)]
             + [whole(3 * dlocal, width), whole(dlocal, width), whole(width, 1)],
             out_specs=[whole(pmax, width), whole(pmax // 2, width)],
             scratch_shapes=[
@@ -251,16 +250,18 @@
     own_x = patches.transpose(0, 2, 1).reshape(rows_img * dlocal, pmax)
     left_x, right_x = shift(own_x, 1), shift(own_x, -1)
     texts = spread_all(text_emb, "plane").reshape(-1, width)
-    far_a, far_b = shift(left_x[:dlocal], 1), shift(right_x[dlocal:], -1)
-    texts, far_a, far_b = lax.optimization_barrier((texts, far_a, far_b))
+    next_first, before_last = 1 - ((me + 1) % shards) // 2, ((me - 1) % shards) // 2
+    far_first = shift(lax.dynamic_slice(left_x, (next_first * dlocal, 0), (dlocal, pmax)), 1)
+    far_last = shift(lax.dynamic_slice(right_x, (before_last * dlocal, 0), (dlocal, pmax)), -1)
+    texts, far_last = lax.optimization_barrier((texts, far_last))
 
     my_image, my_half = me // 2, me % 2
     w_rows = w_qkv.transpose(0, 2, 1).reshape(3 * dlocal, width)
     gain = ln1_gain[:, None]
     my_count = jnp.where(my_image == 0, patch_count[0], patch_count[1])
     other_count = jnp.where(my_image == 0, patch_count[1], patch_count[0])
-    slices = (own_x, left_x, right_x, far_a, far_b)
-    first, _ = attend((me, 1 - my_image, other_count, my_half), slices, w_rows, w_out, gain)
+    slices = (own_x, left_x, right_x)
+    first, _ = attend((me, 1 - my_image, other_count, my_half), slices + (far_first,), w_rows, w_out, gain)
     quarter = half // 2
     even = my_half == 0
     far = jnp.where(even, first[:half], first[half:])
@@ -268,7 +269,7 @@
     far_after = shift(jnp.concatenate([far[:quarter], tail], axis=0), 1)
     far_before = shift(jnp.concatenate([far[quarter:], tail], axis=0), -1)
     my_count, far_after = lax.optimization_barrier((my_count, far_after))
-    second, base = attend((me, my_image, my_count, my_half), slices, w_rows, w_out, gain)
+    second, base = attend((me, my_image, my_count, my_half), slices + (far_last,), w_rows, w_out, gain)
     left_keys, right_keys = far_after[quarter:], far_before[quarter:]
     far_after, far_before = far_after[:quarter], far_before[:quarter]
     after = jnp.where(even, second[half:], first[:half])

time: 139 us -> 138 us (level)
  waiting for transfers between devices: 31.5 us -> 19.5 us
  starting transfers between devices: 76.8 us -> 84.5 us
  other arithmetic: 3.39 us -> 5.31 us
  local copies, waits for them, and re-layouts: 6.74 us -> 8.3 us
    ppermute x11, waiting for transfers between devices: 16.8 us -> 4.61 us  [shift(): return lax.ppermute(value, axis, pairs)]
    all_to_all x2, starting transfers between devices: 21.1 us -> 27.5 us  [spread_all(): lax.all_to_all(jnp.broadcast_to(value[None], (count,) + value.shape), axi...]
    all_to_all x1, starting transfers between devices: 3.29 us -> 4.93 us  [per_device(): lax.all_to_all(send, 'mp', 0, 0).reshape(shards * local_heads, width + 128)]
    unnamed x20 -> x24, local copies, waits for them, and re-layouts: 1.6 us -> 3.16 us
  transfers between devices with their start and end apart: 15 -> 15, of which waited for: 7 -> 5; matrix products, arithmetic and copies ran while one was open for 5% -> 6% of each run, Pallas kernels for 3% -> 7%
where the time goes in v7:
time: 138 us; the launch traced here: 137 us
  starting transfers between devices  84.5 us (61%)
  waiting for transfers between devices  19.5 us (14%)
  Pallas kernels  12.1 us (9%)
  local copies, waits for them, and re-layouts  8.3 us (6%)
  other arithmetic  5.31 us (4%)
  between operations  5.14 us (4%)
  matrix products  1.95 us (1%)
    ppermute x11, starting transfers between devices, shift(): return lax.ppermute(value, axis, pairs)  43.9 us
    all_to_all x2, starting transfers between devices, spread_all(): lax.all_to_all(jnp.broadcast_to(value[None], (count,) + value.shape), axi...  27.5 us
    pallas_call x2, Pallas kernels, attend(): pl.pallas_call(attend_kernel, grid_spec=pltpu.PrefetchScalarGridSpec(num_...  9.37 us
    all_to_all x2, waiting for transfers between devices, spread_all(): lax.all_to_all(jnp.broadcast_to(value[None], (count,) + value.shape), axi...  8.19 us
    all_to_all x1, starting transfers between devices, per_device(): lax.all_to_all(gtxt.astype(bf16), 'plane', 0, 0).astype(f32)  8.13 us
    all_to_all x1, waiting for transfers between devices, per_device(): lax.all_to_all(send, 'mp', 0, 0).reshape(shards * local_heads, width + 128)  5.58 us
    all_to_all x1, starting transfers between devices, per_device(): lax.all_to_all(send, 'mp', 0, 0).reshape(shards * local_heads, width + 128)  4.93 us
    ppermute x11, waiting for transfers between devices, shift(): return lax.ppermute(value, axis, pairs)  4.61 us
  transfers between devices with their start and end apart: 15, of which 5 were waited for; matrix products, arithmetic and copies ran while one was open for 6% of the time, Pallas kernels for 7%

profile of v7, /device:TPU:1, one launch (start us, length us, event | category | flops | bytes accessed | tf_op | source)
XLA Modules:
  0.0 136.8 jit_solution(11829699043813887197)
XLA Ops:
  0.7 6.8 %collective-permute-start = (bf16[576,256]{1,0:T(8,128)(2,1)}, bf16[576,256]{1,0:T(8,128)(2,1)S(1)}, u32[]{:S(2)}, u32[]{:S(2)}) collective-permute-start(bf16[576,256]{1,0:T(8,128)(2,1)} %bitcast.50), channel_id=1, source_target_pairs={{0,1},{1,2},{2,3},{3,0},{4,5},{5,6},{6,7},{7,4},{8,9},{9,10},{10,1... | collective-permute-start | bytes 884744 | tf_op jit(solution)/shard_map/ppermute | solution.py:21
  7.4 6.8 %collective-permute-start.1 = (bf16[576,256]{1,0:T(8,128)(2,1)}, bf16[576,256]{1,0:T(8,128)(2,1)S(1)}, u32[]{:S(2)}, u32[]{:S(2)}) collective-permute-start(bf16[576,256]{1,0:T(8,128)(2,1)} %bitcast.51), channel_id=1, source_target_pairs={{0,3},{1,0},{2,1},{3,2},{4,7},{5,4},{6,5},{7,6},{8,11},{9,8},{10,9... | collective-permute-start | bytes 884744 | tf_op jit(solution)/shard_map/ppermute | solution.py:21
  14.2 1.4 %broadcast_in_dim.36 = bf16[32,2,1152]{2,1,0:T(2,128)(2,1)} broadcast(bf16[2,1152]{1,0:T(2,128)(2,1)} %param.22), dimensions={1,2} | broadcast | bytes 152064 | tf_op jit(solution)/shard_map/broadcast_in_dim | solution.py:15
  15.6 9.7 %all-to-all-start = ((bf16[32,2,1152]{2,1,0:T(2,128)(2,1)}), bf16[32,2,1152]{2,1,0:T(2,128)(2,1)S(1)}, u32[]{:S(2)}, u32[]{:S(2)}) async-start(bf16[32,2,1152]{2,1,0:T(2,128)(2,1)} %broadcast_in_dim.36), calls=%async_computation | async-start | bytes 294912 | tf_op jit(solution)/shard_map/all_to_all | solution.py:15
  29.4 2.2 %collective-permute-start.2 = (bf16[288,256]{1,0:T(8,128)(2,1)S(1)}, bf16[288,256]{1,0:T(8,128)(2,1)S(1)}, u32[]{:S(2)}, u32[]{:S(2)}) collective-permute-start(bf16[288,256]{1,0:T(8,128)(2,1)S(1)} %constant_dynamic-slice_fusion.2), channel_id=1, source_target_pairs={{0,1},{1,2},{2,3},{3,0},{4,5},{5,6},{6,7},{7,4},{8,9},{9,10},{10,1... | collective-permute-start | bytes 442376 | tf_op jit(solution)/shard_map/ppermute | solution.py:21
  31.9 5.2 %collective-permute-start.4 = (bf16[288,256]{1,0:T(8,128)(2,1)S(1)}, bf16[288,256]{1,0:T(8,128)(2,1)S(1)}, u32[]{:S(2)}, u32[]{:S(2)}) collective-permute-start(bf16[288,256]{1,0:T(8,128)(2,1)S(1)} %constant_dynamic-slice_fusion.1), channel_id=1, source_target_pairs={{0,3},{1,0},{2,1},{3,2},{4,7},{5,4},{6,5},{7,6},{8,11},{9,8},{10,9... | collective-permute-start | bytes 442376 | tf_op jit(solution)/shard_map/ppermute | solution.py:21
  37.5 1.6 %copy-done.2 = bf16[3,1152,288]{1,2,0:T(8,128)(2,1)S(1)} copy-done((bf16[3,1152,288]{1,2,0:T(8,128)(2,1)S(1)}, bf16[3,1152,288]{1,2,0:T(8,128)(2,1)}, u32[]{:S(2)}) %copy-start.2) | copy-done | bytes 1990680
  39.1 5.1 %attend.2 = (bf16[256,1152]{1,0:T(8,128)(2,1)S(1)}, f32[128,1152]{1,0:T(8,128)}) custom-call(s32[4]{0:T(128)S(1)} %add_add_fusion.1.scalar_ref, bf16[576,256]{1,0:T(8,128)(2,1)S(1)} %bitcast.52, bf16[576,256]{1,0:T(8,128)(2,1)S(1)} %collective-permute-done.left_ref, bf16[576,256]{1,0:T(8,128)(2,1)S(1)} %collective-permute-done.1.right_ref, ...), custom_call_target="tpu_custom_call" | custom-call | flops 6039797760 | bytes 5013504 | tf_op jit(solution)/shard_map/attend/pallas_call | solution.py:88
  45.0 1.9 %collective-permute-start.3 = (bf16[80,1152]{1,0:T(8,128)(2,1)}, bf16[80,1152]{1,0:T(8,128)(2,1)S(1)}, u32[]{:S(2)}, u32[]{:S(2)}) collective-permute-start(bf16[80,1152]{1,0:T(8,128)(2,1)} %get-tuple-element.38), channel_id=1, source_target_pairs={{0,1},{1,2},{2,3},{3,0},{4,5},{5,6},{6,7},{7,4},{8,9},{9,10},{10,1... | collective-permute-start | bytes 552968 | tf_op jit(solution)/shard_map/ppermute | solution.py:21
  49.7 5.5 %collective-permute-start.6 = (bf16[80,1152]{1,0:T(8,128)(2,1)}, bf16[80,1152]{1,0:T(8,128)(2,1)S(1)}, u32[]{:S(2)}, u32[]{:S(2)}) collective-permute-start(bf16[80,1152]{1,0:T(8,128)(2,1)} %get-tuple-element.37), channel_id=1, source_target_pairs={{0,3},{1,0},{2,1},{3,2},{4,7},{5,4},{6,5},{7,6},{8,11},{9,8},{10,9... | collective-permute-start | bytes 552968 | tf_op jit(solution)/shard_map/ppermute | solution.py:21
  55.3 1.6 %copy-done.3 = bf16[3,1152,288]{1,2,0:T(8,128)(2,1)S(1)} copy-done((bf16[3,1152,288]{1,2,0:T(8,128)(2,1)S(1)}, bf16[3,1152,288]{1,2,0:T(8,128)(2,1)}, u32[]{:S(2)}) %copy-start.3) | copy-done | bytes 1990680
  56.8 4.3 %attend.3 = (bf16[256,1152]{1,0:T(8,128)(2,1)S(1)}, f32[128,1152]{1,0:T(8,128)S(1)}) custom-call(s32[4]{0:T(128)S(1)} %add_add_fusion.2.scalar_ref, bf16[576,256]{1,0:T(8,128)(2,1)S(1)} %bitcast.53, bf16[576,256]{1,0:T(8,128)(2,1)S(1)} %collective-permute-done.left_ref, bf16[576,256]{1,0:T(8,128)(2,1)S(1)} %collective-permute-done.1.right_ref, ...), custom_call_target="tpu_custom_call" | custom-call | flops 6039797760 | bytes 5013504 | tf_op jit(solution)/shard_map/attend/pallas_call | solution.py:88
  61.3 2.2 %collective-permute-start.5 = (bf16[144,1152]{1,0:T(8,128)(2,1)S(1)}, bf16[144,1152]{1,0:T(8,128)(2,1)S(1)}, u32[]{:S(2)}, u32[]{:S(2)}) collective-permute-start(bf16[144,1152]{1,0:T(8,128)(2,1)S(1)} %pad_maximum_fusion), channel_id=1, source_target_pairs={{0,1},{1,2},{2,3},{3,0},{4,5},{5,6},{6,7},{7,4},{8,9},{9,10},{10,1... | collective-permute-start | bytes 995336 | tf_op jit(solution)/shard_map/ppermute | solution.py:21
  63.6 5.3 %collective-permute-start.7 = (bf16[128,1152]{1,0:T(8,128)(2,1)S(1)}, bf16[128,1152]{1,0:T(8,128)(2,1)S(1)}, u32[]{:S(2)}, u32[]{:S(2)}) collective-permute-start(bf16[128,1152]{1,0:T(8,128)(2,1)S(1)} %pad_maximum_fusion.1), channel_id=1, source_target_pairs={{0,3},{1,0},{2,1},{3,2},{4,7},{5,4},{6,5},{7,6},{8,11},{9,8},{10,9... | collective-permute-start | bytes 884744 | tf_op jit(solution)/shard_map/ppermute | solution.py:21
  69.1 4.2 %collective-permute-done.7.before_ref = bf16[128,1152]{1,0:T(8,128)(2,1)S(1)} collective-permute-done((bf16[128,1152]{1,0:T(8,128)(2,1)S(1)}, bf16[128,1152]{1,0:T(8,128)(2,1)S(1)}, u32[]{:S(2)}, u32[]{:S(2)}) %collective-permute-start.7) | collective-permute-done | bytes 294944 | tf_op jit(solution)/shard_map/ppermute | solution.py:21
  73.4 2.1 %mix_rows.1 = f32[4,4,1280]{2,1,0:T(4,128)} custom-call(s32[3]{0:T(128)S(1)} %pad_add_fusion.scalar_ref, f32[128,1152]{1,0:T(8,128)S(1)} %get-tuple-element.14.base_ref, bf16[144,1152]{1,0:T(8,128)(2,1)S(1)} %collective-permute-done.5.after_ref, bf16[128,1152]{1,0:T(8,128)(2,1)S(1)} %collective-permute-done.7.before_ref, ...), custom_call_target="tpu_custom_call" | custom-call | tf_op jit(solution)/shard_map/mix_rows/pallas_call | solution.py:145
  75.4 4.9 %all-to-all-start.1 = ((f32[4,4,1280]{2,1,0:T(4,128)}), f32[4,4,1280]{2,1,0:T(4,128)S(1)}, u32[]{:S(2)}, u32[]{:S(2)}) async-start(f32[4,4,1280]{2,1,0:T(4,128)} %mix_rows.1), calls=%async_computation.1 | async-start | bytes 163840 | tf_op jit(solution)/shard_map/all_to_all | solution.py:287
  82.0 5.6 %all-to-all-done.1 = f32[4,4,1280]{2,1,0:T(4,128)S(1)} async-done(((f32[4,4,1280]{2,1,0:T(4,128)}), f32[4,4,1280]{2,1,0:T(4,128)S(1)}, u32[]{:S(2)}, u32[]{:S(2)}) %all-to-all-start.1) | async-done | bytes 81952 | tf_op jit(solution)/shard_map/all_to_all | solution.py:287
  89.1 17.9 %all-to-all-start.2 = ((bf16[16,2,1280]{2,1,0:T(2,128)(2,1)}), bf16[16,2,1280]{2,1,0:T(2,128)(2,1)S(1)}, u32[]{:S(2)}, u32[]{:S(2)}) async-start(bf16[16,2,1280]{2,1,0:T(2,128)(2,1)} %broadcast_in_dim.66), calls=%async_computation.2 | async-start | bytes 163840 | tf_op jit(solution)/shard_map/all_to_all | solution.py:15
  106.9 8.2 %all-to-all-done.2 = bf16[16,2,1280]{2,1,0:T(2,128)(2,1)S(1)} async-done(((bf16[16,2,1280]{2,1,0:T(2,128)(2,1)}), bf16[16,2,1280]{2,1,0:T(2,128)(2,1)S(1)}, u32[]{:S(2)}, u32[]{:S(2)}) %all-to-all-start.2) | async-done | bytes 81952 | tf_op jit(solution)/shard_map/all_to_all | solution.py:15
  117.6 8.1 %all-to-all-start.3 = ((bf16[32,2,1152]{2,1,0:T(2,128)(2,1)}), bf16[32,2,1152]{2,1,0:T(2,128)(2,1)S(1)}, u32[]{:S(2)}, u32[]{:S(2)}) async-start(bf16[32,2,1152]{2,1,0:T(2,128)(2,1)} %copy.29), calls=%async_computation.3 | async-start | bytes 294912 | tf_op jit(solution)/shard_map/all_to_all | solution.py:313
  125.8 2.4 %collective-permute-start.10 = (f32[2,1152]{1,0:T(2,128)S(1)}, f32[2,1152]{1,0:T(2,128)S(1)}, u32[]{:S(2)}, u32[]{:S(2)}) collective-permute-start(f32[2,1152]{1,0:T(2,128)S(1)} %get-tuple-element.34), channel_id=1, source_target_pairs={{0,12},{4,0},{8,4},{12,8},{1,13},{5,1},{9,5},{13,9},{2,14},{6,2},{... | collective-permute-start | bytes 27656 | tf_op jit(solution)/shard_map/ppermute | solution.py:21
  128.1 2.3 %collective-permute-start.9 = (f32[2,1152]{1,0:T(2,128)S(1)}, f32[2,1152]{1,0:T(2,128)S(1)}, u32[]{:S(2)}, u32[]{:S(2)}) collective-permute-start(f32[2,1152]{1,0:T(2,128)S(1)} %get-tuple-element.35), channel_id=1, source_target_pairs={{0,8},{4,12},{8,0},{12,4},{1,9},{5,13},{9,1},{13,5},{2,10},{6,14},... | collective-permute-start | bytes 27656 | tf_op jit(solution)/shard_map/ppermute | solution.py:21
  130.4 3.4 %collective-permute-start.8 = (f32[2,1152]{1,0:T(2,128)S(1)}, f32[2,1152]{1,0:T(2,128)S(1)}, u32[]{:S(2)}, u32[]{:S(2)}) collective-permute-start(f32[2,1152]{1,0:T(2,128)S(1)} %get-tuple-element.33), channel_id=1, source_target_pairs={{0,4},{4,8},{8,12},{12,0},{1,5},{5,9},{9,13},{13,1},{2,6},{6,10},{... | collective-permute-start | bytes 27656 | tf_op jit(solution)/shard_map/ppermute | solution.py:21
  (100 shorter events, 13.2 us)
Async XLA Ops:
  0.6 36.9 %copy-start.5 = (bf16[2,256,288]{1,2,0:T(8,128)(2,1)S(1)}, bf16[2,256,288]{1,2,0:T(8,128)(2,1)}, u32[]{:S(2)}) copy-start(bf16[2,256,288]{1,2,0:T(8,128)(2,1)} %param.13) | copy-start | bytes 884740
  0.6 31.0 %copy-start.8 = (f32[1152]{0:T(1024)S(1)}, f32[1152]{0:T(1024)}, u32[]{:S(2)}) copy-start(f32[1152]{0:T(1024)} %param.15) | copy-start | bytes 13828
  0.6 36.9 %copy-start.4 = (bf16[288,1152]{1,0:T(8,128)(2,1)S(1)}, bf16[288,1152]{1,0:T(8,128)(2,1)}, u32[]{:S(2)}) copy-start(bf16[288,1152]{1,0:T(8,128)(2,1)} %out_w_ref.4) | copy-start | bytes 1990660
  0.7 28.7 %collective-permute-start = (bf16[576,256]{1,0:T(8,128)(2,1)}, bf16[576,256]{1,0:T(8,128)(2,1)S(1)}, u32[]{:S(2)}, u32[]{:S(2)}) collective-permute-start(bf16[576,256]{1,0:T(8,128)(2,1)} %bitcast.50), channel_id=1, source_target_pairs={{0,1},{1,2},{2,3},{3,0},{4,5},{5,6},{6,7},{7,4},{8,9},{9,10},{10,1... | collective-permute-start | bytes 884744 | tf_op jit(solution)/shard_map/ppermute | solution.py:21
  7.4 24.5 %collective-permute-start.1 = (bf16[576,256]{1,0:T(8,128)(2,1)}, bf16[576,256]{1,0:T(8,128)(2,1)S(1)}, u32[]{:S(2)}, u32[]{:S(2)}) collective-permute-start(bf16[576,256]{1,0:T(8,128)(2,1)} %bitcast.51), channel_id=1, source_target_pairs={{0,3},{1,0},{2,1},{3,2},{4,7},{5,4},{6,5},{7,6},{8,11},{9,8},{10,9... | collective-permute-start | bytes 884744 | tf_op jit(solution)/shard_map/ppermute | solution.py:21
  15.6 34.0 %all-to-all-start = ((bf16[32,2,1152]{2,1,0:T(2,128)(2,1)}), bf16[32,2,1152]{2,1,0:T(2,128)(2,1)S(1)}, u32[]{:S(2)}, u32[]{:S(2)}) async-start(bf16[32,2,1152]{2,1,0:T(2,128)(2,1)} %broadcast_in_dim.36), calls=%async_computation | async-start | bytes 294912 | tf_op jit(solution)/shard_map/all_to_all | solution.py:15
  29.4 8.1 %collective-permute-start.2 = (bf16[288,256]{1,0:T(8,128)(2,1)S(1)}, bf16[288,256]{1,0:T(8,128)(2,1)S(1)}, u32[]{:S(2)}, u32[]{:S(2)}) collective-permute-start(bf16[288,256]{1,0:T(8,128)(2,1)S(1)} %constant_dynamic-slice_fusion.2), channel_id=1, source_target_pairs={{0,1},{1,2},{2,3},{3,0},{4,5},{5,6},{6,7},{7,4},{8,9},{9,10},{10,1... | collective-permute-start | bytes 442376 | tf_op jit(solution)/shard_map/ppermute | solution.py:21
  31.9 17.8 %collective-permute-start.4 = (bf16[288,256]{1,0:T(8,128)(2,1)S(1)}, bf16[288,256]{1,0:T(8,128)(2,1)S(1)}, u32[]{:S(2)}, u32[]{:S(2)}) collective-permute-start(bf16[288,256]{1,0:T(8,128)(2,1)S(1)} %constant_dynamic-slice_fusion.1), channel_id=1, source_target_pairs={{0,3},{1,0},{2,1},{3,2},{4,7},{5,4},{6,5},{7,6},{8,11},{9,8},{10,9... | collective-permute-start | bytes 442376 | tf_op jit(solution)/shard_map/ppermute | solution.py:21
  44.2 4.8 %copy-start.6 = (bf16[2,1152]{1,0:T(2,128)(2,1)S(1)}, bf16[2,1152]{1,0:T(2,128)(2,1)}, u32[]{:S(2)}) copy-start(bf16[2,1152]{1,0:T(2,128)(2,1)} %param.22) | copy-start | bytes 13828
  45.0 10.2 %collective-permute-start.3 = (bf16[80,1152]{1,0:T(8,128)(2,1)}, bf16[80,1152]{1,0:T(8,128)(2,1)S(1)}, u32[]{:S(2)}, u32[]{:S(2)}) collective-permute-start(bf16[80,1152]{1,0:T(8,128)(2,1)} %get-tuple-element.38), channel_id=1, source_target_pairs={{0,1},{1,2},{2,3},{3,0},{4,5},{5,6},{6,7},{7,4},{8,9},{9,10},{10,1... | collective-permute-start | bytes 552968 | tf_op jit(solution)/shard_map/ppermute | solution.py:21
  49.7 13.8 %collective-permute-start.6 = (bf16[80,1152]{1,0:T(8,128)(2,1)}, bf16[80,1152]{1,0:T(8,128)(2,1)S(1)}, u32[]{:S(2)}, u32[]{:S(2)}) collective-permute-start(bf16[80,1152]{1,0:T(8,128)(2,1)} %get-tuple-element.37), channel_id=1, source_target_pairs={{0,3},{1,0},{2,1},{3,2},{4,7},{5,4},{6,5},{7,6},{8,11},{9,8},{10,9... | collective-permute-start | bytes 552968 | tf_op jit(solution)/shard_map/ppermute | solution.py:21
  61.2 7.8 %copy-start.10 = (f32[2]{0:T(128)S(1)}, f32[2]{0:T(128)}, u32[]{:S(2)}) copy-start(f32[2]{0:T(128)} %fusion.15) | copy-start | bytes 28
  61.3 12.1 %collective-permute-start.5 = (bf16[144,1152]{1,0:T(8,128)(2,1)S(1)}, bf16[144,1152]{1,0:T(8,128)(2,1)S(1)}, u32[]{:S(2)}, u32[]{:S(2)}) collective-permute-start(bf16[144,1152]{1,0:T(8,128)(2,1)S(1)} %pad_maximum_fusion), channel_id=1, source_target_pairs={{0,1},{1,2},{2,3},{3,0},{4,5},{5,6},{6,7},{7,4},{8,9},{9,10},{10,1... | collective-permute-start | bytes 995336 | tf_op jit(solution)/shard_map/ppermute | solution.py:21
  63.5 16.9 %copy-start.11 = (s32[2]{0:T(128)S(1)}, s32[2]{0:T(128)}, u32[]{:S(2)}) copy-start(s32[2]{0:T(128)} %param.23) | copy-start | bytes 28
  63.5 18.2 %copy-start.7 = (s32[32,2]{1,0:T(8,128)S(1)}, s32[32,2]{1,0:T(8,128)}, u32[]{:S(2)}) copy-start(s32[32,2]{1,0:T(8,128)} %iota_add_fusion) | copy-start | bytes 772
  63.6 24.0 %copy-start = (bf16[2,1152,288]{1,2,0:T(8,128)(2,1)S(1)}, bf16[2,1152,288]{1,2,0:T(8,128)(2,1)}, u32[]{:S(2)}) copy-start(bf16[2,1152,288]{1,2,0:T(8,128)(2,1)} %param.19) | copy-start | bytes 3981316
  63.6 24.0 %copy-start.1 = (bf16[288,1152]{1,0:T(8,128)(2,1)S(1)}, bf16[288,1152]{1,0:T(8,128)(2,1)}, u32[]{:S(2)}) copy-start(bf16[288,1152]{1,0:T(8,128)(2,1)} %out_w_ref.5) | copy-start | bytes 1990660
  63.6 9.7 %collective-permute-start.7 = (bf16[128,1152]{1,0:T(8,128)(2,1)S(1)}, bf16[128,1152]{1,0:T(8,128)(2,1)S(1)}, u32[]{:S(2)}, u32[]{:S(2)}) collective-permute-start(bf16[128,1152]{1,0:T(8,128)(2,1)S(1)} %pad_maximum_fusion.1), channel_id=1, source_target_pairs={{0,3},{1,0},{2,1},{3,2},{4,7},{5,4},{6,5},{7,6},{8,11},{9,8},{10,9... | collective-permute-start | bytes 884744 | tf_op jit(solution)/shard_map/ppermute | solution.py:21
  75.4 12.1 %all-to-all-start.1 = ((f32[4,4,1280]{2,1,0:T(4,128)}), f32[4,4,1280]{2,1,0:T(4,128)S(1)}, u32[]{:S(2)}, u32[]{:S(2)}) async-start(f32[4,4,1280]{2,1,0:T(4,128)} %mix_rows.1), calls=%async_computation.1 | async-start | bytes 163840 | tf_op jit(solution)/shard_map/all_to_all | solution.py:287
  89.1 26.0 %all-to-all-start.2 = ((bf16[16,2,1280]{2,1,0:T(2,128)(2,1)}), bf16[16,2,1280]{2,1,0:T(2,128)(2,1)S(1)}, u32[]{:S(2)}, u32[]{:S(2)}) async-start(bf16[16,2,1280]{2,1,0:T(2,128)(2,1)} %broadcast_in_dim.66), calls=%async_computation.2 | async-start | bytes 163840 | tf_op jit(solution)/shard_map/all_to_all | solution.py:15
  117.6 17.3 %all-to-all-start.3 = ((bf16[32,2,1152]{2,1,0:T(2,128)(2,1)}), bf16[32,2,1152]{2,1,0:T(2,128)(2,1)S(1)}, u32[]{:S(2)}, u32[]{:S(2)}) async-start(bf16[32,2,1152]{2,1,0:T(2,128)(2,1)} %copy.29), calls=%async_computation.3 | async-start | bytes 294912 | tf_op jit(solution)/shard_map/all_to_all | solution.py:313
  125.8 10.2 %collective-permute-start.10 = (f32[2,1152]{1,0:T(2,128)S(1)}, f32[2,1152]{1,0:T(2,128)S(1)}, u32[]{:S(2)}, u32[]{:S(2)}) collective-permute-start(f32[2,1152]{1,0:T(2,128)S(1)} %get-tuple-element.34), channel_id=1, source_target_pairs={{0,12},{4,0},{8,4},{12,8},{1,13},{5,1},{9,5},{13,9},{2,14},{6,2},{... | collective-permute-start | bytes 27656 | tf_op jit(solution)/shard_map/ppermute | solution.py:21
  128.1 7.8 %collective-permute-start.9 = (f32[2,1152]{1,0:T(2,128)S(1)}, f32[2,1152]{1,0:T(2,128)S(1)}, u32[]{:S(2)}, u32[]{:S(2)}) collective-permute-start(f32[2,1152]{1,0:T(2,128)S(1)} %get-tuple-element.35), channel_id=1, source_target_pairs={{0,8},{4,12},{8,0},{12,4},{1,9},{5,13},{9,1},{13,5},{2,10},{6,14},... | collective-permute-start | bytes 27656 | tf_op jit(solution)/shard_map/ppermute | solution.py:21
  130.4 5.5 %collective-permute-start.8 = (f32[2,1152]{1,0:T(2,128)S(1)}, f32[2,1152]{1,0:T(2,128)S(1)}, u32[]{:S(2)}, u32[]{:S(2)}) collective-permute-start(f32[2,1152]{1,0:T(2,128)S(1)} %get-tuple-element.33), channel_id=1, source_target_pairs={{0,4},{4,8},{8,12},{12,0},{1,5},{5,9},{9,13},{13,1},{2,6},{6,10},{... | collective-permute-start | bytes 27656 | tf_op jit(solution)/shard_map/ppermute | solution.py:21
  (3 other events, 7.8 us)
